TPU v7x, 32 devices: a whole 2x2x4 slice. The times are simulated.
32 devices in a mesh: dp: 8 (over z, core), seq: 4 (over y, x).
Axes of the slice: x: 2, y: 2, z: 4, core: 2. Of those that a mesh axis runs over, the one named last changes fastest.
Arguments:
- tokens: bfloat16 [16, 1024, 1024], P('dp', 'seq'), may hold values from -6 to 6
- lengths: int32 [16, 8], P('dp'), may hold values from 0 to 1024, as said below
- timesteps: int32 [16, 8], P('dp'), may hold values from 0 to 4999
- w_query: bfloat16 [1024, 1024], P(('dp', 'seq')), may hold values from -0.1875 to 0.1875
- b_query: bfloat16 [1024], P(('dp', 'seq')), may hold values from -4 to 4
- w_key: bfloat16 [1024, 1024], P(('dp', 'seq')), may hold values from -0.1875 to 0.1875
- w_value: bfloat16 [1024, 1024], P(('dp', 'seq')), may hold values from -0.1875 to 0.1875
- b_value: bfloat16 [1024], P(('dp', 'seq')), may hold values from -4 to 4
- w_out: bfloat16 [1024, 1024], P(('dp', 'seq')), may hold values from -1.5 to 1.5
- b_out: bfloat16 [1024], P(('dp', 'seq')), may hold values from -4 to 4
- gain_one: bfloat16 [1024], P(('dp', 'seq')), may hold values from 0.099609375 to 1.8984375
- shift_one: bfloat16 [1024], P(('dp', 'seq')), may hold values from -4 to 4
- w_up: bfloat16 [1024, 4096], P(('dp', 'seq')), may hold values from -0.1875 to 0.1875
- b_up: bfloat16 [4096], P(('dp', 'seq')), may hold values from -4 to 4
- w_down: bfloat16 [4096, 1024], P(('dp', 'seq')), may hold values from -0.09375 to 0.09375
- b_down: bfloat16 [1024], P(('dp', 'seq')), may hold values from -4 to 4
- gain_two: bfloat16 [1024], P(('dp', 'seq')), may hold values from 0.099609375 to 1.8984375
- shift_two: bfloat16 [1024], P(('dp', 'seq')), may hold values from -4 to 4
- w_time: bfloat16 [1024], P(('dp', 'seq')), may hold values from -6 to 6
- b_time: bfloat16 [1024], P(('dp', 'seq')), may hold values from -6 to 6
- cotangent: bfloat16 [16, 1024, 1024], P('dp', 'seq'), may hold values from -6 to 6
Outputs:
- output: bfloat16 [16, 1024, 1024], P('dp', 'seq')
- grad_tokens: bfloat16 [16, 1024, 1024], P('dp', 'seq')
- grad_w_query: float32 [1024, 1024], P(('dp', 'seq'))
- grad_b_query: float32 [1024], P(('dp', 'seq'))
- grad_w_key: float32 [1024, 1024], P(('dp', 'seq'))
- grad_w_value: float32 [1024, 1024], P(('dp', 'seq'))
- grad_b_value: float32 [1024], P(('dp', 'seq'))
- grad_w_out: float32 [1024, 1024], P(('dp', 'seq'))
- grad_b_out: float32 [1024], P(('dp', 'seq'))
- grad_gain_one: float32 [1024], P(('dp', 'seq'))
- grad_shift_one: float32 [1024], P(('dp', 'seq'))
- grad_w_up: float32 [1024, 4096], P(('dp', 'seq'))
- grad_b_up: float32 [4096], P(('dp', 'seq'))
- grad_w_down: float32 [4096, 1024], P(('dp', 'seq'))
- grad_b_down: float32 [1024], P(('dp', 'seq'))
- grad_gain_two: float32 [1024], P(('dp', 'seq'))
- grad_shift_two: float32 [1024], P(('dp', 'seq'))
- grad_w_time: float32 [1024], P(('dp', 'seq'))
- grad_b_time: float32 [1024], P(('dp', 'seq'))
Inputs may be any that keep to these rules, and one draw needn't show every extreme that they name: `lengths`: items are packed in order from position 0. Among the 2 sequences of each index of dp, one, chosen by the seed, is a single item of 1024 tokens, with the other slots 0. In every other sequence each item holds 128 or 512 tokens, except that the last nonempty one may be cut shorter, and the slots after it hold 0; fewer than 128 padding positions end it; its first item holds 128 tokens, its second 4 * 128.
All inputs are finite; a program needn't handle non-finite values.
Results may differ from a plain program's by a relative error of at most 0.017.
The roundings to bfloat16 on the way count: a program that leaves them out, or rounds other values in their place, can miss the bound.
Values may be sent and summed in bfloat16 or wider, within the bound.
No kernel may reach another device: no remote copies, remote signals or barrier semaphores. Data moves between devices by JAX's collectives and lax.ppermute only.
A program may use at most 192 MiB of HBM per device.

v0:
```python
import jax
import jax.numpy as jnp
from jax import lax
from jax.sharding import PartitionSpec as P

HD = 64
TSTEPS = 5000


EPSILON = 1e-05
NEGATIVE = -1e30
ROOT_HALF = 0.7071067811865476
DENSITY_SCALE = 0.3989422804014327


def segment_of(lengths, positions):
    item_ends = jnp.cumsum(lengths, axis=1, dtype=jnp.int32)
    reached = (item_ends[:, None, :] <= positions[None, :, None]).astype(jnp.int32)
    return jnp.sum(reached, axis=2, dtype=jnp.int32)


def step_scale(segment, timesteps):
    slot_ids = jnp.arange(timesteps.shape[1], dtype=jnp.int32)
    member = (segment[:, :, None] == slot_ids[None, None, :]).astype(jnp.float32)
    return jnp.sum(member * timesteps[:, None, :].astype(jnp.float32), axis=2) / TSTEPS


def norm_forward(residual, norm_gain, norm_shift):
    center = residual - jnp.mean(residual, axis=-1, keepdims=True)
    inverse = lax.rsqrt(jnp.mean(center * center, axis=-1, keepdims=True) + EPSILON)
    normed = center * inverse
    return (normed * norm_gain + norm_shift, normed, inverse)


def norm_backward(grad_in, normed, inverse, norm_gain):
    grad_norm = grad_in * norm_gain
    mean_one = jnp.mean(grad_norm, axis=-1, keepdims=True)
    mean_two = jnp.mean(grad_norm * normed, axis=-1, keepdims=True)
    return inverse * (grad_norm - mean_one - normed * mean_two)


def gelu_parts(pre_act):
    cumulative = 0.5 * (1.0 + lax.erf(pre_act * ROOT_HALF))
    density = jnp.exp(-0.5 * pre_act * pre_act) * DENSITY_SCALE
    return (pre_act * cumulative, cumulative + pre_act * density)


def split_head(matrix, head_index):
    return lax.dynamic_slice_in_dim(matrix, head_index * HD, HD, axis=2)


def merge_heads(stacked):
    moved = jnp.moveaxis(stacked, 0, 2)
    return moved.reshape(moved.shape[0], moved.shape[1], moved.shape[2] * moved.shape[3])


def dense(left, right):
    return jnp.dot(left, right, preferred_element_type=jnp.float32)


def dense_back(left, right):
    return jnp.einsum("ro,io->ri", left, right, preferred_element_type=jnp.float32)


def weight_grad(left, right):
    return jnp.einsum("ri,ro->io", left, right, preferred_element_type=jnp.float32)


def column_sum(matrix):
    return jnp.sum(matrix.astype(jnp.float32), axis=0)


def head_forward(single_query_head, single_key_head, single_value_head, same_item):
    attention_scores = jnp.einsum(
        "nrt,net->nre", single_query_head, single_key_head, preferred_element_type=jnp.float32
    )
    attention_scores = jnp.where(same_item, attention_scores, NEGATIVE)
    top_score = jnp.max(attention_scores, axis=2, keepdims=True)
    raised = jnp.exp(attention_scores - top_score)
    total = jnp.sum(raised, axis=2, keepdims=True)
    probabilities_reduced = (raised / total).astype(jnp.bfloat16)
    attended_context = jnp.einsum(
        "chi,cie->che", probabilities_reduced, single_value_head, preferred_element_type=jnp.float32
    )
    return (attended_context, top_score[:, :, 0] + jnp.log(total[:, :, 0]))


def head_backward(
    single_query_head, single_key_head, single_value_head, same_item, log_total, context_gradient
):
    attention_scores = jnp.einsum(
        "nrt,net->nre", single_query_head, single_key_head, preferred_element_type=jnp.float32
    )
    attention_scores = jnp.where(same_item, attention_scores, NEGATIVE)
    attention_probabilities = jnp.exp(attention_scores - log_total[:, :, None])
    grad_probs = jnp.einsum(
        "nrt,net->nre", context_gradient, single_value_head, preferred_element_type=jnp.float32
    )
    row_total = jnp.sum(attention_probabilities * grad_probs, axis=2, keepdims=True)
    scores_gradient = (attention_probabilities * (grad_probs - row_total)).astype(jnp.bfloat16)
    grad_query = jnp.einsum(
        "chi,cie->che", scores_gradient, single_key_head, preferred_element_type=jnp.float32
    )
    grad_key = jnp.einsum(
        "tjc,tjz->tcz", scores_gradient, single_query_head, preferred_element_type=jnp.float32
    )
    grad_value = jnp.einsum(
        "tjc,tjz->tcz",
        attention_probabilities.astype(jnp.bfloat16),
        context_gradient,
        preferred_element_type=jnp.float32,
    )
    return (grad_query, grad_key, grad_value)


def attend(query_low, key_all, value_all, same_item):
    head_count = query_low.shape[2] // HD

    def one_head(head_index):
        return head_forward(
            split_head(query_low, head_index),
            split_head(key_all, head_index),
            split_head(value_all, head_index),
            same_item,
        )

    attended_context, log_total = lax.map(one_head, jnp.arange(head_count, dtype=jnp.int32))
    return (merge_heads(attended_context), log_total)


def attend_back(query_low, key_all, value_all, same_item, log_total, context_gradient):
    head_count = query_low.shape[2] // HD

    def one_head(head_index):
        return head_backward(
            split_head(query_low, head_index),
            split_head(key_all, head_index),
            split_head(value_all, head_index),
            same_item,
            log_total[head_index],
            split_head(context_gradient, head_index),
        )

    grad_query, grad_key, grad_value = lax.map(one_head, jnp.arange(head_count, dtype=jnp.int32))
    return (merge_heads(grad_query), merge_heads(grad_key), merge_heads(grad_value))


def forward(tokens_f, tau, same_item, params, fetch_keys):
    (
        query_weight,
        query_bias,
        key_weight,
        value_weight,
        value_bias,
        out_weight,
        out_bias,
        first_gain,
        first_shift,
        up_weight,
        up_bias,
        down_weight,
        down_bias,
        second_gain,
        second_shift,
        time_weight,
        time_bias,
    ) = params
    local_seqs, local_rows, model_width = tokens_f.shape
    query_scale = HD ** (-0.5)
    start = (
        tokens_f + tau[:, :, None] * time_weight.astype(jnp.float32) + time_bias.astype(jnp.float32)
    )
    start_flat = start.reshape(local_seqs * local_rows, model_width)
    start_low = start_flat.astype(jnp.bfloat16)
    query_low = (
        ((dense(start_low, query_weight) + query_bias) * query_scale)
        .astype(jnp.bfloat16)
        .reshape(local_seqs, local_rows, model_width)
    )
    key_low = (
        dense(start_low, key_weight)
        .astype(jnp.bfloat16)
        .reshape(local_seqs, local_rows, model_width)
    )
    value_low = (
        (dense(start_low, value_weight) + value_bias)
        .astype(jnp.bfloat16)
        .reshape(local_seqs, local_rows, model_width)
    )
    key_all, value_all = fetch_keys(key_low, value_low)
    attended_context, log_total = attend(query_low, key_all, value_all, same_item)
    context_low = attended_context.astype(jnp.bfloat16).reshape(
        local_seqs * local_rows, model_width
    )
    attn_out = dense(context_low, out_weight) + out_bias
    first, first_norm, first_inv = norm_forward(
        start_flat + attn_out, first_gain.astype(jnp.float32), first_shift.astype(jnp.float32)
    )
    first_low = first.astype(jnp.bfloat16)
    up_pre = dense(first_low, up_weight) + up_bias
    activ, slope = gelu_parts(up_pre)
    activ_low = activ.astype(jnp.bfloat16)
    down_out = dense(activ_low, down_weight) + down_bias
    final, second_norm, second_inv = norm_forward(
        first + down_out, second_gain.astype(jnp.float32), second_shift.astype(jnp.float32)
    )
    return (
        final,
        start_low,
        query_low,
        key_all,
        value_all,
        log_total,
        context_low,
        first_norm,
        first_inv,
        first_low,
        slope,
        activ_low,
        second_norm,
        second_inv,
    )


def body(
    tokens,
    lengths,
    timesteps,
    w_query,
    b_query,
    w_key,
    w_value,
    b_value,
    w_out,
    b_out,
    gain_one,
    shift_one,
    w_up,
    b_up,
    w_down,
    b_down,
    gain_two,
    shift_two,
    w_time,
    b_time,
    cotangent,
):
    local_seqs, local_rows, model_width = tokens.shape
    seq_devices = lax.axis_size("seq")
    full_length = local_rows * seq_devices
    first_row = lax.axis_index("seq") * local_rows
    query_spots = first_row + jnp.arange(local_rows, dtype=jnp.int32)
    key_spots = jnp.arange(full_length, dtype=jnp.int32)
    query_segment = segment_of(lengths, query_spots)
    key_segment = segment_of(lengths, key_spots)
    same_item = query_segment[:, :, None] == key_segment[:, None, :]
    tau = step_scale(query_segment, timesteps)
    tokens_f = tokens.astype(jnp.float32)
    gathered = (
        lax.all_gather(w_query, ("dp", "seq"), axis=0, tiled=True),
        lax.all_gather(b_query, ("dp", "seq"), axis=0, tiled=True),
        lax.all_gather(w_key, ("dp", "seq"), axis=0, tiled=True),
        lax.all_gather(w_value, ("dp", "seq"), axis=0, tiled=True),
        lax.all_gather(b_value, ("dp", "seq"), axis=0, tiled=True),
        lax.all_gather(w_out, ("dp", "seq"), axis=0, tiled=True),
        lax.all_gather(b_out, ("dp", "seq"), axis=0, tiled=True),
        lax.all_gather(gain_one, ("dp", "seq"), axis=0, tiled=True),
        lax.all_gather(shift_one, ("dp", "seq"), axis=0, tiled=True),
        lax.all_gather(w_up, ("dp", "seq"), axis=0, tiled=True),
        lax.all_gather(b_up, ("dp", "seq"), axis=0, tiled=True),
        lax.all_gather(w_down, ("dp", "seq"), axis=0, tiled=True),
        lax.all_gather(b_down, ("dp", "seq"), axis=0, tiled=True),
        lax.all_gather(gain_two, ("dp", "seq"), axis=0, tiled=True),
        lax.all_gather(shift_two, ("dp", "seq"), axis=0, tiled=True),
        lax.all_gather(w_time, ("dp", "seq"), axis=0, tiled=True),
        lax.all_gather(b_time, ("dp", "seq"), axis=0, tiled=True),
    )

    def fetch_keys(key_low, value_low):
        return (
            lax.all_gather(key_low, "seq", axis=1, tiled=True),
            lax.all_gather(value_low, "seq", axis=1, tiled=True),
        )

    kept = forward(tokens_f, tau, same_item, gathered, fetch_keys)
    output_low = kept[0].astype(jnp.bfloat16).reshape(local_seqs, local_rows, model_width)
    gathered = (
        lax.all_gather(w_query, ("dp", "seq"), axis=0, tiled=True),
        lax.all_gather(b_query, ("dp", "seq"), axis=0, tiled=True),
        lax.all_gather(w_key, ("dp", "seq"), axis=0, tiled=True),
        lax.all_gather(w_value, ("dp", "seq"), axis=0, tiled=True),
        lax.all_gather(b_value, ("dp", "seq"), axis=0, tiled=True),
        lax.all_gather(w_out, ("dp", "seq"), axis=0, tiled=True),
        lax.all_gather(b_out, ("dp", "seq"), axis=0, tiled=True),
        lax.all_gather(gain_one, ("dp", "seq"), axis=0, tiled=True),
        lax.all_gather(shift_one, ("dp", "seq"), axis=0, tiled=True),
        lax.all_gather(w_up, ("dp", "seq"), axis=0, tiled=True),
        lax.all_gather(b_up, ("dp", "seq"), axis=0, tiled=True),
        lax.all_gather(w_down, ("dp", "seq"), axis=0, tiled=True),
        lax.all_gather(b_down, ("dp", "seq"), axis=0, tiled=True),
        lax.all_gather(gain_two, ("dp", "seq"), axis=0, tiled=True),
        lax.all_gather(shift_two, ("dp", "seq"), axis=0, tiled=True),
        lax.all_gather(w_time, ("dp", "seq"), axis=0, tiled=True),
        lax.all_gather(b_time, ("dp", "seq"), axis=0, tiled=True),
    )

    def fetch_again(key_low, value_low):
        return (
            lax.all_gather(key_low, "seq", axis=1, tiled=True),
            lax.all_gather(value_low, "seq", axis=1, tiled=True),
        )

    kept = forward(tokens_f, tau, same_item, gathered, fetch_again)
    (
        final_again,
        start_low,
        query_low,
        key_all,
        value_all,
        log_total,
        context_low,
        first_norm,
        first_inv,
        first_low,
        slope,
        activ_low,
        second_norm,
        second_inv,
    ) = kept
    (
        query_weight,
        query_bias,
        key_weight,
        value_weight,
        value_bias,
        out_weight,
        out_bias,
        first_gain,
        first_shift,
        up_weight,
        up_bias,
        down_weight,
        down_bias,
        second_gain,
        second_shift,
        time_weight,
        time_bias,
    ) = gathered
    grad_final = cotangent.astype(jnp.float32).reshape(local_seqs * local_rows, model_width)
    grad_gain_two = jnp.sum(grad_final * second_norm, axis=0)
    grad_shift_two = jnp.sum(grad_final, axis=0)
    grad_second = norm_backward(
        grad_final, second_norm, second_inv, second_gain.astype(jnp.float32)
    )
    down_grad = grad_second.astype(jnp.bfloat16)
    grad_b_down = column_sum(down_grad)
    grad_w_down = weight_grad(activ_low, down_grad)
    up_grad = (dense_back(down_grad, down_weight) * slope).astype(jnp.bfloat16)
    grad_b_up = column_sum(up_grad)
    grad_w_up = weight_grad(first_low, up_grad)
    ffn_grads = (grad_w_up, grad_b_up, grad_w_down, grad_b_down, grad_gain_two, grad_shift_two)
    first_grad = dense_back(up_grad, up_weight) + grad_second
    grad_gain_one = jnp.sum(first_grad * first_norm, axis=0)
    grad_shift_one = jnp.sum(first_grad, axis=0)
    grad_first = norm_backward(first_grad, first_norm, first_inv, first_gain.astype(jnp.float32))
    attn_grad = grad_first.astype(jnp.bfloat16)
    grad_b_out = column_sum(attn_grad)
    grad_w_out = weight_grad(context_low, attn_grad)
    context_grad = (
        dense_back(attn_grad, out_weight)
        .astype(jnp.bfloat16)
        .reshape(local_seqs, local_rows, model_width)
    )
    query_grad, key_grad_all, value_grad_all = attend_back(
        query_low, key_all, value_all, same_item, log_total, context_grad
    )
    key_grad, value_grad = (
        lax.psum_scatter(
            key_grad_all.astype(jnp.bfloat16), "seq", scatter_dimension=1, tiled=True
        ).astype(jnp.float32),
        lax.psum_scatter(
            value_grad_all.astype(jnp.bfloat16), "seq", scatter_dimension=1, tiled=True
        ).astype(jnp.float32),
    )
    pre_grad = (query_grad.astype(jnp.bfloat16) * HD ** (-0.5)).reshape(
        local_seqs * local_rows, model_width
    )
    key_grad_low = key_grad.astype(jnp.bfloat16).reshape(local_seqs * local_rows, model_width)
    value_grad_low = value_grad.astype(jnp.bfloat16).reshape(local_seqs * local_rows, model_width)
    grad_w_query = weight_grad(start_low, pre_grad)
    grad_b_query = column_sum(pre_grad)
    grad_w_key = weight_grad(start_low, key_grad_low)
    grad_w_value = weight_grad(start_low, value_grad_low)
    grad_b_value = column_sum(value_grad_low)
    start_grad = (
        grad_first
        + dense_back(pre_grad, query_weight)
        + dense_back(key_grad_low, key_weight)
        + dense_back(value_grad_low, value_weight)
    )
    tau_flat = tau.reshape(local_seqs * local_rows)
    grad_w_time = jnp.sum(start_grad * tau_flat[:, None], axis=0)
    grad_b_time = jnp.sum(start_grad, axis=0)
    grad_tokens = start_grad.astype(jnp.bfloat16).reshape(local_seqs, local_rows, model_width)
    every_grad = tuple(
        (
            lax.psum_scatter(grad_w_query, ("dp", "seq"), scatter_dimension=0, tiled=True),
            lax.psum_scatter(grad_b_query, ("dp", "seq"), scatter_dimension=0, tiled=True),
            lax.psum_scatter(grad_w_key, ("dp", "seq"), scatter_dimension=0, tiled=True),
            lax.psum_scatter(grad_w_value, ("dp", "seq"), scatter_dimension=0, tiled=True),
            lax.psum_scatter(grad_b_value, ("dp", "seq"), scatter_dimension=0, tiled=True),
            lax.psum_scatter(grad_w_out, ("dp", "seq"), scatter_dimension=0, tiled=True),
            lax.psum_scatter(grad_b_out, ("dp", "seq"), scatter_dimension=0, tiled=True),
            lax.psum_scatter(grad_gain_one, ("dp", "seq"), scatter_dimension=0, tiled=True),
            lax.psum_scatter(grad_shift_one, ("dp", "seq"), scatter_dimension=0, tiled=True),
            lax.psum_scatter(grad_w_up, ("dp", "seq"), scatter_dimension=0, tiled=True),
            lax.psum_scatter(grad_b_up, ("dp", "seq"), scatter_dimension=0, tiled=True),
            lax.psum_scatter(grad_w_down, ("dp", "seq"), scatter_dimension=0, tiled=True),
            lax.psum_scatter(grad_b_down, ("dp", "seq"), scatter_dimension=0, tiled=True),
            lax.psum_scatter(grad_gain_two, ("dp", "seq"), scatter_dimension=0, tiled=True),
            lax.psum_scatter(grad_shift_two, ("dp", "seq"), scatter_dimension=0, tiled=True),
            lax.psum_scatter(grad_w_time, ("dp", "seq"), scatter_dimension=0, tiled=True),
            lax.psum_scatter(grad_b_time, ("dp", "seq"), scatter_dimension=0, tiled=True),
        )
    )
    attn_grads = every_grad[0:9] + every_grad[15:17]
    ffn_grads = every_grad[9:15]
    return (output_low, grad_tokens) + attn_grads[0:9] + ffn_grads + attn_grads[9:11]


def solution(mesh):
    placed = (
        P("dp", "seq", None),
        P("dp", None),
        P("dp", None),
        P(("dp", "seq"), None),
        P(("dp", "seq")),
        P(("dp", "seq"), None),
        P(("dp", "seq"), None),
        P(("dp", "seq")),
        P(("dp", "seq"), None),
        P(("dp", "seq")),
        P(("dp", "seq")),
        P(("dp", "seq")),
        P(("dp", "seq"), None),
        P(("dp", "seq")),
        P(("dp", "seq"), None),
        P(("dp", "seq")),
        P(("dp", "seq")),
        P(("dp", "seq")),
        P(("dp", "seq")),
        P(("dp", "seq")),
        P("dp", "seq", None),
    )
    return jax.shard_map(
        body,
        mesh=mesh,
        in_specs=placed,
        out_specs=(
            P("dp", "seq", None),
            P("dp", "seq", None),
            P(("dp", "seq"), None),
            P(("dp", "seq")),
            P(("dp", "seq"), None),
            P(("dp", "seq"), None),
            P(("dp", "seq")),
            P(("dp", "seq"), None),
            P(("dp", "seq")),
            P(("dp", "seq")),
            P(("dp", "seq")),
            P(("dp", "seq"), None),
            P(("dp", "seq")),
            P(("dp", "seq"), None),
            P(("dp", "seq")),
            P(("dp", "seq")),
            P(("dp", "seq")),
            P(("dp", "seq")),
            P(("dp", "seq")),
        ),
        check_vma=False,
    )
```

profile of v0, /device:TPU:0, one launch (start us, length us, event | category | flops | bytes accessed | tf_op | source)
XLA Modules:
  0.0 2166.9 jit_solution(12280769411137511024)
XLA Ops:
  17.8 42.4 %all-reduce.22 = (bf16[1024]{0:T(1024)(128)(2,1)S(1)}, bf16[1024]{0:T(1024)(128)(2,1)S(1)}, bf16[1024]{0:T(1024)(128)(2,1)S(1)}, bf16[1024]{0:T(1024)(128)(2,1)S...) all-reduce(bf16[1024]{0:T(1024)(128)(2,1)S(1)} %dynamic-update-slic, ...), channel_id=1, replica_groups=mesh['dp'=8,'seq'=4] {'dp','seq'}, use_global_device_ids=true, to_apply=%add.1 | all-reduce | flops 10240 | bytes 40960
  65.3 5.0 all-gather.16.cloned.1.call-done
  70.4 3.8 add_convert_fusion.1
  76.5 52.0 %all-gather.12.cloned.1.call-done = bf16[1024,1024]{1,0:T(8,128)(2,1)} async-done(((bf16[32,1024]{1,0:T(8,128)(2,1)}), bf16[1024,1024]{1,0:T(8,128)(2,1)}) %all-gather.12.cloned.1.call-update) | async-done | bytes 2097168 | tf_op jit(solution)/shard_map/all_gather | solution.py:262
  128.5 3.8 convolution_convert_fusion.1
  137.1 66.2 %all-gather = bf16[32,1,128]{2,1,0:T(2,128)(2,1)S(1)} all-gather(bf16[1,1,128]{2,1,0:T(2,128)(2,1)S(1)} %bitcast.192), channel_id=1, replica_groups=mesh['dp'=8,'seq'=4] {'dp','seq'}, dimensions={0}, use_global_device_ids=true | all-gather | bytes 8448 | tf_op jit(solution)/shard_map/all_gather | solution.py:270
  204.3 4.1 multiply_convert_fusion.3
  210.7 29.2 %all-gather.18.cloned.1.call-done = bf16[2,1024,1024]{1,2,0:T(8,128)(2,1)} async-done(((bf16[2,256,1024]{1,2,0:T(8,128)(2,1)}), bf16[2,1024,1024]{1,2,0:T(8,128)(2,1)}) %all-gather.18.cloned.1.call-update) | async-done | bytes 4194320 | tf_op jit(solution)/shard_map/all_gather | solution.py:282
  239.9 54.3 %all-gather.14.cloned.1.call-done = bf16[2,1024,1024]{1,2,0:T(8,128)(2,1)} async-done(((bf16[2,256,1024]{1,2,0:T(8,128)(2,1)}), bf16[2,1024,1024]{1,2,0:T(8,128)(2,1)}) %all-gather.14.cloned.1.call-update) | async-done | bytes 4194320 | tf_op jit(solution)/shard_map/all_gather | solution.py:281
  295.3 100.0 %while.39 = (s32[]{:T(128)}, bf16[16,2,256,64]{2,3,1,0:T(8,128)(2,1)}, s32[16]{0:T(128)S(1)}, bf16[2,256,1024]{1,2,0:T(8,128)(2,1)}, bf16[2,1024,1024]{1,2,0:T(8...) while((s32[]{:T(128)}, ...), condition=%wide.region_7.8_spmd.clone, body=%wide.region_4.7_spmd.clone.sunk | while | flops 206047744 | bytes 1076399 | solution.py:127
  399.9 93.3 %while.40 = (s32[]{:T(128)}, bf16[16,2,256,64]{2,3,1,0:T(8,128)(2,1)}, f32[16,2,256]{2,1,0:T(2,128)S(1)}, s32[16]{0:T(128)S(1)}, bf16[2,256,1024]{1,2,0:T(8,128)...) while((s32[]{:T(128)}, ...), condition=%wide.region_15.16_spmd.clone, body=%wide.region_12.15_spmd.clone.sunk | while | flops 140508672 | bytes 7061183 | solution.py:127
  504.3 7.5 all-gather.24.cloned.1.call-done
  511.8 17.4 fusion.117
  529.2 10.1 multiply_convert_fusion.1
  539.3 4.8 fusion.115
  548.1 11.8 convert_reduce_fusion
  559.9 5.2 multiply_reduce_fusion.2
  569.5 192.3 %while.41 = (s32[]{:T(128)}, bf16[16,2,256,64]{2,3,1,0:T(8,128)(2,1)S(1)}, bf16[16,2,1024,64]{2,3,0,1:T(8,128)(2,1)}, bf16[16,2,1024,64]{2,3,0,1:T(8,128)(2,1)},...) while((s32[]{:T(128)}, ...), condition=%wide.region_26.27_spmd.clone, body=%wide.region_24.26_spmd.clone.sunk | while | flops 340262400 | bytes 17981192 | solution.py:144
  773.6 39.6 %reduce-scatter.9.cloned.1.call-done = bf16[2,256,1024]{1,2,0:T(8,128)(2,1)} async-done(((bf16[2,1024,1024]{1,2,0:T(8,128)(2,1)}), bf16[2,256,1024]{1,2,0:T(8,128)(2,1)}) %reduce-scatter.9.cloned.1.call-update) | async-done | bytes 1048592 | tf_op jit(solution)/shard_map/reduce_scatter | solution.py:378
  813.2 4.5 convolution_bitcast_fusion.6
  817.8 51.2 %reduce-scatter.11.cloned.1.call-done = bf16[2,256,1024]{1,2,0:T(8,128)(2,1)} async-done(((bf16[2,1024,1024]{1,2,0:T(8,128)(2,1)}), bf16[2,256,1024]{1,2,0:T(8,128)(2,1)}) %reduce-scatter.11.cloned.1.call-update) | async-done | bytes 1048592 | tf_op jit(solution)/shard_map/reduce_scatter | solution.py:381
  869.0 4.4 convolution_bitcast_fusion.5
  873.5 13.3 fusion.103
  887.0 13.2 fusion.99
  901.0 4.6 fusion.118
  915.8 40.9 %all-reduce.21 = (f32[1024]{0:T(1024)S(1)}, f32[1024]{0:T(1024)S(1)}, f32[1024]{0:T(1024)S(1)}, f32[1024]{0:T(1024)S(1)}, f32[1024]{0:T(1024)S(1)}, /*index=5*/f...) all-reduce(f32[1024]{0:T(1024)S(1)} %reduce_sum.279, ...), channel_id=5, replica_groups=mesh['dp'=8,'seq'=4] {'dp','seq'}, use_global_device_ids=true, to_apply=%region_31.32.clone | all-reduce | flops 14336 | bytes 114688
  963.1 50.4 %reduce-scatter.13.cloned.1.call-done = f32[32,1024]{1,0:T(8,128)} async-done(((f32[1024,1024]{1,0:T(8,128)}), f32[32,1024]{1,0:T(8,128)}) %reduce-scatter.13.cloned.1.call-update) | async-done | bytes 131088 | tf_op jit(solution)/shard_map/reduce_scatter | solution.py:407
  1013.5 142.1 %reduce-scatter.19.cloned.1.call-done = f32[32,1024]{1,0:T(8,128)} async-done(((f32[1024,1024]{1,0:T(8,128)}), f32[32,1024]{1,0:T(8,128)}) %reduce-scatter.19.cloned.1.call-update) | async-done | bytes 131088 | tf_op jit(solution)/shard_map/reduce_scatter | solution.py:412
  1155.5 142.4 %reduce-scatter.15.cloned.1.call-done = f32[32,1024]{1,0:T(8,128)} async-done(((f32[1024,1024]{1,0:T(8,128)}), f32[32,1024]{1,0:T(8,128)}) %reduce-scatter.15.cloned.1.call-update) | async-done | bytes 131088 | tf_op jit(solution)/shard_map/reduce_scatter | solution.py:409
  1297.9 142.3 %reduce-scatter.17.cloned.1.call-done = f32[32,1024]{1,0:T(8,128)} async-done(((f32[1024,1024]{1,0:T(8,128)}), f32[32,1024]{1,0:T(8,128)}) %reduce-scatter.17.cloned.1.call-update) | async-done | bytes 131088 | tf_op jit(solution)/shard_map/reduce_scatter | solution.py:410
  1440.2 358.1 %reduce-scatter.21.cloned.1.call-done = f32[32,4096]{1,0:T(8,128)} async-done(((f32[1024,4096]{1,0:T(8,128)}), f32[32,4096]{1,0:T(8,128)}) %reduce-scatter.21.cloned.1.call-update) | async-done | bytes 524304 | tf_op jit(solution)/shard_map/reduce_scatter | solution.py:416
  1798.3 361.8 %reduce-scatter.23.cloned.1.call-done = f32[128,1024]{1,0:T(8,128)} async-done(((f32[4096,1024]{1,0:T(8,128)}), f32[128,1024]{1,0:T(8,128)}) %reduce-scatter.23.cloned.1.call-update) | async-done | bytes 524304 | tf_op jit(solution)/shard_map/reduce_scatter | solution.py:418
  (451 shorter events, 402.0 us)
Async XLA Ops:
  7.2 63.2 %all-gather.16.cloned.1.call-start = ((), (), s32[]{:S(2)}) async-start(), calls=%async_computation.11 | async-start | bytes 2162688 | tf_op jit(solution)/shard_map/all_gather | solution.py:263
  7.9 120.6 %all-gather.12.cloned.1.call-start = ((), (), s32[]{:S(2)}) async-start(), calls=%async_computation.9 | async-start | bytes 2162688 | tf_op jit(solution)/shard_map/all_gather | solution.py:262
  8.7 195.6 %all-gather.10.cloned.1.call-start = ((), (), s32[]{:S(2)}) async-start(), calls=%async_computation.8 | async-start | bytes 2162688 | tf_op jit(solution)/shard_map/all_gather | solution.py:260
  9.4 230.5 %all-gather.18.cloned.1.call-start = ((), (), s32[]{:S(2)}) async-start(), calls=%async_computation.12 | async-start | bytes 5242880 | tf_op jit(solution)/shard_map/all_gather | solution.py:282
  65.2 431.5 %copy-start.5 = (f32[2,256,1024]{2,1,0:T(8,128)}, f32[2,256,1024]{2,1,0:T(8,128)S(1)}, u32[]{:S(2)}) copy-start(f32[2,256,1024]{2,1,0:T(8,128)S(1)} %get-tuple-element.480) | copy-start | bytes 6291460
  65.3 63.2 %copy-start.13 = (bf16[512,1024]{1,0:T(8,128)(2,1)}, bf16[512,1024]{1,0:T(8,128)(2,1)S(1)}, u32[]{:S(2)}) copy-start(bf16[512,1024]{1,0:T(8,128)(2,1)S(1)} %bitcast_convert_fusion) | copy-start | bytes 3145732
  76.5 217.7 %all-gather.14.cloned.1.call-start = ((), (), s32[]{:S(2)}) async-start(), calls=%async_computation.10 | async-start | bytes 5242880 | tf_op jit(solution)/shard_map/all_gather | solution.py:281
  132.3 4.7 copy-start.20
  132.3 70.9 %copy-start.2 = (bf16[2,256,1024]{2,1,0:T(8,128)(2,1)S(1)}, bf16[2,256,1024]{2,1,0:T(8,128)(2,1)}, u32[]{:S(2)}) copy-start(bf16[2,256,1024]{2,1,0:T(8,128)(2,1)} %param.47) | copy-start | bytes 3145732
  134.7 362.0 %all-gather.20.cloned.1.call-start = ((), (), s32[]{:S(2)}) async-start(), calls=%async_computation.13 | async-start | bytes 2162688 | tf_op jit(solution)/shard_map/all_gather | solution.py:265
  135.3 369.0 %all-gather.22.cloned.1.call-start = ((), (), s32[]{:S(2)}) async-start(), calls=%async_computation.14 | async-start | bytes 8650752 | tf_op jit(solution)/shard_map/all_gather | solution.py:269
  136.1 375.7 %all-gather.24.cloned.1.call-start = ((), (), s32[]{:S(2)}) async-start(), calls=%async_computation.15 | async-start | bytes 8650752 | tf_op jit(solution)/shard_map/all_gather | solution.py:271
  136.8 676.4 %reduce-scatter.9.cloned.1.call-start = ((), (), s32[]{:S(2)}) async-start(), calls=%async_computation.16 | async-start | bytes 5242880 | tf_op jit(solution)/shard_map/reduce_scatter | solution.py:378
  496.7 3.8 copy-start.7
  496.7 3.8 copy-start.22
  503.9 61.2 %copy-start.3 = (f32[512,1024]{1,0:T(8,128)}, f32[512,1024]{1,0:T(8,128)S(1)}, u32[]{:S(2)}) copy-start(f32[512,1024]{1,0:T(8,128)S(1)} %get-tuple-element.485) | copy-start | bytes 6291460
  529.2 10.1 copy-start.21
  539.3 4.8 copy-start.24
  539.3 4.8 copy-start.4
  545.6 14.2 slice-start
  548.1 11.8 copy-start.10
  548.1 11.8 slice-start.1
  559.8 5.2 copy-start.25
  761.8 107.1 %reduce-scatter.11.cloned.1.call-start = ((), (), s32[]{:S(2)}) async-start(), calls=%async_computation.17 | async-start | bytes 5242880 | tf_op jit(solution)/shard_map/reduce_scatter | solution.py:381
  762.4 251.0 %reduce-scatter.13.cloned.1.call-start = ((), (), s32[]{:S(2)}) async-start(), calls=%async_computation.18 | async-start | bytes 4325376 | tf_op jit(solution)/shard_map/reduce_scatter | solution.py:407
  768.4 387.1 %reduce-scatter.19.cloned.1.call-start = ((), (), s32[]{:S(2)}) async-start(), calls=%async_computation.21 | async-start | bytes 4325376 | tf_op jit(solution)/shard_map/reduce_scatter | solution.py:412
  773.5 39.7 %copy-start.17 = (bf16[2,256,1024]{2,1,0:T(8,128)(2,1)S(1)}, bf16[2,256,1024]{2,1,0:T(8,128)(2,1)}, u32[]{:S(2)}) copy-start(bf16[2,256,1024]{2,1,0:T(8,128)(2,1)} %get-tuple-element.479) | copy-start | bytes 3145732
  773.6 524.3 %reduce-scatter.15.cloned.1.call-start = ((), (), s32[]{:S(2)}) async-start(), calls=%async_computation.19 | async-start | bytes 4325376 | tf_op jit(solution)/shard_map/reduce_scatter | solution.py:409
  817.7 622.5 %reduce-scatter.17.cloned.1.call-start = ((), (), s32[]{:S(2)}) async-start(), calls=%async_computation.20 | async-start | bytes 4325376 | tf_op jit(solution)/shard_map/reduce_scatter | solution.py:410
  873.4 924.8 %reduce-scatter.21.cloned.1.call-start = ((), (), s32[]{:S(2)}) async-start(), calls=%async_computation.22 | async-start | bytes 17301504 | tf_op jit(solution)/shard_map/reduce_scatter | solution.py:416
  886.8 1273.3 %reduce-scatter.23.cloned.1.call-start = ((), (), s32[]{:S(2)}) async-start(), calls=%async_computation.23 | async-start | bytes 17301504 | tf_op jit(solution)/shard_map/reduce_scatter | solution.py:418
  901.0 4.6 copy-start.14
  (12 other events, 26.7 us)
Sparse Core Ops, SparseCore 0:
  10.9 59.4 all-gather.15
  73.2 55.2 all-gather.11
  131.4 55.3 all-gather.9
  188.5 51.3 all-gather.17
  241.6 52.5 all-gather.13
  296.9 56.4 all-gather.19
  356.3 76.2 all-gather.21
  435.5 76.1 all-gather.23
  762.0 51.2 reduce-scatter.8
  816.3 52.6 reduce-scatter.10
  871.8 141.5 reduce-scatter.12
  1016.2 139.3 reduce-scatter.18
  1158.4 139.4 reduce-scatter.14
  1300.6 139.5 reduce-scatter.16
  1442.9 355.2 reduce-scatter.20
  1801.0 359.0 reduce-scatter.22
where the time goes:
time: 2180 us; the launch traced here: 2170 us
  waiting for transfers between devices  1440 us (66%)
  matrix products  397 us (18%)
  blocking collectives  149 us (7%)
  local copies, waits for them, and re-layouts  70.6 us (3%)
  loops' own time  63.8 us (3%)
  other arithmetic  29.8 us (1%)
    reduce_scatter x1, waiting for transfers between devices, body(): lax.psum_scatter(grad_w_down, ('dp', 'seq'), scatter_dimension=0, tiled=T...  362 us
    reduce_scatter x1, waiting for transfers between devices, body(): lax.psum_scatter(grad_w_up, ('dp', 'seq'), scatter_dimension=0, tiled=True)  358 us
    reduce_scatter x1, waiting for transfers between devices, body(): lax.psum_scatter(grad_w_key, ('dp', 'seq'), scatter_dimension=0, tiled=True)  142 us
    reduce_scatter x1, waiting for transfers between devices, body(): lax.psum_scatter(grad_w_value, ('dp', 'seq'), scatter_dimension=0, tiled=...  142 us
    reduce_scatter x1, waiting for transfers between devices, body(): lax.psum_scatter(grad_w_out, ('dp', 'seq'), scatter_dimension=0, tiled=True)  142 us
    dot_general x32, matrix products, head_forward(): jnp.einsum('chi,cie->che', probabilities_reduced, single_value_head, pref...  88.1 us
    unnamed x2, blocking collectives  83.3 us
    all_gather x1, blocking collectives, body(): lax.all_gather(b_up, ('dp', 'seq'), axis=0, tiled=True)  66.2 us
  transfers between devices with their start and end apart: 16, of which 13 were waited for; matrix products, arithmetic and copies ran while one was open for 13% of the time, Pallas kernels for 0%

commit v1 on v0

v1 whole, which is shorter than its diff:
```python
import functools

import jax
import jax.numpy as jnp
from jax import lax
from jax.experimental import pallas as pl
from jax.experimental.pallas import tpu as pltpu
from jax.sharding import PartitionSpec as P

HD = 64
TSTEPS = 5000
EPSILON = 1e-05
NEGATIVE = -1e30
ROOT_HALF = 0.7071067811865476
DENSITY_SCALE = 0.3989422804014327
PAD = 16
WIDE = 512
BF16 = jnp.bfloat16
F32 = jnp.float32
VMEM = pltpu.VMEM
SMEM = pltpu.SMEM


def nn(a, b):
    return lax.dot_general(a, b, (((1,), (0,)), ((), ())), preferred_element_type=F32)


def nt(a, b):
    return lax.dot_general(a, b, (((1,), (1,)), ((), ())), preferred_element_type=F32)


def vspec():
    return pl.BlockSpec(memory_space=VMEM)


def sspec():
    return pl.BlockSpec(memory_space=SMEM)


def aspec():
    return pl.BlockSpec(memory_space=pl.ANY)


def params(mib, grid=0):
    if grid:
        return pltpu.CompilerParams(
            vmem_limit_bytes=mib << 20, dimension_semantics=("arbitrary",) * grid
        )
    return pltpu.CompilerParams(vmem_limit_bytes=mib << 20)


def cost(flops, nbytes, trans=0):
    return pl.CostEstimate(flops=int(flops), bytes_accessed=int(nbytes), transcendentals=int(trans))


def tau_rows(len_ref, tim_ref, seq, first, rows):
    spot = first + lax.broadcasted_iota(jnp.int32, (rows, 128), 0)
    begin = jnp.int32(0)
    step = jnp.zeros((rows, 128), jnp.int32)
    for i in range(len_ref.shape[1]):
        end = begin + len_ref[seq, i]
        step = jnp.where((spot >= begin) & (spot < end), tim_ref[seq, i], step)
        begin = end
    return (step.astype(F32) / TSTEPS)[:, :1]


def segments(len_ref, seq, spot):
    end = jnp.int32(0)
    found = jnp.zeros(spot.shape, jnp.int32)
    for i in range(len_ref.shape[1]):
        end = end + len_ref[seq, i]
        found = found + (spot >= end).astype(jnp.int32)
    return found


def item_bias(len_ref, seq, first, keys, rows, out_ref):
    mine = segments(len_ref, seq, first + lax.broadcasted_iota(jnp.int32, (8, rows), 1))
    theirs = segments(len_ref, seq, lax.broadcasted_iota(jnp.int32, (keys, 128), 0))
    for lane in range(rows // 128):
        same = theirs == mine[:1, lane * 128 : (lane + 1) * 128]
        out_ref[:, lane * 128 : (lane + 1) * 128] = jnp.where(same, 0.0, NEGATIVE)


def fold(block):
    rows, width = block.shape
    return block.reshape(rows // 8, 8, width)


def qkv_kernel(ns, nz, r, len_ref, tim_ref, idx, *refs):
    toks = refs[:ns]
    qa, qb = refs[ns : ns + 2]
    q_ref, k_ref, v_ref, low_ref, w_ref, small_ref, bup_ref = refs[ns + 2 : ns + 9]
    wide = refs[ns + 9]
    z, c, j = idx[0], idx[1], idx[2]
    ndev = ns * nz * 2
    seqs, rows, model = toks[0].shape
    hg = q_ref.shape[2]
    for cc, src in enumerate((qa, qb)):
        for a in range(nz):
            for b in range(ns):
                d = ((z ^ a) * 2 + (c ^ cc)) * ns + (j ^ b)
                wide[pl.ds(pl.multiple_of(d * r, r), r), :] = src[a, b, PAD : PAD + r, :].astype(
                    wide.dtype
                )
    w_ref[...] = wide[...].astype(BF16)
    lanes = 14 * r
    count = nz * ns * PAD
    by_owner = jnp.zeros((ndev, lanes), F32)
    for cc, src in enumerate((qa, qb)):
        col = lax.broadcasted_iota(jnp.int32, (ndev, count), 1)
        row = lax.broadcasted_iota(jnp.int32, (ndev, count), 0)
        a = col // (ns * PAD)
        b = (col // PAD) % ns
        d = ((z ^ a) * 2 + (c ^ cc)) * ns + (j ^ b)
        pick = jnp.where((d == row) & (col % PAD == 0), 1.0, 0.0).astype(BF16)
        piece = src[:, :, 0:PAD, :].reshape(count, 3 * hg)
        by_owner = by_owner + nn(pick, piece)[:, :lanes]
    by_owner = by_owner.astype(BF16)

    def whole(part, width):
        i = lax.broadcasted_iota(jnp.int32, (width, ndev * width), 0)
        l = lax.broadcasted_iota(jnp.int32, (width, ndev * width), 1)
        spread = nn(part, jnp.where(l % width == i, 1.0, 0.0).astype(BF16))
        d = lax.broadcasted_iota(jnp.int32, (ndev, ndev * width), 0)
        l = lax.broadcasted_iota(jnp.int32, (ndev, ndev * width), 1)
        return jnp.sum(jnp.where(l // width == d, spread, 0.0), axis=0, keepdims=True)

    for g in range(10):
        small_ref[g : g + 1, :] = whole(by_owner[:, g * r : (g + 1) * r], r)
    small_ref[10:16, :] = jnp.zeros((6, model), F32)
    bup_ref[...] = jnp.broadcast_to(whole(by_owner[:, 10 * r :], 4 * r), bup_ref.shape)
    heads = pl.ds(pl.multiple_of(j * hg, 128), hg)
    bq = small_ref[0:1, heads]
    bv = small_ref[1:2, heads]
    wt = small_ref[8:9, :]
    bt = small_ref[9:10, :]
    for k in range(ns):
        first = pl.multiple_of((j ^ k) * rows, rows)
        here = pl.ds(first, rows)
        for s in range(seqs):
            tau = tau_rows(len_ref, tim_ref, s, first, rows)
            low = (toks[k][s].astype(F32) + tau * wt + bt).astype(BF16)
            low_ref[s, here, :] = low
            got = nn(low, w_ref[...])
            q_ref[s, here, :] = ((got[:, :hg] + bq) * (HD**-0.5)).astype(BF16)
            k_ref[s, here, :] = got[:, hg : 2 * hg].astype(BF16)
            v_ref[s, here, :] = (got[:, 2 * hg :] + bv).astype(BF16)


def project(ns, nz, lengths, timesteps, idx, toks, qa, qb):
    seqs, rows, model = toks[0].shape
    r = qa.shape[2] - PAD
    hg = qa.shape[3] // 3
    full = rows * ns
    heads = jax.ShapeDtypeStruct((seqs, full, hg), BF16)
    outs = [
        heads,
        heads,
        heads,
        jax.ShapeDtypeStruct((seqs, full, model), BF16),
        jax.ShapeDtypeStruct((model, 3 * hg), BF16),
        jax.ShapeDtypeStruct((16, model), F32),
        jax.ShapeDtypeStruct((8, 4 * model), F32),
    ]
    return pl.pallas_call(
        functools.partial(qkv_kernel, ns, nz, r),
        name="project",
        out_shape=outs,
        in_specs=[sspec()] * 3 + [vspec()] * (ns + 2),
        out_specs=[vspec()] * 7,
        scratch_shapes=[VMEM((model, 3 * hg), BF16 if r % 16 == 0 else F32)],
        compiler_params=params(40),
        cost_estimate=cost(2 * seqs * full * model * 3 * hg, 14 << 20),
    )(lengths, timesteps, idx, *toks, qa, qb)


def attend_kernel(ns, len_ref, idx, q_ref, k_ref, v_ref, *refs):
    ctx_refs = refs[:ns]
    ctxt_ref, lse_ref, kh, vt, bias, score = refs[ns:]
    s, i = pl.program_id(0), pl.program_id(1)
    j = idx[2]
    keys, hg = k_ref.shape[1:]
    rows = q_ref.shape[1]
    heads = hg // HD
    step = 256

    @pl.when(i == 0)
    def _():
        for h in range(heads):
            kh[h] = k_ref[0, :, h * HD : (h + 1) * HD]
        vt[...] = v_ref[0].T

    item_bias(len_ref, s, i * rows, keys, rows, bias)
    lse_ref[0] = jnp.zeros(lse_ref.shape[1:], F32)
    parts = []
    for h in range(heads):
        qh = q_ref[0, :, h * HD : (h + 1) * HD]
        top = jnp.full((8, rows), NEGATIVE, F32)
        for b in range(keys // step):
            at = slice(b * step, (b + 1) * step)
            st = nt(kh[h, at, :], qh) + bias[at, :]
            score[h % 2, at, :] = st
            top = jnp.maximum(top, jnp.max(fold(st), axis=0))
        top = jnp.max(top, axis=0, keepdims=True)
        total = jnp.zeros((8, rows), F32)
        acc = jnp.zeros((HD, rows), F32)
        for b in range(keys // step):
            at = slice(b * step, (b + 1) * step)
            p = jnp.exp(score[h % 2, at, :] - top)
            total = total + jnp.sum(fold(p), axis=0)
            acc = acc + nn(vt[h * HD : (h + 1) * HD, at], p.astype(BF16))
        total = jnp.sum(total, axis=0, keepdims=True)
        acc = acc / total
        ctxt_ref[0, h * HD : (h + 1) * HD, :] = acc
        lse_ref[0, h : h + 1, :] = top + jnp.log(total)
        parts.append(acc)
    done = jnp.concatenate(parts, axis=0).T.astype(BF16)
    for k in range(ns):

        @pl.when((j ^ k) == i)
        def _():
            ctx_refs[k][s] = done


def attend(ns, lengths, idx, q, k, v):
    seqs, full, hg = q.shape
    rows = full // ns
    heads = hg // HD
    outs = [jax.ShapeDtypeStruct((seqs, rows, hg), BF16)] * ns + [
        jax.ShapeDtypeStruct((seqs, hg, full), F32),
        jax.ShapeDtypeStruct((seqs, 8, full), F32),
    ]
    whole = pl.BlockSpec((seqs, rows, hg), lambda s, i: (0, 0, 0))
    keyed = pl.BlockSpec((1, full, hg), lambda s, i: (s, 0, 0))
    res = pl.pallas_call(
        functools.partial(attend_kernel, ns),
        name="attend",
        out_shape=outs,
        grid=(seqs, ns),
        in_specs=[
            sspec(),
            sspec(),
            pl.BlockSpec((1, rows, hg), lambda s, i: (s, i, 0)),
            keyed,
            keyed,
        ],
        out_specs=[whole] * ns
        + [
            pl.BlockSpec((1, hg, rows), lambda s, i: (s, 0, i)),
            pl.BlockSpec((1, 8, rows), lambda s, i: (s, 0, i)),
        ],
        scratch_shapes=[
            VMEM((heads, full, HD), BF16),
            VMEM((hg, full), BF16),
            VMEM((full, rows), F32),
            VMEM((2, full, rows), F32),
        ],
        compiler_params=params(40, 2),
        cost_estimate=cost(
            4 * 4 * seqs * full * full * hg, 8 << 20, seqs * full * full * heads
        ),
    )(lengths, idx, q, k, v)
    return res[:ns], res[ns], res[ns + 1]


def attend_back_kernel(ns, seq, len_ref, tim_ref, idx, q_ref, k_ref, v_ref, ctxt_ref, lse_ref, w_ref, *refs):
    dctx = refs[:ns]
    grad_ref = refs[ns]
    p_refs = refs[ns + 1 : 2 * ns + 1]
    sum_ref, bsum_ref, kh, vh, kt, dcx, dk, dv, bias = refs[2 * ns + 1 :]
    i = pl.program_id(0)
    j = idx[2]
    keys, hg = k_ref.shape[1:]
    rows = q_ref.shape[1]
    heads = hg // HD
    step = 256

    @pl.when(i == 0)
    def _():
        for h in range(heads):
            kh[h] = k_ref[0, :, h * HD : (h + 1) * HD]
            vh[h] = v_ref[0, :, h * HD : (h + 1) * HD]
        kt[...] = k_ref[0].T
        for k in range(ns):
            dcx[pl.ds(pl.multiple_of((j ^ k) * rows, rows), rows), :] = dctx[k][0]
        dk[...] = jnp.zeros_like(dk)
        dv[...] = jnp.zeros_like(dv)

    item_bias(len_ref, seq, i * rows, keys, rows, bias)
    here = pl.ds(pl.multiple_of(i * rows, rows), rows)
    dc = dcx[here, :]
    dct = dc.T.astype(F32)
    parts = []
    for h in range(heads):
        cols = slice(h * HD, (h + 1) * HD)
        qh = q_ref[0, :, cols]
        dch = dc[:, cols]
        row_total = jnp.sum(ctxt_ref[0, cols, :] * dct[cols, :], axis=0, keepdims=True)
        lse = lse_ref[0, h : h + 1, :]
        acc = jnp.zeros((HD, rows), F32)
        for b in range(keys // step):
            at = slice(b * step, (b + 1) * step)
            p = jnp.exp(nt(kh[h, at, :], qh) + bias[at, :] - lse)
            dp = nt(vh[h, at, :], dch)
            ds = (p * (dp - row_total)).astype(BF16)
            dv[h, at, :] += nn(p.astype(BF16), dch)
            dk[h, at, :] += nn(ds, qh)
            acc = acc + nn(kt[cols, at], ds)
        parts.append(acc)
    dq = jnp.concatenate(parts, axis=0).T.astype(BF16).astype(F32) * (HD**-0.5)
    grad_ref[here, 0:hg] = dq.astype(BF16)

    @pl.when(i == ns - 1)
    def _():
        for h in range(heads):
            grad_ref[:, hg + h * HD : hg + (h + 1) * HD] = dk[h].astype(BF16)
            grad_ref[:, 2 * hg + h * HD : 2 * hg + (h + 1) * HD] = dv[h].astype(BF16)
        plain = jnp.zeros((8, w_ref.shape[0]), F32)
        timed = jnp.zeros((8, w_ref.shape[0]), F32)
        bias_sum = jnp.zeros((8, 3 * hg), F32)
        for k in range(ns):
            first = pl.multiple_of((j ^ k) * rows, rows)
            block = grad_ref[pl.ds(first, rows), :]
            part = nt(block, w_ref[...])
            p_refs[k][...] = part.astype(BF16)
            plain = plain + jnp.sum(fold(part), axis=0)
            tau = tau_rows(len_ref, tim_ref, seq, first, rows)
            timed = timed + jnp.sum(fold(part * tau), axis=0)
            bias_sum = bias_sum + jnp.sum(fold(block.astype(F32)), axis=0)
        sum_ref[...] = jnp.zeros_like(sum_ref)
        sum_ref[0:1, :] = jnp.sum(timed, axis=0, keepdims=True)
        sum_ref[1:2, :] = jnp.sum(plain, axis=0, keepdims=True)
        bsum_ref[...] = jnp.broadcast_to(jnp.sum(bias_sum, axis=0, keepdims=True), bsum_ref.shape)


def attend_back(ns, seq, lengths, timesteps, idx, q, k, v, ctxt, lse, w, dctx):
    seqs, full, hg = q.shape
    rows = full // ns
    heads = hg // HD
    model = w.shape[0]
    one = lambda shape: pl.BlockSpec(shape, lambda i: (0,) * len(shape))
    keyed = pl.BlockSpec((1, full, hg), lambda i: (seq, 0, 0))
    outs = (
        [jax.ShapeDtypeStruct((full, 3 * hg), BF16)]
        + [jax.ShapeDtypeStruct((rows, model), BF16)] * ns
        + [jax.ShapeDtypeStruct((8, model), F32), jax.ShapeDtypeStruct((8, 3 * hg), F32)]
    )
    res = pl.pallas_call(
        functools.partial(attend_back_kernel, ns, seq),
        name="attend_back",
        out_shape=outs,
        grid=(ns,),
        in_specs=[sspec()] * 3
        + [
            pl.BlockSpec((1, rows, hg), lambda i: (seq, i, 0)),
            keyed,
            keyed,
            pl.BlockSpec((1, hg, rows), lambda i: (seq, 0, i)),
            pl.BlockSpec((1, 8, rows), lambda i: (seq, 0, i)),
            one((model, 3 * hg)),
        ]
        + [pl.BlockSpec((1, rows, hg), lambda i: (seq, 0, 0))] * ns,
        out_specs=[one((full, 3 * hg))]
        + [one((rows, model))] * ns
        + [one((8, model)), one((8, 3 * hg))],
        scratch_shapes=[
            VMEM((heads, full, HD), BF16),
            VMEM((heads, full, HD), BF16),
            VMEM((hg, full), BF16),
            VMEM((full, hg), BF16),
            VMEM((heads, full, HD), F32),
            VMEM((heads, full, HD), F32),
            VMEM((full, rows), F32),
        ],
        compiler_params=params(48, 1),
        cost_estimate=cost(
            10 * 4 * full * full * hg + 2 * full * model * 3 * hg,
            10 << 20,
            full * full * heads,
        ),
    )(lengths, timesteps, idx, q, k, v, ctxt, lse, w, *dctx)
    return res[0], res[1 : ns + 1], res[ns + 1], res[ns + 2]


def middle_kernel(ns, nz, r, rels, len_ref, tim_ref, idx, tok_ref, cot_ref, small_ref, bup_ref, *refs):
    ctxs = refs[:ns]
    nu = len(rels[0])
    u1 = refs[ns : ns + nu]
    u2 = refs[ns + nu : ns + 2 * nu]
    dn = refs[ns + 2 * nu : ns + 2 * nu + 2 * nz]
    rest = refs[ns + 2 * nu + 2 * nz :]
    out_ref, act_o, dg_o, ug_o, fl_o, cx_o, ag_o, r1_o = rest[:8]
    dctx = rest[8 : 8 + ns]
    sum_ref, gbup_ref = rest[8 + ns : 10 + ns]
    wu, wd, act, slope, ug, fl, cx, dg, first, norm, r2, inv, stage, wsem, osem = rest[10 + ns :]
    z, c, j = idx[0], idx[1], idx[2]
    seqs, rows, model = tok_ref.shape
    ff = wd.shape[0]
    hg = ctxs[0].shape[2]
    tokens = seqs * rows
    half = wu.shape[1] // 2
    for part, (arrays, rel) in enumerate(((u1, rels[0]), (u2, rels[1]))):
        for src, (cc, offs) in zip(arrays, rel):
            for m, b in enumerate(offs):
                for a in range(nz):
                    d = ((z ^ a) * 2 + (c ^ cc)) * ns + (j ^ b)
                    pltpu.make_async_copy(
                        src.at[m, a],
                        wu.at[pl.ds(pl.multiple_of(d * r, r), r), pl.ds(part * half, half)],
                        wsem.at[part],
                    ).start()
    for n, src in enumerate(dn):
        t, cc = n // 2, n % 2
        for m, b in enumerate(rels[2]):
            d = (lax.rem(z + nz - t, nz) * 2 + (c ^ cc)) * ns + (j ^ b)
            pltpu.make_async_copy(
                src.at[m],
                wd.at[pl.ds(pl.multiple_of(d * 4 * r, 4 * r), 4 * r), :],
                wsem.at[2],
            ).start()
    for k in range(ns):
        at = pl.ds(pl.multiple_of((j ^ k) * hg, 128), hg)
        for s in range(seqs):
            cx[s * rows : (s + 1) * rows, at] = ctxs[k][s]
    sum_ref[...] = jnp.zeros_like(sum_ref)
    pltpu.make_async_copy(cx, cx_o, osem.at[0]).start()
    u1_all = wu.at[:, pl.ds(0, half)]
    pltpu.make_async_copy(u1_all, u1_all, wsem.at[0]).wait()

    b_out = small_ref[2:3, :]
    gain_one, shift_one = small_ref[3:4, :], small_ref[4:5, :]
    b_down = small_ref[5:6, :]
    gain_two, shift_two = small_ref[6:7, :], small_ref[7:8, :]
    w_time, b_time = small_ref[8:9, :], small_ref[9:10, :]
    block = 128
    per = rows // block

    def add_sum(row, value):
        sum_ref[row : row + 1, :] += jnp.sum(jnp.sum(fold(value), axis=0), axis=0, keepdims=True)

    def mean(value):
        return jnp.sum(value, axis=-1, keepdims=True) * (1.0 / model)

    def one_first(s, b):
        at = pl.ds(pl.multiple_of((s * per + b) * block, block), block)
        inside = pl.ds(pl.multiple_of(b * block, block), block)
        attn = nn(cx[at, :], wu[:, 0:model])
        tau = tau_rows(len_ref, tim_ref, s, j * rows + b * block, block)
        start = tok_ref[s, inside, :].astype(F32) + tau * w_time + b_time
        res = start + (attn + b_out)
        center = res - mean(res)
        inverse = lax.rsqrt(mean(center * center) + EPSILON)
        normed = center * inverse
        norm[at, :] = normed
        inv[at, :] = jnp.broadcast_to(inverse, (block, 128))
        value = normed * gain_one + shift_one
        first[at, :] = value
        fl[at, :] = value.astype(BF16)

    for s in range(seqs):
        lax.fori_loop(0, per, lambda b, _: (one_first(s, b), 0)[1], 0)
    pltpu.make_async_copy(fl, fl_o, osem.at[1]).start()
    u2_all = wu.at[:, pl.ds(half, half)]
    pltpu.make_async_copy(u2_all, u2_all, wsem.at[1]).wait()

    def one_up(n, _):
        at = pl.ds(pl.multiple_of(n * WIDE, WIDE), WIDE)
        wat = pl.ds(pl.multiple_of(model + n * WIDE, WIDE), WIDE)
        for h in range(2):
            rr = slice(h * tokens // 2, (h + 1) * tokens // 2)
            pre = nn(fl[rr, :], wu[:, wat]) + bup_ref[0:1, at]
            cumulative = 0.5 * (1.0 + lax.erf(pre * ROOT_HALF))
            density = jnp.exp(-0.5 * pre * pre) * DENSITY_SCALE
            act[rr, at] = (pre * cumulative).astype(BF16)
            slope[rr, at] = cumulative + pre * density
        return 0

    lax.fori_loop(0, ff // WIDE, one_up, 0)
    pltpu.make_async_copy(act, act_o, osem.at[2]).start()
    pltpu.make_async_copy(wd, wd, wsem.at[2]).wait()

    def one_second(s, b):
        at = pl.ds(pl.multiple_of((s * per + b) * block, block), block)
        inside = pl.ds(pl.multiple_of(b * block, block), block)
        res = first[at, :] + (nn(act[at, :], wd[...]) + b_down)
        center = res - mean(res)
        inverse = lax.rsqrt(mean(center * center) + EPSILON)
        normed = center * inverse
        out_ref[s, inside, :] = (normed * gain_two + shift_two).astype(BF16)
        g = cot_ref[s, inside, :].astype(F32)
        add_sum(4, g * normed)
        add_sum(5, g)
        gn = g * gain_two
        grad = inverse * (gn - mean(gn) - normed * mean(gn * normed))
        r2[at, :] = grad
        low = grad.astype(BF16)
        dg[at, :] = low
        add_sum(3, low.astype(F32))

    for s in range(seqs):
        lax.fori_loop(0, per, lambda b, _: (one_second(s, b), 0)[1], 0)
    pltpu.make_async_copy(dg, dg_o, osem.at[3]).start()

    def one_up_grad(n, _):
        at = pl.ds(pl.multiple_of(n * WIDE, WIDE), WIDE)
        total = jnp.zeros((8, WIDE), F32)
        for h in range(2):
            rr = slice(h * tokens // 2, (h + 1) * tokens // 2)
            low = (nt(dg[rr, :], wd[at, :]) * slope[rr, at]).astype(BF16)
            ug[rr, at] = low
            total = total + jnp.sum(fold(low.astype(F32)), axis=0)
        gbup_ref[:, at] = jnp.broadcast_to(jnp.sum(total, axis=0, keepdims=True), (8, WIDE))
        return 0

    lax.fori_loop(0, ff // WIDE, one_up_grad, 0)
    pltpu.make_async_copy(ug, ug_o, osem.at[4]).start()
    pltpu.make_async_copy(fl, fl_o, osem.at[1]).wait()

    def one_first_grad(s, b):
        at = pl.ds(pl.multiple_of((s * per + b) * block, block), block)
        inside = pl.ds(pl.multiple_of(b * block, block), block)
        fg = nt(ug[at, :], wu[:, model:]) + r2[at, :]
        normed = norm[at, :]
        add_sum(1, fg * normed)
        add_sum(2, fg)
        gn = fg * gain_one
        grad = inv[at, :][:, :1] * (gn - mean(gn) - normed * mean(gn * normed))
        first[at, :] = grad
        low = grad.astype(BF16)
        fl[at, :] = low
        add_sum(0, low.astype(F32))
        tau = tau_rows(len_ref, tim_ref, s, j * rows + b * block, block)
        add_sum(6, grad * tau)
        add_sum(7, grad)
        stage[...] = nt(low, wu[:, 0:model]).astype(BF16)
        for k in range(ns):
            cols = pl.ds(pl.multiple_of((j ^ k) * hg, 128), hg)
            dctx[k][s, inside, :] = stage[:, cols]

    for s in range(seqs):
        lax.fori_loop(0, per, lambda b, _: (one_first_grad(s, b), 0)[1], 0)
    ag_copy = pltpu.make_async_copy(fl, ag_o, osem.at[5])
    ag_copy.start()
    r1_copy = pltpu.make_async_copy(first, r1_o, osem.at[6])
    r1_copy.start()
    pltpu.make_async_copy(cx, cx_o, osem.at[0]).wait()
    pltpu.make_async_copy(act, act_o, osem.at[2]).wait()
    pltpu.make_async_copy(dg, dg_o, osem.at[3]).wait()
    pltpu.make_async_copy(ug, ug_o, osem.at[4]).wait()
    ag_copy.wait()
    r1_copy.wait()


def middle(ns, nz, r, rels, lengths, timesteps, idx, tokens, cotangent, small, bup, ctxs, u1, u2, dn):
    seqs, rows, model = tokens.shape
    total = seqs * rows
    ff = bup.shape[1]
    hg = ctxs[0].shape[2]
    sh = lambda *a: jax.ShapeDtypeStruct(a[:-1], a[-1])
    outs = [
        sh(seqs, rows, model, BF16),
        sh(total, ff, BF16),
        sh(total, model, BF16),
        sh(total, ff, BF16),
        sh(total, model, BF16),
        sh(total, model, BF16),
        sh(total, model, BF16),
        sh(total, model, F32),
    ]
    outs += [sh(seqs, rows, hg, BF16)] * ns + [sh(16, model, F32), sh(8, ff, F32)]
    res = pl.pallas_call(
        functools.partial(middle_kernel, ns, nz, r, rels),
        name="middle",
        out_shape=outs,
        in_specs=[sspec()] * 3
        + [vspec()] * (4 + ns)
        + [aspec()] * (len(u1) + len(u2) + len(dn)),
        out_specs=[vspec()] + [aspec()] * 7 + [vspec()] * (ns + 2),
        scratch_shapes=[
            VMEM((model, model + ff), BF16),
            VMEM((ff, model), BF16),
            VMEM((total, ff), BF16),
            VMEM((total, ff), F32),
            VMEM((total, ff), BF16),
            VMEM((total, model), BF16),
            VMEM((total, model), BF16),
            VMEM((total, model), BF16),
            VMEM((total, model), F32),
            VMEM((total, model), F32),
            VMEM((total, model), F32),
            VMEM((total, 128), F32),
            VMEM((128, model), BF16),
            pltpu.SemaphoreType.DMA((3,)),
            pltpu.SemaphoreType.DMA((7,)),
        ],
        compiler_params=params(54),
        cost_estimate=cost(
            2 * total * (2 * model * model + 4 * model * ff), 40 << 20, 3 * total * ff
        ),
    )(lengths, timesteps, idx, tokens, cotangent, small, bup, *ctxs, *u1, *u2, *dn)
    return res[:8], res[8 : 8 + ns], res[8 + ns], res[9 + ns]


def scatter_rows(ns, nz, r, ring, idx, total, keep_ref, send_ref):
    z, c, j = idx[0], idx[1], idx[2]
    for cc, dst in enumerate((keep_ref, send_ref)):
        for a in range(nz):
            owner = lax.rem(z + a, nz) if ring else z ^ a
            for b in range(ns):
                d = (owner * 2 + (c ^ cc)) * ns + (j ^ b)
                dst[a, b] = total[pl.ds(pl.multiple_of(d * r, r), r), :].astype(BF16)


def up_grad_kernel(ns, nz, r, split, idx, *refs):
    if split:
        cx_ref, ag_ref, fl_ref, ug_ref, keep_ref, send_ref, flipped, total = refs
    else:
        fl_ref, ug_ref, keep_ref, send_ref, flipped, total = refs
    i = pl.program_id(0)
    if split:

        @pl.when(i == 0)
        def _():
            flipped[...] = cx_ref[...].T

        @pl.when(i < split)
        def _():
            at = pl.ds(pl.multiple_of(jnp.minimum(i, split - 1) * WIDE, WIDE), WIDE)
            total[...] = nn(flipped[...], ag_ref[:, at])

    @pl.when(i == split)
    def _():
        flipped[...] = fl_ref[...].T

    @pl.when(i >= split)
    def _():
        total[...] = nn(flipped[...], ug_ref[...])

    scatter_rows(ns, nz, r, False, idx, total, keep_ref, send_ref)


def up_grad(ns, nz, r, idx, cx, ag, fl, ug, part):
    total, model = fl.shape
    ff = ug.shape[1]
    width = (model + ff) // 2
    split = model // WIDE if part == 0 else 0
    skip = 0 if part == 0 else width // WIDE - model // WIDE
    one = lambda shape: pl.BlockSpec(shape, lambda i: (0,) * len(shape))
    block = pl.BlockSpec((nz, ns, r, WIDE), lambda i: (0, 0, 0, i))
    ins = ([cx, ag] if part == 0 else []) + [fl, ug]
    return pl.pallas_call(
        functools.partial(up_grad_kernel, ns, nz, r, split),
        name="up_grad",
        out_shape=[jax.ShapeDtypeStruct((nz, ns, r, width), BF16)] * 2,
        grid=(width // WIDE,),
        in_specs=[sspec()]
        + [one((total, model))] * (len(ins) - 1)
        + [pl.BlockSpec((total, WIDE), lambda i: (0, jnp.maximum(i - split, 0) + skip))],
        out_specs=[block, block],
        scratch_shapes=[VMEM((model, total), BF16), VMEM((model, WIDE), F32)],
        compiler_params=params(40, 1),
        cost_estimate=cost(2 * total * model * width, 10 << 20),
    )(idx, *ins)


def down_grad_kernel(ns, nz, r, idx, act_ref, dg_ref, keep_ref, send_ref, flipped, total):
    @pl.when(pl.program_id(0) == 0)
    def _():
        flipped[...] = act_ref[...].T

    total[...] = nn(flipped[...], dg_ref[...])
    scatter_rows(ns, nz, 4 * r, True, idx, total, keep_ref, send_ref)


def down_grad(ns, nz, r, idx, act, dg):
    total, ff = act.shape
    model = dg.shape[1]
    width = 256
    block = pl.BlockSpec((nz, ns, 4 * r, width), lambda i: (0, 0, 0, i))
    return pl.pallas_call(
        functools.partial(down_grad_kernel, ns, nz, r),
        name="down_grad",
        out_shape=[jax.ShapeDtypeStruct((nz, ns, 4 * r, model), BF16)] * 2,
        grid=(model // width,),
        in_specs=[
            sspec(),
            pl.BlockSpec((total, ff), lambda i: (0, 0)),
            pl.BlockSpec((total, width), lambda i: (0, i)),
        ],
        out_specs=[block, block],
        scratch_shapes=[VMEM((ff, total), BF16), VMEM((ff, width), F32)],
        compiler_params=params(40, 1),
        cost_estimate=cost(2 * total * model * ff, 14 << 20),
    )(idx, act, dg)


def qkv_grad_kernel(ns, nz, r, idx, low_ref, g0_ref, g1_ref, sums_ref, gbup_ref, s0_ref, s1_ref, b0_ref, b1_ref, keep_ref, send_ref, total, own, vec):
    z, c, j = idx[0], idx[1], idx[2]
    ndev = ns * nz * 2
    model = low_ref.shape[2]
    hg = g0_ref.shape[1] // 3
    total[...] = nn(low_ref[0].T, g0_ref[...]) + nn(low_ref[1].T, g1_ref[...])
    vec[...] = jnp.zeros_like(vec)
    heads = pl.ds(pl.multiple_of(j * hg, 128), hg)
    both = b0_ref[0:1, :] + b1_ref[0:1, :]
    vec[0:1, heads] = both[:, :hg]
    vec[1:2, heads] = both[:, 2 * hg :]
    vec[2:8, :] = sums_ref[0:6, :]
    vec[8:10, :] = sums_ref[6:8, :] + s0_ref[0:2, :] + s1_ref[0:2, :]
    own[...] = jnp.zeros_like(own)

    def split(row, width):
        d = lax.broadcasted_iota(jnp.int32, (ndev, ndev * width), 0)
        l = lax.broadcasted_iota(jnp.int32, (ndev, ndev * width), 1)
        spread = jnp.where(l // width == d, row, 0.0).astype(BF16)
        i = lax.broadcasted_iota(jnp.int32, (width, ndev * width), 0)
        l = lax.broadcasted_iota(jnp.int32, (width, ndev * width), 1)
        return nt(spread, jnp.where(l % width == i, 1.0, 0.0).astype(BF16))

    pieces = [split(vec[g : g + 1, :], r) for g in range(10)]
    pieces.append(split(gbup_ref[0:1, :], 4 * r))
    own[:, 0 : 14 * r] = jnp.concatenate(pieces, axis=1)
    for cc, dst in enumerate((keep_ref, send_ref)):
        for a in range(nz):
            for b in range(ns):
                d = ((z ^ a) * 2 + (c ^ cc)) * ns + (j ^ b)
                dst[a, b, PAD:, :] = total[pl.ds(pl.multiple_of(d * r, r), r), :].astype(BF16)
                dst[a, b, 0:PAD, :] = jnp.broadcast_to(
                    own[pl.ds(d, 1), :], (PAD, own.shape[1])
                ).astype(BF16)


def qkv_grad(ns, nz, r, idx, low, g0, g1, sums, gbup, s0, s1, b0, b1):
    seqs, full, model = low.shape
    width = g0.shape[1]
    out = jax.ShapeDtypeStruct((nz, ns, PAD + r, width), BF16)
    return pl.pallas_call(
        functools.partial(qkv_grad_kernel, ns, nz, r),
        name="qkv_grad",
        out_shape=[out, out],
        in_specs=[sspec()] + [vspec()] * 9,
        out_specs=[vspec()] * 2,
        scratch_shapes=[
            VMEM((model, width), F32),
            VMEM((ns * nz * 2, width), F32),
            VMEM((16, model), F32),
        ],
        compiler_params=params(40),
        cost_estimate=cost(2 * seqs * full * model * width, 12 << 20),
    )(idx, low, g0, g1, sums, gbup, s0, s1, b0, b1)


def finish_kernel(ns, r, idx, own_ref, *refs):
    others = refs[: ns - 1]
    q_ref, k_ref, v_ref, small_ref = refs[ns - 1 :]
    j = idx[2]
    hg = own_ref.shape[1] // 3
    small = own_ref[0:1, :]
    for k in range(ns):
        part = own_ref[...] if k == 0 else others[k - 1][...].astype(F32)
        cols = pl.ds(pl.multiple_of((j ^ k) * hg, 128), hg)
        for n, dst in enumerate((q_ref, k_ref, v_ref)):
            dst[:, cols] = part[PAD:, n * hg : (n + 1) * hg]
        if k:
            small = small + part[0:1, :]
    small_ref[...] = jnp.broadcast_to(small, small_ref.shape)


def finish(ns, r, model, idx, own, others):
    width = own.shape[1]
    out = jax.ShapeDtypeStruct((r, model), F32)
    return pl.pallas_call(
        functools.partial(finish_kernel, ns, r),
        name="finish",
        out_shape=[out, out, out, jax.ShapeDtypeStruct((8, width), F32)],
        in_specs=[sspec()] + [vspec()] * ns,
        out_specs=[vspec()] * 4,
        compiler_params=params(16),
    )(idx, own, *others)


def to_seq(value, k):
    ns = lax.axis_size("seq")
    return lax.ppermute(value, "seq", [(i, i ^ k) for i in range(ns)])


def to_mate(value):
    nd = lax.axis_size("dp")
    return lax.ppermute(value, "dp", [(i, i ^ 1) for i in range(nd)])


def to_z(value, a):
    nd = lax.axis_size("dp")
    return lax.ppermute(value, "dp", [(i, i ^ (2 * a)) for i in range(nd)])


def to_ring(value):
    nd = lax.axis_size("dp")
    return lax.ppermute(value, "dp", [(i, (i + 2) % nd) for i in range(nd)])


def bits_of(ns):
    return list(range(ns.bit_length() - 1))


def gather_direct(block, order, nz):
    cur = jnp.stack([block] + [to_z(block, a) for a in range(1, nz)])[None]
    for bit in order[:-1]:
        cur = jnp.concatenate([cur, to_seq(cur, 1 << bit)], axis=0)
    last = to_seq(cur, 1 << order[-1])
    offs = []
    for m in range(cur.shape[0]):
        offs.append(sum(((m >> i) & 1) << bit for i, bit in enumerate(order[:-1])))
    far = tuple(o | (1 << order[-1]) for o in offs)
    rel = ((0, tuple(offs)), (0, far), (1, tuple(offs)), (1, far))
    return [cur, last, to_mate(cur), to_mate(last)], rel


def gather_ring(block, order, nz):
    cur = block[None]
    offs = [0]
    for bit in order:
        cur = jnp.concatenate([cur, to_seq(cur, 1 << bit)], axis=0)
        offs = offs + [o | (1 << bit) for o in offs]
    arrays = [cur, to_mate(cur)]
    for _ in range(1, nz):
        cur = to_ring(cur)
        arrays += [cur, to_mate(cur)]
    return arrays, tuple(offs)


def added(terms):
    return functools.reduce(lambda a, b: a + b, [t.astype(F32) for t in terms])


def scatter_bits(terms, order, axis):
    left = sorted(order)
    for bit in order:
        place = axis + len(left) - 1 - left.index(bit)
        away = added([lax.index_in_dim(t, 1, place, keepdims=False) for t in terms])
        got = to_seq(away.astype(BF16), 1 << bit)
        terms = [lax.index_in_dim(t, 0, place, keepdims=False) for t in terms] + [got]
        left.remove(bit)
    return terms


def in_bits(value, ns, axis):
    shape = value.shape
    return value.reshape(shape[:axis] + (2,) * (ns.bit_length() - 1) + shape[axis + 1 :])


def scatter_direct(keep, send, order, ns, nz):
    terms = [in_bits(t, ns, 1) for t in (keep, to_mate(send))]
    terms = scatter_bits(terms, order, 1)
    got = [to_z(added([t[a] for t in terms]).astype(BF16), a) for a in range(1, nz)]
    return added([t[0] for t in terms] + got)


def scatter_ring(keep, send, order, ns, nz):
    terms = [in_bits(t, ns, 1) for t in (keep, to_mate(send))]
    moving = []
    for slot in range(nz - 1, 0, -1):
        moving = [to_ring(added([t[slot] for t in terms] + moving).astype(BF16))]
    terms = scatter_bits([t[0] for t in terms] + moving, order, 0)
    return added(terms)


def body(
    tokens,
    lengths,
    timesteps,
    w_query,
    b_query,
    w_key,
    w_value,
    b_value,
    w_out,
    b_out,
    gain_one,
    shift_one,
    w_up,
    b_up,
    w_down,
    b_down,
    gain_two,
    shift_two,
    w_time,
    b_time,
    cotangent,
):
    seqs, rows, model = tokens.shape
    ns = lax.axis_size("seq")
    nz = lax.axis_size("dp") // 2
    r = w_query.shape[0]
    hg = model // ns
    dp = lax.axis_index("dp")
    j = lax.axis_index("seq")
    idx = jnp.stack([dp // 2, dp % 2, j]).astype(jnp.int32)
    bits = bits_of(ns)
    back = bits[::-1]

    toks = [tokens] + [to_seq(tokens, k) for k in range(1, ns)]
    row = jnp.concatenate(
        [b_query, b_value, b_out, gain_one, shift_one, b_down, gain_two, shift_two, w_time, b_time, b_up]
    )
    row = jnp.zeros((PAD, 3 * hg), BF16).at[0, : row.shape[0]].set(row)
    blocks = jnp.concatenate(
        [w.reshape(r, ns, hg).transpose(1, 0, 2) for w in (w_query, w_key, w_value)], axis=2
    )
    blocks = jnp.concatenate([jnp.broadcast_to(row, (ns,) + row.shape), blocks], axis=1)
    mine = [lax.dynamic_index_in_dim(blocks, j ^ k, 0, keepdims=False) for k in range(ns)]
    near = jnp.stack([mine[0]] + [to_seq(mine[k], k) for k in range(1, ns)])
    qa = jnp.stack([near] + [to_z(near, a) for a in range(1, nz)])
    qb = to_mate(qa)

    half = (5 * model) // 2
    outer = jnp.concatenate([w_out, w_up], axis=1)
    u1, rel1 = gather_direct(outer[:, :half], back, nz)
    u2, rel2 = gather_direct(outer[:, half:], bits, nz)
    dn, rel3 = gather_ring(w_down, bits, nz)

    q, k, v, low, w_qkv, small, bup = project(ns, nz, lengths, timesteps, idx, toks, qa, qb)
    ctx_out, ctxt, lse = attend(ns, lengths, idx, q, k, v)
    ctxs = [ctx_out[0]] + [to_seq(ctx_out[n], n) for n in range(1, ns)]
    kept, dctx_out, sums, gbup = middle(
        ns, nz, r, (rel1, rel2, rel3), lengths, timesteps, idx, tokens, cotangent, small, bup, ctxs, u1, u2, dn
    )
    output, act, dg, ug, fl, cx, ag, r1 = kept
    dctx = [dctx_out[0]] + [to_seq(dctx_out[n], n) for n in range(1, ns)]
    grad_u1 = scatter_direct(*up_grad(ns, nz, r, idx, cx, ag, fl, ug, 0), bits, ns, nz)
    grad_u2 = scatter_direct(*up_grad(ns, nz, r, idx, cx, ag, fl, ug, 1), back, ns, nz)
    grad_down = scatter_ring(*down_grad(ns, nz, r, idx, act, dg), bits, ns, nz)
    backs = [
        attend_back(ns, s, lengths, timesteps, idx, q, k, v, ctxt, lse, w_qkv, dctx)
        for s in range(seqs)
    ]
    r1 = r1.reshape(seqs, rows, model)
    grad_tokens = []
    for s in range(seqs):
        parts = backs[s][1]
        got = [to_seq(parts[n], n) for n in range(1, ns)]
        grad_tokens.append(added([r1[s], parts[0]] + got).astype(BF16))
    grad_tokens = jnp.stack(grad_tokens)
    keep, send = qkv_grad(
        ns, nz, r, idx, low, backs[0][0], backs[1][0], sums, gbup, backs[0][2], backs[1][2], backs[0][3], backs[1][3]
    )
    terms = [keep, to_mate(send)]
    got = [to_z(added([t[a] for t in terms]).astype(BF16), a) for a in range(1, nz)]
    own = added([t[0] for t in terms] + got)
    others = [to_seq(own[n].astype(BF16), n) for n in range(1, ns)]
    g_query, g_key, g_value, vectors = finish(ns, r, model, idx, own[0], others)
    pick = lambda n: vectors[0, n * r : (n + 1) * r]
    g_up = jnp.concatenate([grad_u1[:, model:], grad_u2], axis=1)
    return (
        output,
        grad_tokens,
        g_query,
        pick(0),
        g_key,
        g_value,
        pick(1),
        grad_u1[:, :model],
        pick(2),
        pick(3),
        pick(4),
        g_up,
        vectors[0, 10 * r : 14 * r],
        grad_down,
        pick(5),
        pick(6),
        pick(7),
        pick(8),
        pick(9),
    )


def solution(mesh):
    split = P(("dp", "seq"))
    rows = P(("dp", "seq"), None)
    token = P("dp", "seq", None)
    items = P("dp", None)
    return jax.shard_map(
        body,
        mesh=mesh,
        in_specs=(
            token, items, items, rows, split, rows, rows, split, rows, split, split, split,
            rows, split, rows, split, split, split, split, split, token,
        ),
        out_specs=(
            token, token, rows, split, rows, rows, split, rows, split, split, split,
            rows, split, rows, split, split, split, split, split,
        ),
        check_vma=False,
    )
```

time: 2180 us -> 544 us (0.25)
  waiting for transfers between devices: 1440 us -> 227 us
  matrix products: 397 us -> 0 us
  Pallas kernels: 0 us -> 154 us
  blocking collectives: 149 us -> 0 us
  starting transfers between devices: 1.22 us -> 103 us
  loops' own time: 63.8 us -> 0 us
  local copies, waits for them, and re-layouts: 70.6 us -> 32.7 us
    reduce_scatter x8 -> x0, waiting for transfers between devices: 1290 us -> none  [the longest x1 362 us: body(): lax.psum_scatter(grad_w_down, ('dp', 'seq'), scatter_dimension=0, tiled=T...]
    dot_general x148 -> x0, matrix products: 367 us -> none  [the longest x32 88.1 us: head_forward(): jnp.einsum('chi,cie->che', probabilities_reduced, single_value_head, pref...]
    ppermute x0 -> x70, waiting for transfers between devices: none -> 227 us  [the longest x33 141 us: to_seq(): return lax.ppermute(value, 'seq', [(i, i ^ k) for i in range(ns)])]
    pallas_call x0 -> x10, Pallas kernels: none -> 154 us  [the longest x1 47.4 us: middle(): pl.pallas_call(functools.partial(middle_kernel, ns, nz, r, rels), name='m...]
    all_gather x8 -> x0, waiting for transfers between devices: 148 us -> none  [the longest x1 54.3 us: fetch_keys(): lax.all_gather(key_low, 'seq', axis=1, tiled=True)]
    ppermute x0 -> x70, starting transfers between devices: none -> 103 us  [the longest x18 54.5 us: to_z(): return lax.ppermute(value, 'dp', [(i, i ^ 2 * a) for i in range(nd)])]
    unnamed x2 -> x0, blocking collectives: 83.3 us -> none
    all_gather x1 -> x0, blocking collectives: 66.2 us -> none  [body(): lax.all_gather(b_up, ('dp', 'seq'), axis=0, tiled=True)]
  transfers between devices with their start and end apart: 16 -> 70, of which waited for: 13 -> 28; matrix products, arithmetic and copies ran while one was open for 13% -> 4% of each run, Pallas kernels for 0% -> 16%
where the time goes in v1:
time: 544 us; the launch traced here: 536 us
  waiting for transfers between devices  227 us (42%)
  Pallas kernels  154 us (28%)
  starting transfers between devices  103 us (19%)
  local copies, waits for them, and re-layouts  32.7 us (6%)
  other arithmetic  17.6 us (3%)
    ppermute x33, waiting for transfers between devices, to_seq(): return lax.ppermute(value, 'seq', [(i, i ^ k) for i in range(ns)])  141 us
    ppermute x18, waiting for transfers between devices, to_z(): return lax.ppermute(value, 'dp', [(i, i ^ 2 * a) for i in range(nd)])  66.7 us
    ppermute x18, starting transfers between devices, to_z(): return lax.ppermute(value, 'dp', [(i, i ^ 2 * a) for i in range(nd)])  54.5 us
    pallas_call x1, Pallas kernels, middle(): pl.pallas_call(functools.partial(middle_kernel, ns, nz, r, rels), name='m...  47.4 us
    pallas_call x2, Pallas kernels, attend_back(): pl.pallas_call(functools.partial(attend_back_kernel, ns, seq), name='atte...  46.1 us
    ppermute x33, starting transfers between devices, to_seq(): return lax.ppermute(value, 'seq', [(i, i ^ k) for i in range(ns)])  42.3 us
    pallas_call x1, Pallas kernels, attend(): pl.pallas_call(functools.partial(attend_kernel, ns), name='attend', out_s...  24.3 us
    unnamed x132, local copies, waits for them, and re-layouts  19.9 us
  transfers between devices with their start and end apart: 70, of which 28 were waited for; matrix products, arithmetic and copies ran while one was open for 4% of the time, Pallas kernels for 16%

profile of v1, /device:TPU:0, one launch (start us, length us, event | category | flops | bytes accessed | tf_op | source)
XLA Modules:
  0.0 535.5 jit_solution(6432834959260256168)
XLA Ops:
  0.7 7.5 %concatenate.30 = bf16[448]{0:T(512)(128)(2,1)S(1)} concatenate(bf16[32]{0:T(256)(128)(2,1)} %param.27, bf16[32]{0:T(256)(128)(2,1)} %param.30, bf16[32]{0:T(256)(128)(2,1)} %param.32, bf16[32]{0:T(256)(128)(2,1)} %param.33, bf16[32]{0:T(256)(128)(2,1)} %param.34, bf16[32]{0:T(256)(128)(2,1)} %param.38, bf16[32]{0:T(256)(128)(2,1)} %param.39, bf16[32]{0:T(256)(128)(2,1)} %param.40, ...), dimensions={0} | concatenate | bytes 1792 | tf_op jit(solution)/shard_map/concatenate | solution.py:903
  10.0 4.0 collective-permute-start.5
  26.0 9.3 %collective-permute-done.14 = bf16[32,2560]{1,0:T(8,128)(2,1)S(1)} collective-permute-done((bf16[32,2560]{1,0:T(8,128)(2,1)S(1)}, bf16[32,2560]{1,0:T(8,128)(2,1)S(1)}, u32[]{:S(2)}, u32[]{:S(2)}) %collective-permute-start.14) | collective-permute-done | bytes 163872 | tf_op jit(solution)/shard_map/ppermute | solution.py:794
  41.7 11.9 %collective-permute-done.7 = bf16[4,48,768]{2,1,0:T(8,128)(2,1)S(1)} collective-permute-done((bf16[4,48,768]{2,1,0:T(8,128)(2,1)S(1)}, bf16[4,48,768]{2,1,0:T(8,128)(2,1)S(1)}, u32[]{:S(2)}, u32[]{:S(2)}) %collective-permute-start.7) | collective-permute-done | bytes 294944 | tf_op jit(solution)/shard_map/ppermute | solution.py:794
  53.6 5.3 collective-permute-start.20
  59.1 10.8 %collective-permute-done.21 = bf16[32,2560]{1,0:T(8,128)(2,1)S(1)} collective-permute-done((bf16[32,2560]{1,0:T(8,128)(2,1)S(1)}, bf16[32,2560]{1,0:T(8,128)(2,1)S(1)}, u32[]{:S(2)}, u32[]{:S(2)}) %collective-permute-start.21) | collective-permute-done | bytes 163872 | tf_op jit(solution)/shard_map/ppermute | solution.py:794
  79.5 17.5 %collective-permute-done.2.refs_3_ = bf16[2,256,1024]{2,1,0:T(8,128)(2,1)} collective-permute-done((bf16[2,256,1024]{2,1,0:T(8,128)(2,1)S(1)}, bf16[2,256,1024]{2,1,0:T(8,128)(2,1)}, u32[]{:S(2)}, u32[]{:S(2)}) %collective-permute-start.2) | collective-permute-done | bytes 1048608 | tf_op jit(solution)/shard_map/ppermute | solution.py:784
  97.4 21.6 %collective-permute-done.1.refs_2_ = bf16[2,256,1024]{2,1,0:T(8,128)(2,1)} collective-permute-done((bf16[2,256,1024]{2,1,0:T(8,128)(2,1)S(1)}, bf16[2,256,1024]{2,1,0:T(8,128)(2,1)}, u32[]{:S(2)}, u32[]{:S(2)}) %collective-permute-start.1) | collective-permute-done | bytes 1048608 | tf_op jit(solution)/shard_map/ppermute | solution.py:784
  119.5 8.6 %project.1 = (bf16[2,1024,256]{2,1,0:T(8,128)(2,1)S(1)}, bf16[2,1024,256]{2,1,0:T(8,128)(2,1)S(1)}, bf16[2,1024,256]{2,1,0:T(8,128)(2,1)S(1)}, bf16[2,1024,1024]...) custom-call(s32[2,8]{1,0:T(2,128)S(1)} %copy-done.6, ...), custom_call_target="tpu_custom_call" | custom-call | flops 3221225472 | bytes 14680064 | tf_op jit(solution)/shard_map/project/pallas_call | solution.py:165
  129.0 24.3 %attend.1 = (bf16[2,256,256]{2,1,0:T(8,128)(2,1)S(1)}, bf16[2,256,256]{2,1,0:T(8,128)(2,1)S(1)}, bf16[2,256,256]{2,1,0:T(8,128)(2,1)S(1)}, bf16[2,256,256]{2,1,0...) custom-call(s32[2,8]{1,0:T(2,128)S(1)} %copy-done.6, s32[3]{0:T(128)S(1)} %pad_add_fusion.idx, ...), custom_call_target="tpu_custom_call" | custom-call | flops 8589934592 | bytes 8388608 | tf_op jit(solution)/shard_map/attend/pallas_call | solution.py:235
  157.2 5.5 %collective-permute-done.10.refs_1_ = bf16[2,256,256]{2,1,0:T(8,128)(2,1)S(1)} collective-permute-done((bf16[2,256,256]{2,1,0:T(8,128)(2,1)S(1)}, bf16[2,256,256]{2,1,0:T(8,128)(2,1)S(1)}, u32[]{:S(2)}, u32[]{:S(2)}) %collective-permute-start.10) | collective-permute-done | bytes 262176 | tf_op jit(solution)/shard_map/ppermute | solution.py:784
  170.0 26.1 %collective-permute-done.24.refs_9_ = bf16[2,4,32,2560]{3,2,1,0:T(8,128)(2,1)S(1)} collective-permute-done((bf16[2,4,32,2560]{3,2,1,0:T(8,128)(2,1)S(1)}, bf16[2,4,32,2560]{3,2,1,0:T(8,128)(2,1)S(1)}, u32[]{:S(2)}, u32[]{:S(2)}) %collective-permute-start.24) | collective-permute-done | bytes 1310752 | tf_op jit(solution)/shard_map/ppermute | solution.py:784
  197.3 5.2 collective-permute-done.31.refs_15_
  206.6 47.4 %middle.1 = (bf16[2,256,1024]{2,1,0:T(8,128)(2,1)}, bf16[512,4096]{1,0:T(8,128)(2,1)}, bf16[512,1024]{1,0:T(8,128)(2,1)}, bf16[512,4096]{1,0:T(8,128)(2,1)}, bf1...) custom-call(s32[2,8]{1,0:T(2,128)} %len_ref.9, ...), custom_call_target="tpu_custom_call" | custom-call | flops 19327352832 | bytes 41943040 | tf_op jit(solution)/shard_map/middle/pallas_call | solution.py:571
  263.4 6.1 %up_grad.2 = (bf16[4,4,32,2560]{3,2,1,0:T(8,128)(2,1)S(1)}, bf16[4,4,32,2560]{3,2,1,0:T(8,128)(2,1)S(1)}) custom-call(s32[3]{0:T(128)S(1)} %copy-done.1, bf16[512,1024]{1,0:T(8,128)(2,1)S(1)} %copy-done.15, bf16[512,1024]{1,0:T(8,128)(2,1)S(1)} %copy-done.16, bf16[512,1024]{1,0:T(8,128)(2,1)S(1)} %copy-done.13, bf16[512,4096]{1,0:T(8,128)(2,1)S(1)} %copy-done.10), custom_call_target="tpu_custom_call" | custom-call | flops 2684354560 | bytes 10485760 | tf_op jit(solution)/shard_map/up_grad/pallas_call | solution.py:651
  271.0 22.9 %attend_back.3 = (bf16[1024,768]{1,0:T(8,128)(2,1)}, bf16[256,1024]{1,0:T(8,128)(2,1)S(1)}, bf16[256,1024]{1,0:T(8,128)(2,1)S(1)}, bf16[256,1024]{1,0:T(8,128)(2...) custom-call(s32[2,8]{1,0:T(2,128)S(1)} %copy-done.7, s32[2,8]{1,0:T(2,128)S(1)} %copy-done.9, ...), custom_call_target="tpu_custom_call" | custom-call | flops 12348030976 | bytes 10485760 | tf_op jit(solution)/shard_map/attend_back/pallas_call | solution.py:348
  294.7 23.2 %attend_back.2 = (bf16[1024,768]{1,0:T(8,128)(2,1)}, bf16[256,1024]{1,0:T(8,128)(2,1)S(1)}, bf16[256,1024]{1,0:T(8,128)(2,1)}, bf16[256,1024]{1,0:T(8,128)(2,1)S...) custom-call(s32[2,8]{1,0:T(2,128)S(1)} %copy-done.7, s32[2,8]{1,0:T(2,128)S(1)} %copy-done.9, ...), custom_call_target="tpu_custom_call" | custom-call | flops 12348030976 | bytes 10485760 | tf_op jit(solution)/shard_map/attend_back/pallas_call | solution.py:348
  322.9 4.7 qkv_grad.1
  334.0 9.1 %down_grad.1 = (bf16[4,4,128,1024]{3,2,1,0:T(8,128)(2,1)S(1)}, bf16[4,4,128,1024]{3,2,1,0:T(8,128)(2,1)S(1)}) custom-call(s32[3]{0:T(128)S(1)} %copy-done.1, bf16[512,4096]{1,0:T(8,128)(2,1)S(1)} %copy-done.20, bf16[512,1024]{1,0:T(8,128)(2,1)S(1)} %copy-done.22), custom_call_target="tpu_custom_call" | custom-call | flops 4294967296 | bytes 14680064 | tf_op jit(solution)/shard_map/down_grad/pallas_call | solution.py:680
  348.5 6.2 %up_grad.3 = (bf16[4,4,32,2560]{3,2,1,0:T(8,128)(2,1)S(1)}, bf16[4,4,32,2560]{3,2,1,0:T(8,128)(2,1)}) custom-call(s32[3]{0:T(128)S(1)} %copy-done.1, bf16[512,1024]{1,0:T(8,128)(2,1)S(1)} %copy-done.14, bf16[512,4096]{1,0:T(8,128)(2,1)S(1)} %copy-done.11), custom_call_target="tpu_custom_call" | custom-call | flops 2684354560 | bytes 10485760 | tf_op jit(solution)/shard_map/up_grad/pallas_call | solution.py:651
  357.9 19.4 %collective-permute-done.40 = bf16[256,1024]{1,0:T(8,128)(2,1)} collective-permute-done((bf16[256,1024]{1,0:T(8,128)(2,1)S(1)}, bf16[256,1024]{1,0:T(8,128)(2,1)}, u32[]{:S(2)}, u32[]{:S(2)}) %collective-permute-start.40) | collective-permute-done | bytes 524320 | tf_op jit(solution)/shard_map/ppermute | solution.py:784
  377.8 4.6 collective-permute-start.48
  385.9 7.0 %collective-permute-start.47 = (bf16[4,48,768]{2,1,0:T(8,128)(2,1)S(1)}, bf16[4,48,768]{2,1,0:T(8,128)(2,1)S(1)}, u32[]{:S(2)}, u32[]{:S(2)}) collective-permute-start(bf16[4,48,768]{2,1,0:T(8,128)(2,1)S(1)} %get-tuple-element.150), channel_id=1, source_target_pairs={{0,16},{4,20},{8,24},{12,28},{16,0},{20,4},{24,8},{28,12},{1,17},{... | collective-permute-start | bytes 884744 | tf_op jit(solution)/shard_map/ppermute | solution.py:794
  396.4 10.7 %collective-permute-done.47 = bf16[4,48,768]{2,1,0:T(8,128)(2,1)S(1)} collective-permute-done((bf16[4,48,768]{2,1,0:T(8,128)(2,1)S(1)}, bf16[4,48,768]{2,1,0:T(8,128)(2,1)S(1)}, u32[]{:S(2)}, u32[]{:S(2)}) %collective-permute-start.47) | collective-permute-done | bytes 294944 | tf_op jit(solution)/shard_map/ppermute | solution.py:794
  425.3 23.7 %collective-permute-done.53 = bf16[4,2,32,2560]{3,2,1,0:T(8,128)(2,1)S(1)} collective-permute-done((bf16[4,2,32,2560]{3,2,1,0:T(8,128)(2,1)S(1)}, bf16[4,2,32,2560]{3,2,1,0:T(8,128)(2,1)S(1)}, u32[]{:S(2)}, u32[]{:S(2)}) %collective-permute-start.53) | collective-permute-done | bytes 1310752 | tf_op jit(solution)/shard_map/ppermute | solution.py:784
  453.9 9.9 %collective-permute-done.54 = bf16[4,32,2560]{2,1,0:T(8,128)(2,1)S(1)} collective-permute-done((bf16[4,32,2560]{2,1,0:T(8,128)(2,1)S(1)}, bf16[4,32,2560]{2,1,0:T(8,128)(2,1)S(1)}, u32[]{:S(2)}, u32[]{:S(2)}) %collective-permute-start.54) | collective-permute-done | bytes 655392 | tf_op jit(solution)/shard_map/ppermute | solution.py:784
  467.6 10.7 %collective-permute-done.66 = bf16[2,2,128,1024]{3,2,1,0:T(8,128)(2,1)S(1)} collective-permute-done((bf16[2,2,128,1024]{3,2,1,0:T(8,128)(2,1)S(1)}, bf16[2,2,128,1024]{3,2,1,0:T(8,128)(2,1)S(1)}, u32[]{:S(2)}, u32[]{:S(2)}) %collective-permute-start.66) | collective-permute-done | bytes 1048608 | tf_op jit(solution)/shard_map/ppermute | solution.py:799
  481.2 6.2 %collective-permute-start.63 = (bf16[32,2560]{1,0:T(8,128)(2,1)S(1)}, bf16[32,2560]{1,0:T(8,128)(2,1)S(1)}, u32[]{:S(2)}, u32[]{:S(2)}) collective-permute-start(bf16[32,2560]{1,0:T(8,128)(2,1)S(1)} %get-tuple-element.143), channel_id=1, source_target_pairs={{0,24},{4,28},{8,16},{12,20},{16,8},{20,12},{24,0},{28,4},{1,25},{... | collective-permute-start | bytes 491528 | tf_op jit(solution)/shard_map/ppermute | solution.py:794
  487.4 14.0 %collective-permute-start.62 = (bf16[32,2560]{1,0:T(8,128)(2,1)S(1)}, bf16[32,2560]{1,0:T(8,128)(2,1)S(1)}, u32[]{:S(2)}, u32[]{:S(2)}) collective-permute-start(bf16[32,2560]{1,0:T(8,128)(2,1)S(1)} %get-tuple-element.144), channel_id=1, source_target_pairs={{0,16},{4,20},{8,24},{12,28},{16,0},{20,4},{24,8},{28,12},{1,17},{... | collective-permute-start | bytes 491528 | tf_op jit(solution)/shard_map/ppermute | solution.py:794
  501.3 16.0 %collective-permute-done.56 = bf16[32,2560]{1,0:T(8,128)(2,1)S(1)} collective-permute-done((bf16[32,2560]{1,0:T(8,128)(2,1)S(1)}, bf16[32,2560]{1,0:T(8,128)(2,1)S(1)}, u32[]{:S(2)}, u32[]{:S(2)}) %collective-permute-start.56) | collective-permute-done | bytes 163872 | tf_op jit(solution)/shard_map/ppermute | solution.py:794
  523.7 4.0 collective-permute-done.68
  530.5 3.8 collective-permute-done.69
  (300 shorter events, 126.7 us)
Async XLA Ops:
  22.0 31.6 %collective-permute-start.7 = (bf16[4,48,768]{2,1,0:T(8,128)(2,1)S(1)}, bf16[4,48,768]{2,1,0:T(8,128)(2,1)S(1)}, u32[]{:S(2)}, u32[]{:S(2)}) collective-permute-start(bf16[4,48,768]{2,1,0:T(8,128)(2,1)S(1)} %get-tuple-element.157), channel_id=1, source_target_pairs={{0,16},{4,20},{8,24},{12,28},{16,0},{20,4},{24,8},{28,12},{1,17},{... | collective-permute-start | bytes 884744 | tf_op jit(solution)/shard_map/ppermute | solution.py:794
  24.1 29.6 %collective-permute-start.6 = (bf16[4,48,768]{2,1,0:T(8,128)(2,1)S(1)}, bf16[4,48,768]{2,1,0:T(8,128)(2,1)S(1)}, u32[]{:S(2)}, u32[]{:S(2)}) collective-permute-start(bf16[4,48,768]{2,1,0:T(8,128)(2,1)S(1)} %get-tuple-element.157), channel_id=1, source_target_pairs={{0,8},{4,12},{8,0},{12,4},{16,24},{20,28},{24,16},{28,20},{1,9},{5... | collective-permute-start | bytes 884744 | tf_op jit(solution)/shard_map/ppermute | solution.py:794
  38.7 33.1 %collective-permute-start.28 = (bf16[2,128,1024]{2,1,0:T(8,128)(2,1)S(1)}, bf16[2,128,1024]{2,1,0:T(8,128)(2,1)S(1)}, u32[]{:S(2)}, u32[]{:S(2)}) collective-permute-start(bf16[2,128,1024]{2,1,0:T(8,128)(2,1)S(1)} %pad_maximum_fusion.5), channel_id=1, source_target_pairs={{0,2},{1,3},{2,0},{3,1},{4,6},{5,7},{6,4},{7,5},{8,10},{9,11},{10,... | collective-permute-start | bytes 1572872 | tf_op jit(solution)/shard_map/ppermute | solution.py:784
  41.2 34.6 %collective-permute-start.16 = (bf16[1,4,32,2560]{3,2,1,0:T(8,128)(2,1)}, bf16[1,4,32,2560]{3,2,1,0:T(8,128)(2,1)}, u32[]{:S(2)}, u32[]{:S(2)}) collective-permute-start(bf16[1,4,32,2560]{3,2,1,0:T(8,128)(2,1)} %maximum_bitcast_fusion), channel_id=1, source_target_pairs={{0,2},{1,3},{2,0},{3,1},{4,6},{5,7},{6,4},{7,5},{8,10},{9,11},{10,... | collective-permute-start | bytes 1966088 | tf_op jit(solution)/shard_map/ppermute | solution.py:784
  69.8 49.6 %collective-permute-start.9 = (bf16[4,4,48,768]{3,2,1,0:T(8,128)(2,1)S(1)}, bf16[4,4,48,768]{3,2,1,0:T(8,128)(2,1)S(1)}, u32[]{:S(2)}, u32[]{:S(2)}) collective-permute-start(bf16[4,4,48,768]{3,2,1,0:T(8,128)(2,1)S(1)} %pad_maximum_fusion.2.refs_4_), channel_id=1, source_target_pairs={{0,4},{4,0},{8,12},{12,8},{16,20},{20,16},{24,28},{28,24},{1,5},{5... | collective-permute-start | bytes 3538952 | tf_op jit(solution)/shard_map/ppermute | solution.py:789
  69.9 27.1 %collective-permute-start.2 = (bf16[2,256,1024]{2,1,0:T(8,128)(2,1)S(1)}, bf16[2,256,1024]{2,1,0:T(8,128)(2,1)}, u32[]{:S(2)}, u32[]{:S(2)}) collective-permute-start(bf16[2,256,1024]{2,1,0:T(8,128)(2,1)S(1)} %copy-done.5), channel_id=1, source_target_pairs={{0,3},{1,2},{2,1},{3,0},{4,7},{5,6},{6,5},{7,4},{8,11},{9,10},{10,... | collective-permute-start | bytes 3145736 | tf_op jit(solution)/shard_map/ppermute | solution.py:784
  71.4 47.5 %collective-permute-start.1 = (bf16[2,256,1024]{2,1,0:T(8,128)(2,1)S(1)}, bf16[2,256,1024]{2,1,0:T(8,128)(2,1)}, u32[]{:S(2)}, u32[]{:S(2)}) collective-permute-start(bf16[2,256,1024]{2,1,0:T(8,128)(2,1)S(1)} %copy-done.5), channel_id=1, source_target_pairs={{0,2},{1,3},{2,0},{3,1},{4,6},{5,7},{6,4},{7,5},{8,10},{9,11},{10,... | collective-permute-start | bytes 3145736 | tf_op jit(solution)/shard_map/ppermute | solution.py:784
  72.9 46.6 %collective-permute-start = (bf16[2,256,1024]{2,1,0:T(8,128)(2,1)S(1)}, bf16[2,256,1024]{2,1,0:T(8,128)(2,1)}, u32[]{:S(2)}, u32[]{:S(2)}) collective-permute-start(bf16[2,256,1024]{2,1,0:T(8,128)(2,1)S(1)} %copy-done.5), channel_id=1, source_target_pairs={{0,1},{1,0},{2,3},{3,2},{4,5},{5,4},{6,7},{7,6},{8,9},{9,8},{10,11... | collective-permute-start | bytes 3145736 | tf_op jit(solution)/shard_map/ppermute | solution.py:784
  75.8 52.4 %collective-permute-start.30 = (bf16[4,128,1024]{2,1,0:T(8,128)(2,1)S(1)}, bf16[4,128,1024]{2,1,0:T(8,128)(2,1)S(1)}, u32[]{:S(2)}, u32[]{:S(2)}) collective-permute-start(bf16[4,128,1024]{2,1,0:T(8,128)(2,1)S(1)} %pad_maximum_fusion.3.refs_12_), channel_id=1, source_target_pairs={{0,8},{4,12},{8,16},{12,20},{16,24},{20,28},{24,0},{28,4},{1,9},{5... | collective-permute-start | bytes 3145736 | tf_op jit(solution)/shard_map/ppermute | solution.py:799
  96.9 58.1 %collective-permute-start.23 = (bf16[1,4,32,2560]{3,2,1,0:T(8,128)(2,1)S(1)}, bf16[1,4,32,2560]{3,2,1,0:T(8,128)(2,1)S(1)}, u32[]{:S(2)}, u32[]{:S(2)}) collective-permute-start(bf16[1,4,32,2560]{3,2,1,0:T(8,128)(2,1)S(1)} %maximum_bitcast_fusion.1), channel_id=1, source_target_pairs={{0,1},{1,0},{2,3},{3,2},{4,5},{5,4},{6,7},{7,6},{8,9},{9,8},{10,11... | collective-permute-start | bytes 1966088 | tf_op jit(solution)/shard_map/ppermute | solution.py:784
  119.0 50.0 %collective-permute-start.29 = (bf16[4,128,1024]{2,1,0:T(8,128)(2,1)S(1)}, bf16[4,128,1024]{2,1,0:T(8,128)(2,1)S(1)}, u32[]{:S(2)}, u32[]{:S(2)}) collective-permute-start(bf16[4,128,1024]{2,1,0:T(8,128)(2,1)S(1)} %pad_maximum_fusion.3.refs_12_), channel_id=1, source_target_pairs={{0,4},{4,0},{8,12},{12,8},{16,20},{20,16},{24,28},{28,24},{1,5},{5... | collective-permute-start | bytes 3145736 | tf_op jit(solution)/shard_map/ppermute | solution.py:789
  128.2 41.4 %collective-permute-start.32 = (bf16[4,128,1024]{2,1,0:T(8,128)(2,1)S(1)}, bf16[4,128,1024]{2,1,0:T(8,128)(2,1)S(1)}, u32[]{:S(2)}, u32[]{:S(2)}) collective-permute-start(bf16[4,128,1024]{2,1,0:T(8,128)(2,1)S(1)} %collective-permute-done.30.refs_14_), channel_id=1, source_target_pairs={{0,8},{4,12},{8,16},{12,20},{16,24},{20,28},{24,0},{28,4},{1,9},{5... | collective-permute-start | bytes 3145736 | tf_op jit(solution)/shard_map/ppermute | solution.py:799
  162.7 33.4 %collective-permute-start.24 = (bf16[2,4,32,2560]{3,2,1,0:T(8,128)(2,1)S(1)}, bf16[2,4,32,2560]{3,2,1,0:T(8,128)(2,1)S(1)}, u32[]{:S(2)}, u32[]{:S(2)}) collective-permute-start(bf16[2,4,32,2560]{3,2,1,0:T(8,128)(2,1)S(1)} %pad_maximum_fusion.1.refs_8_), channel_id=1, source_target_pairs={{0,2},{1,3},{2,0},{3,1},{4,6},{5,7},{6,4},{7,5},{8,10},{9,11},{10,... | collective-permute-start | bytes 3932168 | tf_op jit(solution)/shard_map/ppermute | solution.py:784
  165.2 30.9 %collective-permute-start.17 = (bf16[2,4,32,2560]{3,2,1,0:T(8,128)(2,1)S(1)}, bf16[2,4,32,2560]{3,2,1,0:T(8,128)(2,1)S(1)}, u32[]{:S(2)}, u32[]{:S(2)}) collective-permute-start(bf16[2,4,32,2560]{3,2,1,0:T(8,128)(2,1)S(1)} %pad_maximum_fusion.refs_4_), channel_id=1, source_target_pairs={{0,1},{1,0},{2,3},{3,2},{4,5},{5,4},{6,7},{7,6},{8,9},{9,8},{10,11... | collective-permute-start | bytes 3932168 | tf_op jit(solution)/shard_map/ppermute | solution.py:784
  169.0 27.7 %collective-permute-start.25 = (bf16[2,4,32,2560]{3,2,1,0:T(8,128)(2,1)S(1)}, bf16[2,4,32,2560]{3,2,1,0:T(8,128)(2,1)S(1)}, u32[]{:S(2)}, u32[]{:S(2)}) collective-permute-start(bf16[2,4,32,2560]{3,2,1,0:T(8,128)(2,1)S(1)} %pad_maximum_fusion.1.refs_8_), channel_id=1, source_target_pairs={{0,4},{4,0},{8,12},{12,8},{16,20},{20,16},{24,28},{28,24},{1,5},{5... | collective-permute-start | bytes 3932168 | tf_op jit(solution)/shard_map/ppermute | solution.py:789
  169.0 27.8 %collective-permute-start.18 = (bf16[2,4,32,2560]{3,2,1,0:T(8,128)(2,1)S(1)}, bf16[2,4,32,2560]{3,2,1,0:T(8,128)(2,1)S(1)}, u32[]{:S(2)}, u32[]{:S(2)}) collective-permute-start(bf16[2,4,32,2560]{3,2,1,0:T(8,128)(2,1)S(1)} %pad_maximum_fusion.refs_4_), channel_id=1, source_target_pairs={{0,4},{4,0},{8,12},{12,8},{16,20},{20,16},{24,28},{28,24},{1,5},{5... | collective-permute-start | bytes 3932168 | tf_op jit(solution)/shard_map/ppermute | solution.py:789
  169.6 27.6 %collective-permute-start.34 = (bf16[4,128,1024]{2,1,0:T(8,128)(2,1)S(1)}, bf16[4,128,1024]{2,1,0:T(8,128)(2,1)S(1)}, u32[]{:S(2)}, u32[]{:S(2)}) collective-permute-start(bf16[4,128,1024]{2,1,0:T(8,128)(2,1)S(1)} %collective-permute-done.32.refs_16_), channel_id=1, source_target_pairs={{0,8},{4,12},{8,16},{12,20},{16,24},{20,28},{24,0},{28,4},{1,9},{5... | collective-permute-start | bytes 3145736 | tf_op jit(solution)/shard_map/ppermute | solution.py:799
  293.9 38.6 %collective-permute-start.42 = (bf16[256,1024]{1,0:T(8,128)(2,1)S(1)}, bf16[256,1024]{1,0:T(8,128)(2,1)S(1)}, u32[]{:S(2)}, u32[]{:S(2)}) collective-permute-start(bf16[256,1024]{1,0:T(8,128)(2,1)S(1)} %get-tuple-element.107), channel_id=1, source_target_pairs={{0,1},{1,0},{2,3},{3,2},{4,5},{5,4},{6,7},{7,6},{8,9},{9,8},{10,11... | collective-permute-start | bytes 1572872 | tf_op jit(solution)/shard_map/ppermute | solution.py:784
  329.0 27.2 %collective-permute-start.43 = (bf16[256,1024]{1,0:T(8,128)(2,1)}, bf16[256,1024]{1,0:T(8,128)(2,1)}, u32[]{:S(2)}, u32[]{:S(2)}) collective-permute-start(bf16[256,1024]{1,0:T(8,128)(2,1)} %get-tuple-element.108), channel_id=1, source_target_pairs={{0,2},{1,3},{2,0},{3,1},{4,6},{5,7},{6,4},{7,5},{8,10},{9,11},{10,... | collective-permute-start | bytes 1572872 | tf_op jit(solution)/shard_map/ppermute | solution.py:784
  332.5 44.8 %collective-permute-start.40 = (bf16[256,1024]{1,0:T(8,128)(2,1)S(1)}, bf16[256,1024]{1,0:T(8,128)(2,1)}, u32[]{:S(2)}, u32[]{:S(2)}) collective-permute-start(bf16[256,1024]{1,0:T(8,128)(2,1)S(1)} %get-tuple-element.104), channel_id=1, source_target_pairs={{0,2},{1,3},{2,0},{3,1},{4,6},{5,7},{6,4},{7,5},{8,10},{9,11},{10,... | collective-permute-start | bytes 1572872 | tf_op jit(solution)/shard_map/ppermute | solution.py:784
  354.8 65.8 %collective-permute-start.52 = (bf16[4,4,32,2560]{3,2,1,0:T(8,128)(2,1)S(1)}, bf16[4,4,32,2560]{3,2,1,0:T(8,128)(2,1)S(1)}, u32[]{:S(2)}, u32[]{:S(2)}) collective-permute-start(bf16[4,4,32,2560]{3,2,1,0:T(8,128)(2,1)S(1)} %copy-done.4), channel_id=1, source_target_pairs={{0,4},{4,0},{8,12},{12,8},{16,20},{20,16},{24,28},{28,24},{1,5},{5... | collective-permute-start | bytes 7864328 | tf_op jit(solution)/shard_map/ppermute | solution.py:789
  356.2 65.4 %collective-permute-start.58 = (bf16[4,4,32,2560]{3,2,1,0:T(8,128)(2,1)}, bf16[4,4,32,2560]{3,2,1,0:T(8,128)(2,1)S(1)}, u32[]{:S(2)}, u32[]{:S(2)}) collective-permute-start(bf16[4,4,32,2560]{3,2,1,0:T(8,128)(2,1)} %get-tuple-element.132), channel_id=1, source_target_pairs={{0,4},{4,0},{8,12},{12,8},{16,20},{20,16},{24,28},{28,24},{1,5},{5... | collective-permute-start | bytes 7864328 | tf_op jit(solution)/shard_map/ppermute | solution.py:789
  356.7 66.9 %collective-permute-start.64 = (bf16[4,4,128,1024]{3,2,1,0:T(8,128)(2,1)}, bf16[4,4,128,1024]{3,2,1,0:T(8,128)(2,1)S(1)}, u32[]{:S(2)}, u32[]{:S(2)}) collective-permute-start(bf16[4,4,128,1024]{3,2,1,0:T(8,128)(2,1)} %copy-done.2), channel_id=1, source_target_pairs={{0,4},{4,0},{8,12},{12,8},{16,20},{20,16},{24,28},{28,24},{1,5},{5... | collective-permute-start | bytes 12582920 | tf_op jit(solution)/shard_map/ppermute | solution.py:789
  420.9 28.1 %collective-permute-start.53 = (bf16[4,2,32,2560]{3,2,1,0:T(8,128)(2,1)S(1)}, bf16[4,2,32,2560]{3,2,1,0:T(8,128)(2,1)S(1)}, u32[]{:S(2)}, u32[]{:S(2)}) collective-permute-start(bf16[4,2,32,2560]{3,2,1,0:T(8,128)(2,1)S(1)} %fusion), channel_id=1, source_target_pairs={{0,1},{1,0},{2,3},{3,2},{4,5},{5,4},{6,7},{7,6},{8,9},{9,8},{10,11... | collective-permute-start | bytes 3932168 | tf_op jit(solution)/shard_map/ppermute | solution.py:784
  422.0 29.4 %collective-permute-start.59 = (bf16[4,2,32,2560]{3,2,1,0:T(8,128)(2,1)S(1)}, bf16[4,2,32,2560]{3,2,1,0:T(8,128)(2,1)S(1)}, u32[]{:S(2)}, u32[]{:S(2)}) collective-permute-start(bf16[4,2,32,2560]{3,2,1,0:T(8,128)(2,1)S(1)} %fusion.1), channel_id=1, source_target_pairs={{0,2},{1,3},{2,0},{3,1},{4,6},{5,7},{6,4},{7,5},{8,10},{9,11},{10,... | collective-permute-start | bytes 3932168 | tf_op jit(solution)/shard_map/ppermute | solution.py:784
  450.3 28.0 %collective-permute-start.66 = (bf16[2,2,128,1024]{3,2,1,0:T(8,128)(2,1)S(1)}, bf16[2,2,128,1024]{3,2,1,0:T(8,128)(2,1)S(1)}, u32[]{:S(2)}, u32[]{:S(2)}) collective-permute-start(bf16[2,2,128,1024]{3,2,1,0:T(8,128)(2,1)S(1)} %add_convert_fusion.3), channel_id=1, source_target_pairs={{0,8},{4,12},{8,16},{12,20},{16,24},{20,28},{24,0},{28,4},{1,9},{5... | collective-permute-start | bytes 3145736 | tf_op jit(solution)/shard_map/ppermute | solution.py:799
  451.6 27.2 %collective-permute-start.60 = (bf16[4,32,2560]{2,1,0:T(8,128)(2,1)S(1)}, bf16[4,32,2560]{2,1,0:T(8,128)(2,1)S(1)}, u32[]{:S(2)}, u32[]{:S(2)}) collective-permute-start(bf16[4,32,2560]{2,1,0:T(8,128)(2,1)S(1)} %fusion.3), channel_id=1, source_target_pairs={{0,1},{1,0},{2,3},{3,2},{4,5},{5,4},{6,7},{7,6},{8,9},{9,8},{10,11... | collective-permute-start | bytes 1966088 | tf_op jit(solution)/shard_map/ppermute | solution.py:784
  465.4 51.9 %collective-permute-start.56 = (bf16[32,2560]{1,0:T(8,128)(2,1)S(1)}, bf16[32,2560]{1,0:T(8,128)(2,1)S(1)}, u32[]{:S(2)}, u32[]{:S(2)}) collective-permute-start(bf16[32,2560]{1,0:T(8,128)(2,1)S(1)} %get-tuple-element.147), channel_id=1, source_target_pairs={{0,16},{4,20},{8,24},{12,28},{16,0},{20,4},{24,8},{28,12},{1,17},{... | collective-permute-start | bytes 491528 | tf_op jit(solution)/shard_map/ppermute | solution.py:794
  478.7 39.5 %collective-permute-start.67 = (bf16[2,2,128,1024]{3,2,1,0:T(8,128)(2,1)S(1)}, bf16[2,2,128,1024]{3,2,1,0:T(8,128)(2,1)S(1)}, u32[]{:S(2)}, u32[]{:S(2)}) collective-permute-start(bf16[2,2,128,1024]{3,2,1,0:T(8,128)(2,1)S(1)} %add_convert_fusion.2), channel_id=1, source_target_pairs={{0,8},{4,12},{8,16},{12,20},{16,24},{20,28},{24,0},{28,4},{1,9},{5... | collective-permute-start | bytes 3145736 | tf_op jit(solution)/shard_map/ppermute | solution.py:799
  479.0 41.0 %collective-permute-start.61 = (bf16[32,2560]{1,0:T(8,128)(2,1)S(1)}, bf16[32,2560]{1,0:T(8,128)(2,1)S(1)}, u32[]{:S(2)}, u32[]{:S(2)}) collective-permute-start(bf16[32,2560]{1,0:T(8,128)(2,1)S(1)} %get-tuple-element.142), channel_id=1, source_target_pairs={{0,8},{4,12},{8,0},{12,4},{16,24},{20,28},{24,16},{28,20},{1,9},{5... | collective-permute-start | bytes 491528 | tf_op jit(solution)/shard_map/ppermute | solution.py:794
  481.2 38.8 %collective-permute-start.63 = (bf16[32,2560]{1,0:T(8,128)(2,1)S(1)}, bf16[32,2560]{1,0:T(8,128)(2,1)S(1)}, u32[]{:S(2)}, u32[]{:S(2)}) collective-permute-start(bf16[32,2560]{1,0:T(8,128)(2,1)S(1)} %get-tuple-element.143), channel_id=1, source_target_pairs={{0,24},{4,28},{8,16},{12,20},{16,8},{20,12},{24,0},{28,4},{1,25},{... | collective-permute-start | bytes 491528 | tf_op jit(solution)/shard_map/ppermute | solution.py:794
  487.4 36.2 %collective-permute-start.62 = (bf16[32,2560]{1,0:T(8,128)(2,1)S(1)}, bf16[32,2560]{1,0:T(8,128)(2,1)S(1)}, u32[]{:S(2)}, u32[]{:S(2)}) collective-permute-start(bf16[32,2560]{1,0:T(8,128)(2,1)S(1)} %get-tuple-element.144), channel_id=1, source_target_pairs={{0,16},{4,20},{8,24},{12,28},{16,0},{20,4},{24,8},{28,12},{1,17},{... | collective-permute-start | bytes 491528 | tf_op jit(solution)/shard_map/ppermute | solution.py:794
  (105 other events, 1600.8 us)

commit v2 on v1

v2 whole, which is shorter than its diff:
```python
import functools

import jax
import jax.numpy as jnp
from jax import lax
from jax.experimental import pallas as pl
from jax.experimental.pallas import tpu as pltpu
from jax.sharding import PartitionSpec as P

HD = 64
TSTEPS = 5000
EPSILON = 1e-05
NEGATIVE = -1e30
ROOT_HALF = 0.7071067811865476
DENSITY_SCALE = 0.3989422804014327
PAD = 128
WIDE = 512
BF16 = jnp.bfloat16
F32 = jnp.float32
VMEM = pltpu.VMEM
SMEM = pltpu.SMEM


def nn(a, b):
    return lax.dot_general(a, b, (((1,), (0,)), ((), ())), preferred_element_type=F32)


def nt(a, b):
    return lax.dot_general(a, b, (((1,), (1,)), ((), ())), preferred_element_type=F32)


def flipped_bits(value, count):
    return sum(((value >> i) & 1) << (count - 1 - i) for i in range(count))


def tn(a, b):
    return lax.dot_general(a, b, (((0,), (0,)), ((), ())), preferred_element_type=F32)


def shift_of(ns, core, slot):
    other = flipped_bits(slot, ns.bit_length() - 1)
    return slot + core * (other - slot)


def vspec():
    return pl.BlockSpec(memory_space=VMEM)


def sspec():
    return pl.BlockSpec(memory_space=SMEM)


def aspec():
    return pl.BlockSpec(memory_space=pl.ANY)


def params(mib, grid=0):
    if grid:
        return pltpu.CompilerParams(
            vmem_limit_bytes=mib << 20, dimension_semantics=("arbitrary",) * grid
        )
    return pltpu.CompilerParams(vmem_limit_bytes=mib << 20)


def cost(flops, nbytes, trans=0):
    return pl.CostEstimate(flops=int(flops), bytes_accessed=int(nbytes), transcendentals=int(trans))


def tau_rows(len_ref, tim_ref, seq, first, rows):
    spot = first + lax.broadcasted_iota(jnp.int32, (rows, 128), 0)
    begin = jnp.int32(0)
    step = jnp.zeros((rows, 128), jnp.int32)
    for i in range(len_ref.shape[1]):
        end = begin + len_ref[seq, i]
        step = jnp.where((spot >= begin) & (spot < end), tim_ref[seq, i], step)
        begin = end
    return (step.astype(F32) / TSTEPS)[:, :1]


def segments(len_ref, seq, spot):
    end = jnp.int32(0)
    found = jnp.zeros(spot.shape, jnp.int32)
    for i in range(len_ref.shape[1]):
        end = end + len_ref[seq, i]
        found = found + (spot >= end).astype(jnp.int32)
    return found


def item_bias(len_ref, seq, first, keys, rows, out_ref):
    mine = segments(len_ref, seq, first + lax.broadcasted_iota(jnp.int32, (8, rows), 1))
    theirs = segments(len_ref, seq, lax.broadcasted_iota(jnp.int32, (keys, 128), 0))
    for lane in range(rows // 128):
        same = theirs == mine[:1, lane * 128 : (lane + 1) * 128]
        out_ref[:, lane * 128 : (lane + 1) * 128] = jnp.where(same, 0.0, NEGATIVE)


def fold(block):
    rows, width = block.shape
    return block.reshape(rows // 8, 8, width)


def pack_kernel(ns, count, idx, *refs):
    srcs, (out_ref, outer_ref), dsts, sem = refs[:count], refs[count : count + 2], refs[count + 2 : -1], refs[-1]
    r, model = srcs[0].shape
    ff = srcs[-1].shape[1]
    hg = model // ns
    targets = list(dsts) + [outer_ref.at[:, 0:model], outer_ref.at[:, model : model + ff]]
    copies = [pltpu.make_async_copy(a, b, sem.at[n]) for n, (a, b) in enumerate(zip(srcs, targets))]
    for copy in copies:
        copy.start()
    for copy in copies:
        copy.wait()
    c, j = idx[1], idx[2]
    rows = [v[...].astype(F32).reshape(1, r) for v in dsts[3:-1]]
    rows.append(jnp.zeros((PAD - len(rows), r), F32))
    small = jnp.concatenate(rows, axis=0).T.astype(BF16)
    for m in range(ns):
        at = pl.ds(pl.multiple_of((j ^ shift_of(ns, c, m)) * hg, 128), hg)
        for n in range(3):
            out_ref[m, :, n * hg : (n + 1) * hg] = dsts[n][:, at]
        out_ref[m, :, 3 * hg :] = small
    row = dsts[-1][...].astype(F32).reshape(1, 4 * r)
    if PAD > 4 * r:
        row = jnp.concatenate([row, jnp.zeros((1, PAD - 4 * r), F32)], axis=1)
    outer_ref[:, model + ff :] = jnp.broadcast_to(row, (r, PAD)).astype(BF16)


def pack(ns, idx, w_query, w_key, w_value, vectors, b_up, w_out, w_up):
    r, model = w_query.shape
    args = (w_query, w_key, w_value, *vectors, b_up, w_out, w_up)
    return pl.pallas_call(
        functools.partial(pack_kernel, ns, len(args)),
        name="pack",
        out_shape=[
            jax.ShapeDtypeStruct((ns, r, 3 * (model // ns) + PAD), BF16),
            jax.ShapeDtypeStruct((r, model + w_up.shape[1] + PAD), BF16),
        ],
        in_specs=[sspec()] + [aspec()] * len(args),
        out_specs=[vspec()] * 2,
        scratch_shapes=[VMEM(a.shape, a.dtype) for a in args[:-2]]
        + [pltpu.SemaphoreType.DMA((len(args),))],
        compiler_params=params(60),
    )(idx, *args)


def qkv_kernel(ns, nz, r, len_ref, tim_ref, idx, *refs):
    toks = refs[:2]
    qa, qb = refs[2:4]
    q_ref, k_ref, v_ref, low_ref, w_ref, small_ref, wide = refs[4:]
    z, c, j = idx[0], idx[1], idx[2]
    half, seqs, rows, model = toks[0].shape
    hg = q_ref.shape[2]
    for cc, src in enumerate((qa, qb)):
        for a in range(nz):
            for b in range(ns):
                d = ((z ^ a) * 2 + (c ^ cc)) * ns + (j ^ shift_of(ns, c ^ cc, b))
                wide[pl.ds(pl.multiple_of(d * r, r), r), :] = src[a, b].astype(wide.dtype)
    w_ref[...] = wide[:, : 3 * hg].astype(BF16)
    small_ref[...] = wide[:, 3 * hg :].astype(F32).T[:16, :]
    heads = pl.ds(pl.multiple_of(j * hg, 128), hg)
    bq = small_ref[0:1, heads]
    bv = small_ref[1:2, heads]
    wt = small_ref[8:9, :]
    bt = small_ref[9:10, :]
    for k in range(ns):
        first = pl.multiple_of((j ^ shift_of(ns, c, k)) * rows, rows)
        here = pl.ds(first, rows)
        for s in range(seqs):
            tau = tau_rows(len_ref, tim_ref, s, first, rows)
            low = (toks[k // half][k % half, s].astype(F32) + tau * wt + bt).astype(BF16)
            low_ref[s, here, :] = low
            got = nn(low, w_ref[...])
            q_ref[s, here, :] = ((got[:, :hg] + bq) * (HD**-0.5)).astype(BF16)
            k_ref[s, here, :] = got[:, hg : 2 * hg].astype(BF16)
            v_ref[s, here, :] = (got[:, 2 * hg :] + bv).astype(BF16)


def project(ns, nz, lengths, timesteps, idx, toks, qa, qb):
    seqs, rows, model = toks[0].shape[1:]
    r = qa.shape[2]
    hg = (qa.shape[3] - PAD) // 3
    full = rows * ns
    heads = jax.ShapeDtypeStruct((seqs, full, hg), BF16)
    outs = [
        heads,
        heads,
        heads,
        jax.ShapeDtypeStruct((seqs, full, model), BF16),
        jax.ShapeDtypeStruct((model, 3 * hg), BF16),
        jax.ShapeDtypeStruct((16, model), F32),
    ]
    return pl.pallas_call(
        functools.partial(qkv_kernel, ns, nz, r),
        name="project",
        out_shape=outs,
        in_specs=[sspec()] * 3 + [vspec()] * 4,
        out_specs=[vspec()] * 6,
        scratch_shapes=[VMEM((model, 3 * hg + PAD), BF16 if r % 16 == 0 else F32)],
        compiler_params=params(58),
        cost_estimate=cost(2 * seqs * full * model * 3 * hg, 14 << 20),
    )(lengths, timesteps, idx, *toks, qa, qb)


PAIR = 128
QUERIES = 512


def slots_of(full):
    return 2 if full <= 1024 else 1


def item_bias_all(len_ref, seq, bias):
    keys = bias.shape[0]
    for b in range(keys // QUERIES):
        item_bias(len_ref, seq, b * QUERIES, keys, QUERIES, bias.at[:, b * QUERIES : (b + 1) * QUERIES])


def attend_kernel(ns, s, len_ref, idx, q_ref, k_ref, v_ref, *refs):
    ctx_refs = refs[:ns]
    ctxf_ref, lse_ref, bias, probs, scale = refs[ns:]
    j = idx[2]
    full = k_ref.shape[1]
    rows = full // ns

    alone = whole_sequence(len_ref, s, full)

    @pl.when((pl.program_id(0) == 0) & jnp.logical_not(alone))
    def _():
        item_bias_all(len_ref, s, bias)

    scale[...] = jnp.zeros_like(scale)
    lse_ref[...] = jnp.zeros_like(lse_ref)

    def heads(add):
        attend_heads(full, add, q_ref, k_ref, v_ref, ctxf_ref, lse_ref, probs, scale)

    pl.when(alone)(lambda: heads(lambda st, at: st))
    pl.when(jnp.logical_not(alone))(lambda: heads(lambda st, at: st + bias[:, at]))
    for k in range(ns):
        here = pl.ds(pl.multiple_of((j ^ k) * rows, rows), rows)
        ctx_refs[k][...] = ctxf_ref[0, here, :].astype(BF16)


def whole_sequence(len_ref, seq, full):
    end = jnp.int32(0)
    same = jnp.bool_(True)
    for i in range(len_ref.shape[1]):
        end = end + len_ref[seq, i]
        same = same & ((end <= 0) | (end >= full))
    return same


def attend_heads(full, add, q_ref, k_ref, v_ref, ctxf_ref, lse_ref, probs, scale):
    for h in range(PAIR // HD):
        cols = slice(h * HD, (h + 1) * HD)
        kh, vh = k_ref[0, :, cols], v_ref[0, :, cols]
        for b in range(full // QUERIES):
            at = slice(b * QUERIES, (b + 1) * QUERIES)
            st = add(nt(kh, q_ref[0, at, cols]), at)
            top = jnp.max(jnp.max(fold(st), axis=0), axis=0, keepdims=True)
            p = jnp.exp(st - top)
            total = jnp.sum(jnp.sum(fold(p), axis=0), axis=0, keepdims=True)
            probs[h % probs.shape[0], :, at] = p.astype(BF16)
            scale[h : h + 1, at] = 1.0 / total
            lse_ref[0, h : h + 1, at] = top + jnp.log(total)
        by_row = scale[...].T
        ctxf_ref[0, :, cols] = tn(probs[h % probs.shape[0]], vh) * by_row[:, h : h + 1]


def attend(ns, seq, lengths, idx, q, k, v):
    seqs, full, hg = q.shape
    rows = full // ns
    groups = hg // PAIR
    outs = [jax.ShapeDtypeStruct((rows, hg), BF16)] * ns + [
        jax.ShapeDtypeStruct((1, full, hg), F32),
        jax.ShapeDtypeStruct((1, 8 * groups, full), F32),
    ]
    wide = pl.BlockSpec((1, full, PAIR), lambda i: (seq, 0, i))
    res = pl.pallas_call(
        functools.partial(attend_kernel, ns, seq),
        name="attend",
        out_shape=outs,
        grid=(groups,),
        in_specs=[sspec(), sspec(), wide, wide, wide],
        out_specs=[pl.BlockSpec((rows, PAIR), lambda i: (0, i))] * ns
        + [
            pl.BlockSpec((1, full, PAIR), lambda i: (0, 0, i)),
            pl.BlockSpec((1, 8, full), lambda i: (0, i, 0)),
        ],
        scratch_shapes=[
            VMEM((full, full), F32),
            VMEM((slots_of(full), full, full), BF16),
            VMEM((8, full), F32),
        ],
        compiler_params=params(58, 1),
        cost_estimate=cost(4 * 4 * full * full * hg, 4 << 20),
    )(lengths, idx, q, k, v)
    return res[:ns], res[ns], res[ns + 1]


def attend_back_kernel(ns, seq, len_ref, tim_ref, idx, q_ref, k_ref, v_ref, ctxf_ref, lse_ref, w_ref, *refs):
    dctx = refs[:ns]
    grad_ref, pk_ref, ps_ref, sum_ref, bsum_ref, bias, dcx, probs, score = refs[ns:]
    i = pl.program_id(0)
    c, j = idx[1], idx[2]
    full = k_ref.shape[1]
    rows = full // ns
    hg = grad_ref.shape[1] // 3

    alone = whole_sequence(len_ref, seq, full)

    @pl.when((i == 0) & jnp.logical_not(alone))
    def _():
        item_bias_all(len_ref, seq, bias)

    for k in range(ns):
        dcx[pl.ds(pl.multiple_of((j ^ k) * rows, rows), rows), :] = dctx[k][0]

    def heads(add):
        back_heads(full, add, i, q_ref, k_ref, v_ref, ctxf_ref, lse_ref, grad_ref, dcx, probs, score)

    pl.when(alone)(lambda: heads(lambda st, at: st))
    pl.when(jnp.logical_not(alone))(lambda: heads(lambda st, at: st + bias[:, at]))
    @pl.when(i == pl.num_programs(0) - 1)
    def _():
        plain = jnp.zeros((8, w_ref.shape[0]), F32)
        timed = jnp.zeros((8, w_ref.shape[0]), F32)
        bias_sum = jnp.zeros((8, 3 * hg), F32)
        for k in range(ns):
            first = pl.multiple_of((j ^ shift_of(ns, c, k)) * rows, rows)
            block = grad_ref[pl.ds(first, rows), :]
            part = nt(block, w_ref[...])
            (pk_ref if k < ns // 2 else ps_ref)[k % (ns // 2)] = part.astype(BF16)
            plain = plain + jnp.sum(fold(part), axis=0)
            tau = tau_rows(len_ref, tim_ref, seq, first, rows)
            timed = timed + jnp.sum(fold(part * tau), axis=0)
            bias_sum = bias_sum + jnp.sum(fold(block.astype(F32)), axis=0)
        sum_ref[...] = jnp.zeros_like(sum_ref)
        sum_ref[0:1, :] = jnp.sum(timed, axis=0, keepdims=True)
        sum_ref[1:2, :] = jnp.sum(plain, axis=0, keepdims=True)
        bsum_ref[...] = jnp.broadcast_to(jnp.sum(bias_sum, axis=0, keepdims=True), bsum_ref.shape)


def back_heads(full, add, i, q_ref, k_ref, v_ref, ctxf_ref, lse_ref, grad_ref, dcx, probs, score):
    grads = []
    for h in range(PAIR // HD):
        cols = slice(h * HD, (h + 1) * HD)
        qh, kh, vh = q_ref[0, :, cols], k_ref[0, :, cols], v_ref[0, :, cols]
        dch = dcx[:, cols]
        row_total = jnp.sum((ctxf_ref[0, :, cols] * dch.astype(F32)).T, axis=0, keepdims=True)
        for b in range(full // QUERIES):
            at = slice(b * QUERIES, (b + 1) * QUERIES)
            p = jnp.exp(add(nt(kh, qh[at, :]), at) - lse_ref[0, h : h + 1, at])
            ds = p * (nt(vh, dch[at, :]) - row_total[:, at])
            probs[h % probs.shape[0], :, at] = p.astype(BF16)
            score[h % score.shape[0], :, at] = ds.astype(BF16)
        dq = tn(score[h % score.shape[0]], kh).astype(BF16).astype(F32) * (HD**-0.5)
        grads.append((dq, nn(score[h % score.shape[0]], qh), nn(probs[h % probs.shape[0]], dch)))
    hg = grad_ref.shape[1] // 3
    for n in range(3):
        at = pl.ds(pl.multiple_of(n * hg + i * PAIR, PAIR), PAIR)
        grad_ref[:, at] = jnp.concatenate([g[n] for g in grads], axis=1).astype(BF16)


def attend_back(ns, seq, lengths, timesteps, idx, q, k, v, ctxf, lse, w, dctx):
    seqs, full, hg = q.shape
    rows = full // ns
    groups = hg // PAIR
    model = w.shape[0]
    one = lambda shape: pl.BlockSpec(shape, lambda i: (0,) * len(shape))
    wide = pl.BlockSpec((1, full, PAIR), lambda i: (seq, 0, i))
    outs = (
        [jax.ShapeDtypeStruct((full, 3 * hg), BF16)]
        + [jax.ShapeDtypeStruct((ns // 2, rows, model), BF16)] * 2
        + [jax.ShapeDtypeStruct((8, model), F32), jax.ShapeDtypeStruct((8, 3 * hg), F32)]
    )
    return pl.pallas_call(
        functools.partial(attend_back_kernel, ns, seq),
        name="attend_back",
        out_shape=outs,
        grid=(groups,),
        in_specs=[sspec()] * 3
        + [
            wide,
            wide,
            wide,
            pl.BlockSpec((1, full, PAIR), lambda i: (0, 0, i)),
            pl.BlockSpec((1, 8, full), lambda i: (0, i, 0)),
            one((model, 3 * hg)),
        ]
        + [pl.BlockSpec((1, rows, PAIR), lambda i: (seq, 0, i))] * ns,
        out_specs=[one((full, 3 * hg))]
        + [one((ns // 2, rows, model))] * 2
        + [one((8, model)), one((8, 3 * hg))],
        scratch_shapes=[
            VMEM((full, full), F32),
            VMEM((full, PAIR), BF16),
            VMEM((slots_of(full), full, full), BF16),
            VMEM((slots_of(full), full, full), BF16),
        ],
        compiler_params=params(58, 1),
        cost_estimate=cost(10 * 4 * full * full * hg, 10 << 20),
    )(lengths, timesteps, idx, q, k, v, ctxf, lse, w, *dctx)


def middle_kernel(ns, nz, r, len_ref, tim_ref, idx, tok_ref, cot_ref, small_ref, *refs):
    ctxs = refs[: 2 * ns]
    refs = refs[2 * ns :]
    outer, dn, rest = refs[:4], refs[4 : 4 + 2 * nz], refs[4 + 2 * nz :]
    out_ref, keep_o, send_o, ug_o, fl_o, cx_o, ag_o, r1_o = rest[:8]
    dctx = rest[8 : 8 + ns]
    sum_ref, gbup_ref = rest[8 + ns : 10 + ns]
    wu, wd, act, slope, ug, fl, cx, dg, first, norm, inv, stage, bup_ref, slots, wsem, osem, gsem = rest[10 + ns :]
    z, c, j = idx[0], idx[1], idx[2]
    seqs, rows, model = tok_ref.shape
    ff = wd.shape[0]
    hg = ctxs[0].shape[1]
    tokens = seqs * rows
    ends = (0, model, wu.shape[1])
    for part in range(2):
        at = slice(ends[part], ends[part + 1])
        for n, src in enumerate(outer):
            core = c ^ (n // 2)
            for m in range(ns // 2):
                shift = shift_of(ns, core, m + (n % 2) * (ns // 2))
                for a in range(nz):
                    d = ((z ^ a) * 2 + core) * ns + (j ^ shift)
                    pltpu.make_async_copy(
                        src.at[m, a, :, at],
                        wu.at[pl.ds(pl.multiple_of(d * r, r), r), at],
                        wsem.at[part],
                    ).start()
    for n, src in enumerate(dn):
        core = c ^ (n % 2)
        for m in range(ns):
            d = (lax.rem(z + nz - n // 2, nz) * 2 + core) * ns + (j ^ shift_of(ns, core, m))
            pltpu.make_async_copy(
                src.at[m],
                wd.at[pl.ds(pl.multiple_of(d * 4 * r, 4 * r), 4 * r), :],
                wsem.at[2],
            ).start()
    for k in range(ns):
        at = pl.ds(pl.multiple_of((j ^ k) * hg, 128), hg)
        for s in range(seqs):
            cx[s * rows : (s + 1) * rows, at] = ctxs[s * ns + k][...]
    sum_ref[...] = jnp.zeros_like(sum_ref)
    pltpu.make_async_copy(cx, cx_o, osem.at[0]).start()
    u1_all = wu.at[:, 0 : ends[1]]
    pltpu.make_async_copy(u1_all, u1_all, wsem.at[0]).wait()

    b_out = small_ref[2:3, :]
    gain_one, shift_one = small_ref[3:4, :], small_ref[4:5, :]
    b_down = small_ref[5:6, :]
    gain_two, shift_two = small_ref[6:7, :], small_ref[7:8, :]
    w_time, b_time = small_ref[8:9, :], small_ref[9:10, :]
    block = rows
    per = 1

    def add_sum(row, value):
        sum_ref[row : row + 1, :] += jnp.sum(jnp.sum(fold(value), axis=0), axis=0, keepdims=True)

    def mean(value):
        return jnp.sum(value, axis=-1, keepdims=True) * (1.0 / model)

    def one_first(s, b):
        at = pl.ds(pl.multiple_of((s * per + b) * block, block), block)
        inside = pl.ds(pl.multiple_of(b * block, block), block)
        attn = nn(cx[at, :], wu[:, 0:model])
        tau = tau_rows(len_ref, tim_ref, s, j * rows + b * block, block)
        start = tok_ref[s, inside, :].astype(F32) + tau * w_time + b_time
        res = start + (attn + b_out)
        center = res - mean(res)
        inverse = lax.rsqrt(mean(center * center) + EPSILON)
        normed = center * inverse
        norm[at, :] = normed
        inv[at, :] = jnp.broadcast_to(inverse, (block, 128))
        value = normed * gain_one + shift_one
        first[at, :] = value
        fl[at, :] = value.astype(BF16)

    for s in range(seqs):
        one_first(s, 0)
    pltpu.make_async_copy(fl, fl_o, osem.at[1]).start()
    u2_all = wu.at[:, ends[1] : ends[2]]
    pltpu.make_async_copy(u2_all, u2_all, wsem.at[1]).wait()
    for d in range(ns * nz * 2):
        bup_ref[0:1, d * 4 * r : (d + 1) * 4 * r] = wu[d * r : d * r + 1, model + ff : model + ff + 4 * r].astype(F32)

    def one_up(n, _):
        at = pl.ds(pl.multiple_of(n * WIDE, WIDE), WIDE)
        wat = pl.ds(pl.multiple_of(model + n * WIDE, WIDE), WIDE)
        for h in range(2):
            rr = slice(h * tokens // 2, (h + 1) * tokens // 2)
            pre = nn(fl[rr, :], wu[:, wat]) + bup_ref[0:1, at]
            cumulative = 0.5 * (1.0 + lax.erf(pre * ROOT_HALF))
            density = jnp.exp(-0.5 * pre * pre) * DENSITY_SCALE
            act[rr, at] = (pre * cumulative).astype(BF16)
            slope[rr, at] = cumulative + pre * density
        return 0

    lax.fori_loop(0, ff // WIDE, one_up, 0)
    pltpu.make_async_copy(wd, wd, wsem.at[2]).wait()

    def one_second(s, b):
        at = pl.ds(pl.multiple_of((s * per + b) * block, block), block)
        inside = pl.ds(pl.multiple_of(b * block, block), block)
        res = first[at, :] + (nn(act[at, :], wd[...]) + b_down)
        center = res - mean(res)
        inverse = lax.rsqrt(mean(center * center) + EPSILON)
        normed = center * inverse
        out_ref[s, inside, :] = (normed * gain_two + shift_two).astype(BF16)
        g = cot_ref[s, inside, :].astype(F32)
        add_sum(4, g * normed)
        add_sum(5, g)
        gn = g * gain_two
        grad = inverse * (gn - mean(gn) - normed * mean(gn * normed))
        first[at, :] = grad
        low = grad.astype(BF16)
        dg[at, :] = low
        add_sum(3, low.astype(F32))

    for s in range(seqs):
        one_second(s, 0)

    wide = ns * 4 * r

    def grad_copy(n, dst):
        return pltpu.make_async_copy(slots.at[n % 2], dst.at[n % nz], gsem.at[n % 2])

    for n in range(2 * nz):
        core = c ^ 1 if n < nz else c
        dst = send_o if n < nz else keep_o
        own = pl.multiple_of((lax.rem(z + n % nz, nz) * 2 + core) * wide, wide)
        total = tn(act[:, pl.ds(own, wide)], dg[...])
        if n >= 2:
            grad_copy(n - 2, send_o if n - 2 < nz else keep_o).wait()
        for b in range(ns):
            slots[n % 2, place_of(ns, core, j ^ b)] = total[b * 4 * r : (b + 1) * 4 * r].astype(BF16)
        grad_copy(n, dst).start()

    def one_up_grad(n, _):
        at = pl.ds(pl.multiple_of(n * WIDE, WIDE), WIDE)
        total = jnp.zeros((8, WIDE), F32)
        for h in range(2):
            rr = slice(h * tokens // 2, (h + 1) * tokens // 2)
            low = (nt(dg[rr, :], wd[at, :]) * slope[rr, at]).astype(BF16)
            ug[rr, at] = low
            total = total + jnp.sum(fold(low.astype(F32)), axis=0)
        row = jnp.sum(total, axis=0, keepdims=True)
        for m in range(WIDE // (4 * r)):
            gbup_ref[pl.ds(n * (WIDE // (4 * r)) + m, 1), :] = row[:, m * 4 * r : (m + 1) * 4 * r]
        return 0

    lax.fori_loop(0, ff // WIDE, one_up_grad, 0)
    pltpu.make_async_copy(ug, ug_o, osem.at[4]).start()
    pltpu.make_async_copy(fl, fl_o, osem.at[1]).wait()

    def one_first_grad(s, b):
        at = pl.ds(pl.multiple_of((s * per + b) * block, block), block)
        inside = pl.ds(pl.multiple_of(b * block, block), block)
        fg = nt(ug[at, :], wu[:, model : model + ff]) + first[at, :]
        normed = norm[at, :]
        add_sum(1, fg * normed)
        add_sum(2, fg)
        gn = fg * gain_one
        grad = inv[at, :][:, :1] * (gn - mean(gn) - normed * mean(gn * normed))
        first[at, :] = grad
        low = grad.astype(BF16)
        fl[at, :] = low
        add_sum(0, low.astype(F32))
        tau = tau_rows(len_ref, tim_ref, s, j * rows + b * block, block)
        add_sum(6, grad * tau)
        add_sum(7, grad)
        stage[...] = nt(low, wu[:, 0:model]).astype(BF16)
        for k in range(ns):
            cols = pl.ds(pl.multiple_of((j ^ k) * hg, 128), hg)
            dctx[k][s, inside, :] = stage[:, cols]

    for s in range(seqs):
        one_first_grad(s, 0)
    ag_copy = pltpu.make_async_copy(fl, ag_o, osem.at[5])
    ag_copy.start()
    r1_copy = pltpu.make_async_copy(first, r1_o, osem.at[6])
    r1_copy.start()
    pltpu.make_async_copy(cx, cx_o, osem.at[0]).wait()
    for n in (2 * nz - 2, 2 * nz - 1):
        grad_copy(n, keep_o).wait()
    pltpu.make_async_copy(ug, ug_o, osem.at[4]).wait()
    ag_copy.wait()
    r1_copy.wait()


def middle(ns, nz, r, lengths, timesteps, idx, tokens, cotangent, small, ctxs, outer, dn):
    seqs, rows, model = tokens.shape
    total = seqs * rows
    ff = dn[0].shape[1] * ns * nz * 2
    hg = ctxs[0].shape[1]
    sh = lambda *a: jax.ShapeDtypeStruct(a[:-1], a[-1])
    outs = [
        sh(seqs, rows, model, BF16),
        sh(nz, ns, 4 * r, model, BF16),
        sh(nz, ns, 4 * r, model, BF16),
        sh(total, ff, BF16),
        sh(total, model, BF16),
        sh(total, model, BF16),
        sh(total, model, BF16),
        sh(total, model, F32),
    ]
    outs += [sh(seqs, rows, hg, BF16)] * ns + [sh(16, model, F32), sh(ff // (4 * r), 4 * r, F32)]
    res = pl.pallas_call(
        functools.partial(middle_kernel, ns, nz, r),
        name="middle",
        out_shape=outs,
        in_specs=[sspec()] * 3
        + [vspec()] * (3 + 2 * ns)
        + [aspec()] * (len(outer) + len(dn)),
        out_specs=[vspec()] + [aspec()] * 7 + [vspec()] * (ns + 2),
        scratch_shapes=[
            VMEM((model, model + ff + PAD), BF16),
            VMEM((ff, model), BF16),
            VMEM((total, ff), BF16),
            VMEM((total, ff), F32),
            VMEM((total, ff), BF16),
            VMEM((total, model), BF16),
            VMEM((total, model), BF16),
            VMEM((total, model), BF16),
            VMEM((total, model), F32),
            VMEM((total, model), F32),
            VMEM((total, 128), F32),
            VMEM((rows, model), BF16),
            VMEM((8, ff), F32),
            VMEM((2, ns, 4 * r, model), BF16),
            pltpu.SemaphoreType.DMA((3,)),
            pltpu.SemaphoreType.DMA((7,)),
            pltpu.SemaphoreType.DMA((2,)),
        ],
        compiler_params=params(60),
        cost_estimate=cost(
            2 * total * (2 * model * model + 4 * model * ff), 40 << 20, 3 * total * ff
        ),
    )(lengths, timesteps, idx, tokens, cotangent, small, *ctxs, *outer, *dn)
    return res[:8], res[8 : 8 + ns], res[8 + ns], res[9 + ns]


def place_of(ns, core, offset):
    return offset + core * (flipped_bits(offset, ns.bit_length() - 1) - offset)


def gather_columns(ns, nz, r, core, idx, src, dst, first):
    wide = ns * r
    for a in range(nz):
        pair = pl.multiple_of((idx[0] ^ a) * 2 * wide, 2 * wide)
        if wide % 128 == 0:
            got = src[:, pl.ds(pl.multiple_of(pair + core * wide, wide), wide)]
        else:
            both = src[:, pl.ds(pair, 2 * wide)]
            got = jnp.where(core == 0, both[:, :wide], both[:, wide:])
        dst[:, first + a * wide : first + (a + 1) * wide] = got


def store_slots(ns, nz, r, core, walk, idx, total, dst, at=slice(None)):
    for a in range(nz):
        for b in range(ns):
            slot = place_of(ns, core if walk else 0, idx[2] ^ b)
            n = (a * ns + b) * r
            dst[a, slot, :, at] = total[n : n + r].astype(BF16)


def up_grad_kernel(ns, nz, r, idx, cx_ref, ag_ref, fl_ref, ug_ref, gbup_ref, keep_ref, send_ref, left):
    i = pl.program_id(0)
    split = ag_ref.shape[1] // WIDE
    last = pl.num_programs(0) - 1
    half = cx_ref.shape[1] // 2
    c = idx[1]

    def both(right):
        total = tn(left[...], right)
        store_slots(ns, nz, r, c, True, idx, total[:half], keep_ref)
        store_slots(ns, nz, r, c ^ 1, True, idx, total[half:], send_ref)

    @pl.when(i == 0)
    def _():
        gather_columns(ns, nz, r, c, idx, cx_ref, left, 0)
        gather_columns(ns, nz, r, c ^ 1, idx, cx_ref, left, half)

    @pl.when(i < split)
    def _():
        both(ag_ref[:, pl.ds(pl.multiple_of(jnp.minimum(i, split - 1) * WIDE, WIDE), WIDE)])

    @pl.when(i == split)
    def _():
        gather_columns(ns, nz, r, c, idx, fl_ref, left, 0)
        gather_columns(ns, nz, r, c ^ 1, idx, fl_ref, left, half)

    @pl.when((i >= split) & (i < last))
    def _():
        both(ug_ref[...])

    @pl.when(i == last)
    def _():
        keep_ref[...] = jnp.zeros_like(keep_ref)
        send_ref[...] = jnp.zeros_like(send_ref)
        for cc, dst in enumerate((keep_ref, send_ref)):
            core = c ^ cc
            for a in range(nz):
                for b in range(ns):
                    d = ((idx[0] ^ a) * 2 + core) * ns + (idx[2] ^ shift_of(ns, core, b))
                    row = gbup_ref[pl.ds(d, 1), :]
                    dst[a, b, :, 0 : 4 * r] = jnp.broadcast_to(row, (r, 4 * r)).astype(BF16)


def up_grad(ns, nz, r, idx, cx, ag, fl, ug, gbup):
    total, model = fl.shape
    ff = ug.shape[1]
    width = model + ff + PAD
    split, top = model // WIDE, ff // WIDE - 1
    one = lambda shape: pl.BlockSpec(shape, lambda i: (0,) * len(shape))
    block = pl.BlockSpec((nz, ns, r, WIDE), lambda i: (0, 0, 0, i))
    return pl.pallas_call(
        functools.partial(up_grad_kernel, ns, nz, r),
        name="up_grad",
        out_shape=[jax.ShapeDtypeStruct((nz, ns, r, width), BF16)] * 2,
        grid=(pl.cdiv(width, WIDE),),
        in_specs=[
            sspec(),
            one(cx.shape),
            one(ag.shape),
            one(fl.shape),
            pl.BlockSpec((total, WIDE), lambda i: (0, jnp.minimum(jnp.maximum(i - split, 0), top))),
            one(gbup.shape),
        ],
        out_specs=[block, block],
        scratch_shapes=[VMEM((total, model), BF16)],
        compiler_params=params(58, 1),
        cost_estimate=cost(2 * total * model * width, 10 << 20),
    )(idx, cx, ag, fl, ug, gbup)


def qkv_grad_kernel(ns, nz, r, idx, low_ref, g0_ref, g1_ref, sums_ref, s0_ref, s1_ref, b0_ref, b1_ref, keep_ref, send_ref, left, vec, tall):
    c, j = idx[1], idx[2]
    hg = g0_ref.shape[1] // 3
    vec[...] = jnp.zeros_like(vec)
    heads = pl.ds(pl.multiple_of(j * hg, 128), hg)
    both = b0_ref[0:1, :] + b1_ref[0:1, :]
    vec[0:1, heads] = both[:, :hg]
    vec[1:2, heads] = both[:, 2 * hg :]
    vec[2:8, :] = sums_ref[0:6, :]
    vec[8:10, :] = sums_ref[6:8, :] + s0_ref[0:2, :] + s1_ref[0:2, :]
    tall[...] = vec[...].T
    half = left.shape[1] // 2
    for cc, dst in enumerate((keep_ref, send_ref)):
        core = c ^ cc
        total = 0.0
        for s, g in enumerate((g0_ref, g1_ref)):
            gather_columns(ns, nz, r, core, idx, low_ref.at[s], left, cc * half)
            total = total + tn(left[:, cc * half : (cc + 1) * half], g[...])
        store_slots(ns, nz, r, 0, False, idx, total, dst, slice(0, 3 * hg))
        for a in range(nz):
            for b in range(ns):
                d = ((idx[0] ^ a) * 2 + core) * ns + (j ^ b)
                dst[a, b, :, 3 * hg :] = tall[pl.ds(pl.multiple_of(d * r, r), r), :].astype(BF16)


def qkv_grad(ns, nz, r, idx, low, g0, g1, sums, s0, s1, b0, b1):
    seqs, full, model = low.shape
    width = g0.shape[1] + PAD
    out = jax.ShapeDtypeStruct((nz, ns, r, width), BF16)
    return pl.pallas_call(
        functools.partial(qkv_grad_kernel, ns, nz, r),
        name="qkv_grad",
        out_shape=[out, out],
        in_specs=[sspec()] + [vspec()] * 8,
        out_specs=[vspec()] * 2,
        scratch_shapes=[
            VMEM((full, model), BF16),
            VMEM((PAD, model), F32),
            VMEM((model, PAD), F32),
        ],
        compiler_params=params(58),
        cost_estimate=cost(2 * seqs * full * model * width, 12 << 20),
    )(idx, low, g0, g1, sums, s0, s1, b0, b1)


def finish_kernel(ns, r, idx, own_ref, *refs):
    others = refs[: ns - 1]
    q_ref, k_ref, v_ref, small_ref = refs[ns - 1 :]
    j = idx[2]
    hg = (own_ref.shape[1] - PAD) // 3
    small = own_ref[:, 3 * hg :]
    for k in range(ns):
        part = own_ref[...] if k == 0 else others[k - 1][...].astype(F32)
        cols = pl.ds(pl.multiple_of((j ^ k) * hg, 128), hg)
        for n, dst in enumerate((q_ref, k_ref, v_ref)):
            dst[:, cols] = part[:, n * hg : (n + 1) * hg]
        if k:
            small = small + part[:, 3 * hg :]
    small_ref[...] = small.T[:16, :]


def finish(ns, r, model, idx, own, others):
    out = jax.ShapeDtypeStruct((r, model), F32)
    return pl.pallas_call(
        functools.partial(finish_kernel, ns, r),
        name="finish",
        out_shape=[out, out, out, jax.ShapeDtypeStruct((16, r), F32)],
        in_specs=[sspec()] + [vspec()] * ns,
        out_specs=[vspec()] * 4,
        compiler_params=params(16),
    )(idx, own, *others)


def to_seq(value, k):
    ns = lax.axis_size("seq")
    return lax.ppermute(value, "seq", [(i, i ^ k) for i in range(ns)])


def to_mate(value):
    nd = lax.axis_size("dp")
    return lax.ppermute(value, "dp", [(i, i ^ 1) for i in range(nd)])


def to_z(value, a):
    nd = lax.axis_size("dp")
    return lax.ppermute(value, "dp", [(i, i ^ (2 * a)) for i in range(nd)])


def to_ring(value):
    nd = lax.axis_size("dp")
    return lax.ppermute(value, "dp", [(i, (i + 2) % nd) for i in range(nd)])


def to_bit(value, place):
    ns, nd = lax.axis_size("seq"), lax.axis_size("dp")
    high = ns.bit_length() - 2
    pairs = []
    for dp in range(nd):
        bit = 1 << (high - place if dp % 2 else place)
        pairs += [(dp * ns + i, dp * ns + (i ^ bit)) for i in range(ns)]
    return lax.ppermute(value, ("dp", "seq"), pairs)


def gather_plane(block, ns):
    cur = block[None]
    high = ns.bit_length() - 2
    for place in range(high):
        cur = jnp.concatenate([cur, to_bit(cur, place)], axis=0)
    return [cur, to_bit(cur, high)]


def exchange_plane(blocks, ns):
    kept = [blocks[m] for m in range(ns)]
    early = None
    for place in range(ns.bit_length() - 1):
        bit = 1 << place
        away = [m for m in range(ns) if m & bit]
        got = to_bit(jnp.stack([kept[m] for m in away]), place)
        early = got if early is None else early
        for n, m in enumerate(away):
            kept[m] = got[n]
    return jnp.stack(kept), early


def added(terms):
    return functools.reduce(lambda a, b: a + b, [t.astype(F32) for t in terms])


def added_rows(lists):
    return jnp.stack([added(terms) for terms in lists]).astype(BF16)


def hold(*values):
    return lax.optimization_barrier(values)


def after(values, others):
    return lax.optimization_barrier((values, others))


class Scatter:
    def __init__(self, keep, send, ns, nz):
        self.ns, self.nz = ns, nz
        self.terms = [keep] + self.exchange(send)
        self.last = None

    def exchange(self, send):
        return [to_mate(send)]

    def high(self, half):
        return [t[: self.nz, half : self.ns] for t in self.terms]

    def bit(self):
        half = self.ns // 2
        self.last = added(self.high(half)).astype(BF16)
        self.terms = self.terms + [to_bit(self.last, self.ns.bit_length() - 2)]
        self.ns = half

    def finish(self, at=slice(None), row=slice(None)):
        while self.step():
            pass
        return added([t[0, 0, row, at] for t in self.terms])


class ScatterDirect(Scatter):
    ahead = None

    def exchange(self, send):
        half = self.ns // 2
        self.ahead = to_mate(send[:, half:])
        return [to_mate(send[:, :half])]

    def high(self, half):
        if self.ahead is None:
            return super().high(half)
        parts = [t[: self.nz, half : self.ns] for t in self.terms[:1]] + [self.ahead]
        self.ahead = None
        return parts

    def step(self):
        if self.ns > 1:
            self.bit()
        elif self.nz > 1:
            self.last = [added([t[a, 0] for t in self.terms]).astype(BF16) for a in range(1, self.nz)]
            self.terms = self.terms + [to_z(v, a + 1)[None, None] for a, v in enumerate(self.last)]
            self.nz = 1
        else:
            return False
        return True


class ScatterRing(Scatter):
    moving = None

    def fix(self):
        self.terms = self.terms + [self.moving[None]]

    def step(self):
        if self.nz > 1:
            self.nz -= 1
            parts = [t[self.nz] for t in self.terms] + ([] if self.moving is None else [self.moving])
            self.last = added(parts).astype(BF16)
            self.moving = to_ring(self.last)
        elif self.ns > 1:
            self.bit()
        else:
            return False
        return True


def body(
    tokens,
    lengths,
    timesteps,
    w_query,
    b_query,
    w_key,
    w_value,
    b_value,
    w_out,
    b_out,
    gain_one,
    shift_one,
    w_up,
    b_up,
    w_down,
    b_down,
    gain_two,
    shift_two,
    w_time,
    b_time,
    cotangent,
):
    seqs, rows, model = tokens.shape
    ns = lax.axis_size("seq")
    nz = lax.axis_size("dp") // 2
    r = w_query.shape[0]
    hg = model // ns
    dp = lax.axis_index("dp")
    j = lax.axis_index("seq")
    idx = jnp.stack([dp // 2, dp % 2, j]).astype(jnp.int32)

    high = ns.bit_length() - 1
    vectors = [b_query, b_value, b_out, gain_one, shift_one, b_down, gain_two, shift_two, w_time, b_time]
    mine, outer = pack(ns, idx, w_query, w_key, w_value, vectors, b_up, w_out, w_up)
    tok, down = tokens[None], w_down[None]
    kept = [mine[m] for m in range(ns)]
    outer_z, near_z = [], []
    waiting = list(range(1, nz))
    for place in range(high):
        got = [to_bit(tok, place), to_bit(down, place) if place < high - 1 else None]
        away = [m for m in range(ns) if m & (1 << place)]
        pieces = to_bit(jnp.stack([kept[m] for m in away]), place)
        now = waiting[:1] if place < high - 1 else waiting
        waiting = waiting[len(now) :]
        outer_z = outer_z + [to_z(outer, a) for a in now]
        tok, down, outer, kept, got, pieces, outer_z = hold(tok, down, outer, kept, got, pieces, outer_z)
        for n, m in enumerate(away):
            kept[m] = pieces[n]
        if place < high - 1:
            tok = jnp.concatenate([tok, got[0]], axis=0)
            down = jnp.concatenate([down, got[1]], axis=0)
    toks = [tok, got[0]]
    near = jnp.stack(kept)
    near_z = [to_z(near, a) for a in range(1, nz)]
    cur = jnp.stack([outer] + outer_z)[None]
    down_next, cur_next = to_bit(down, high - 1), to_bit(cur, 0)
    toks, near, near_z, down, down_next, cur, cur_next = hold(
        toks, near, near_z, down, down_next, cur, cur_next
    )
    qa = jnp.stack([near] + near_z)
    qb = to_mate(qa)
    down = jnp.concatenate([down, down_next], axis=0)
    downs = [down, to_ring(down)]
    for place in range(1, high):
        cur = jnp.concatenate([cur, cur_next], axis=0)
        cur_next = to_bit(cur, place)
    qa, _ = after(qa, (down, cur))

    projected = project(ns, nz, lengths, timesteps, idx, toks, qa, qb)
    q, k, v, low, w_qkv, small = projected
    fronts, ctxs = [], []
    for s in range(seqs):
        front = attend(ns, s, lengths, idx, q, k, v)
        front, downs = hold(front, downs)
        downs.append(to_ring(downs[-1]))
        if s == seqs - 1:
            front, ctxs, cur_next = hold(front, ctxs, cur_next)
        fronts.append(front)
        ctxs = ctxs + [front[0][0]] + [to_seq(front[0][n], n) for n in range(1, ns)]
        q, _ = after(q, front[0])
    near_half, _ = after(cur, fronts[-1][0])
    outer = [cur, cur_next, to_mate(near_half), to_mate(cur_next)]
    while len(downs) < nz:
        downs.append(to_ring(downs[-1]))
    downs = [x for d in downs for x in (d, to_mate(d))]
    kept, dctx_out, sums, gbup = middle(
        ns, nz, r, lengths, timesteps, idx, tokens, cotangent, small, ctxs, outer, downs
    )
    output, keep, send, ug, fl, cx, ag, r1 = kept

    two = ScatterRing(keep, send, ns, nz)
    dctx = [to_seq(dctx_out[n], n) for n in range(1, ns)]
    (fl, ug), _ = after((fl, ug), dctx_out)
    got = up_grad(ns, nz, r, idx, cx, ag, fl, ug, gbup)
    got, (dctx, two.terms[-1]) = after(got, (dctx, two.terms[-1]))
    dctx = [dctx_out[0]] + list(dctx)
    one = ScatterDirect(*got, ns, nz)
    two.step()
    one.step()
    dctx, _ = after(dctx, (one.last, two.last))
    r1 = r1.reshape(seqs, rows, model)
    backs = []
    for s in range(seqs):
        back = attend_back(ns, s, lengths, timesteps, idx, q, k, v, fronts[s][1], fronts[s][2], w_qkv, dctx)
        back, two.moving = hold(back, two.moving)
        backs.append(back)
        two.step()
        dctx, _ = after(dctx, two.last)
    low, _ = after(low, two.last)
    keep, send = qkv_grad(
        ns, nz, r, idx, low, backs[0][0], backs[1][0], sums, backs[0][3], backs[1][3], backs[0][4], backs[1][4]
    )
    near = [keep, to_mate(send)]

    one.terms[-1], near[0] = hold(one.terms[-1], near[0])
    one.step()
    one.terms[-1], near[1] = hold(one.terms[-1], near[1])
    planes = [[b[1], b[2]] for b in backs]
    planes, _ = after(planes, one.terms[-1])
    planes = [[p[0], to_bit(p[1], high - 1)] for p in planes]
    one.step()
    near, two.moving, planes, one.terms = hold(near, two.moving, planes, one.terms)
    two.fix()
    near_z = [to_z(added([t[a] for t in near]).astype(BF16), a) for a in range(1, nz)]
    two.step()
    n = ns // 2
    while n > 1:
        away = added_rows([[t[n // 2 : n] for t in p] for p in planes])
        n //= 2
        got = to_bit(away, n.bit_length() - 1)
        planes = [p + [got[i]] for i, p in enumerate(planes)]
    near_z, two.terms, planes = hold(near_z, two.terms, planes)
    own = added([t[0] for t in near] + near_z)
    others = [to_seq(own[n].astype(BF16), n) for n in range(1, ns)]
    grad_down = two.finish()
    grad_tokens = jnp.stack([added([t[0] for t in p] + [r1[s]]).astype(BF16) for s, p in enumerate(planes)])
    g_query, g_key, g_value, vectors = finish(ns, r, model, idx, own[0], others)
    return (
        output,
        grad_tokens,
        g_query,
        vectors[0],
        g_key,
        g_value,
        vectors[1],
        one.finish(slice(0, model)),
        vectors[2],
        vectors[3],
        vectors[4],
        one.finish(slice(model, 5 * model)),
        one.finish(slice(5 * model, 5 * model + 4 * r), 0),
        grad_down,
        vectors[5],
        vectors[6],
        vectors[7],
        vectors[8],
        vectors[9],
    )


def solution(mesh):
    split = P(("dp", "seq"))
    rows = P(("dp", "seq"), None)
    token = P("dp", "seq", None)
    items = P("dp", None)
    return jax.shard_map(
        body,
        mesh=mesh,
        in_specs=(
            token, items, items, rows, split, rows, rows, split, rows, split, split, split,
            rows, split, rows, split, split, split, split, split, token,
        ),
        out_specs=(
            token, token, rows, split, rows, rows, split, rows, split, split, split,
            rows, split, rows, split, split, split, split, split,
        ),
        check_vma=False,
    )
```

time: 544 us -> 417 us (0.77)
  waiting for transfers between devices: 227 us -> 169 us
  starting transfers between devices: 103 us -> 49 us
  local copies, waits for them, and re-layouts: 32.7 us -> 14.7 us
  other arithmetic: 17.6 us -> 29.7 us
  Pallas kernels: 154 us -> 147 us
    ppermute x33 -> x12, waiting for transfers between devices: 141 us -> 13.7 us  [to_seq(): return lax.ppermute(value, 'seq', [(i, i ^ k) for i in range(ns)])]
    ppermute x0 -> x15, waiting for transfers between devices: none -> 54.2 us  [to_bit(): return lax.ppermute(value, ('dp', 'seq'), pairs)]
    ppermute x18 -> x12, starting transfers between devices: 54.5 us -> 14.7 us  [to_z(): return lax.ppermute(value, 'dp', [(i, i ^ 2 * a) for i in range(nd)])]
    ppermute x33 -> x12, starting transfers between devices: 42.3 us -> 14.2 us  [to_seq(): return lax.ppermute(value, 'seq', [(i, i ^ k) for i in range(ns)])]
    ppermute x6, waiting for transfers between devices: 10.7 us -> 35.5 us  [to_ring(): return lax.ppermute(value, 'dp', [(i, (i + 2) % nd) for i in range(nd)])]
    ppermute x0 -> x15, starting transfers between devices: none -> 18 us  [to_bit(): return lax.ppermute(value, ('dp', 'seq'), pairs)]
    convert_element_type x12 -> x9, other arithmetic: 5.69 us -> 18 us  [the longest x3 9.89 us: step(): self.last = added(parts).astype(BF16)]
    unnamed x132 -> x75, local copies, waits for them, and re-layouts: 19.9 us -> 8.2 us
  transfers between devices with their start and end apart: 70 -> 56, of which waited for: 28 -> 25; matrix products, arithmetic and copies ran while one was open for 4% -> 6% of each run, Pallas kernels for 16% -> 25%
where the time goes in v2:
time: 417 us; the launch traced here: 411 us
  waiting for transfers between devices  169 us (41%)
  Pallas kernels  147 us (35%)
  starting transfers between devices  49 us (12%)
  other arithmetic  29.7 us (7%)
  local copies, waits for them, and re-layouts  14.7 us (4%)
    ppermute x12, waiting for transfers between devices, to_z(): return lax.ppermute(value, 'dp', [(i, i ^ 2 * a) for i in range(nd)])  56.6 us
    ppermute x15, waiting for transfers between devices, to_bit(): return lax.ppermute(value, ('dp', 'seq'), pairs)  54.2 us
    pallas_call x1, Pallas kernels, middle(): pl.pallas_call(functools.partial(middle_kernel, ns, nz, r), name='middle'...  43.3 us
    pallas_call x2, Pallas kernels, attend_back(): pl.pallas_call(functools.partial(attend_back_kernel, ns, seq), name='atte...  41.2 us
    ppermute x6, waiting for transfers between devices, to_ring(): return lax.ppermute(value, 'dp', [(i, (i + 2) % nd) for i in range(nd)])  35.5 us
    pallas_call x2, Pallas kernels, attend(): pl.pallas_call(functools.partial(attend_kernel, ns, seq), name='attend',...  26.6 us
    ppermute x15, starting transfers between devices, to_bit(): return lax.ppermute(value, ('dp', 'seq'), pairs)  18 us
    ppermute x12, starting transfers between devices, to_z(): return lax.ppermute(value, 'dp', [(i, i ^ 2 * a) for i in range(nd)])  14.7 us
  transfers between devices with their start and end apart: 56, of which 25 were waited for; matrix products, arithmetic and copies ran while one was open for 6% of the time, Pallas kernels for 25%

profile of v2, /device:TPU:0, one launch (start us, length us, event | category | flops | bytes accessed | tf_op | source)
XLA Modules:
  0.0 411.2 jit_solution(13521042298311498661)
XLA Ops:
  0.7 3.0 collective-permute-start
  11.8 8.9 %collective-permute-done.2 = bf16[2,32,896]{2,1,0:T(8,128)(2,1)S(1)} collective-permute-done((bf16[2,32,896]{2,1,0:T(8,128)(2,1)S(1)}, bf16[2,32,896]{2,1,0:T(8,128)(2,1)S(1)}, u32[]{:S(2)}, u32[]{:S(2)}) %collective-permute-start.2) | collective-permute-done | bytes 114720 | tf_op jit(solution)/shard_map/ppermute | solution.py:839
  24.2 3.6 collective-permute-start.7
  28.5 21.0 %collective-permute-done.5 = bf16[2,32,896]{2,1,0:T(8,128)(2,1)S(1)} collective-permute-done((bf16[2,32,896]{2,1,0:T(8,128)(2,1)S(1)}, bf16[2,32,896]{2,1,0:T(8,128)(2,1)S(1)}, u32[]{:S(2)}, u32[]{:S(2)}) %collective-permute-start.5) | collective-permute-done | bytes 114720 | tf_op jit(solution)/shard_map/ppermute | solution.py:839
  49.4 5.8 %collective-permute-done.6 = bf16[32,5248]{1,0:T(8,128)(2,1)S(1)} collective-permute-done((bf16[32,5248]{1,0:T(8,128)(2,1)S(1)}, bf16[32,5248]{1,0:T(8,128)(2,1)S(1)}, u32[]{:S(2)}, u32[]{:S(2)}) %collective-permute-start.6) | collective-permute-done | bytes 335904 | tf_op jit(solution)/shard_map/ppermute | solution.py:824
  63.4 6.0 %collective-permute-done.10 = bf16[4,32,896]{2,1,0:T(8,128)(2,1)S(1)} collective-permute-done((bf16[4,32,896]{2,1,0:T(8,128)(2,1)S(1)}, bf16[4,32,896]{2,1,0:T(8,128)(2,1)S(1)}, u32[]{:S(2)}, u32[]{:S(2)}) %collective-permute-start.10) | collective-permute-done | bytes 229408 | tf_op jit(solution)/shard_map/ppermute | solution.py:824
  69.5 9.5 %collective-permute-done.9 = bf16[4,32,896]{2,1,0:T(8,128)(2,1)S(1)} collective-permute-done((bf16[4,32,896]{2,1,0:T(8,128)(2,1)S(1)}, bf16[4,32,896]{2,1,0:T(8,128)(2,1)S(1)}, u32[]{:S(2)}, u32[]{:S(2)}) %collective-permute-start.9) | collective-permute-done | bytes 229408 | tf_op jit(solution)/shard_map/ppermute | solution.py:824
  83.5 9.4 %project.1 = (bf16[2,1024,256]{2,1,0:T(8,128)(2,1)}, bf16[2,1024,256]{2,1,0:T(8,128)(2,1)}, bf16[2,1024,256]{2,1,0:T(8,128)(2,1)}, bf16[2,1024,1024]{2,1,0:T(8,1...) custom-call(s32[2,8]{1,0:T(2,128)} %len_ref.11, s32[2,8]{1,0:T(2,128)} %tim_ref.7, s32[3]{0:T(128)} %pad_add_fusion.idx, ...), custom_call_target="tpu_custom_call" | custom-call | flops 3221225472 | bytes 14680064 | tf_op jit(solution)/shard_map/project/pallas_call | solution.py:192
  92.9 12.5 %attend.2 = (bf16[256,256]{1,0:T(8,128)(2,1)}, bf16[256,256]{1,0:T(8,128)(2,1)}, bf16[256,256]{1,0:T(8,128)(2,1)}, bf16[256,256]{1,0:T(8,128)(2,1)}, f32[1,1024,256]{2,1,0:T(8,128)}, /*index=5*/f32[1,16,1024]{2,1,0:T(8,128)}) custom-call(s32[2,8]{1,0:T(2,128)} %len_ref.11, s32[3]{0:T(128)} %pad_add_fusion.idx, ...), custom_call_target="tpu_custom_call" | custom-call | flops 4294967296 | bytes 4194304 | tf_op jit(solution)/shard_map/attend/pallas_call | solution.py:279
  105.4 3.0 collective-permute-done.14.refs_14_
  111.9 14.2 %attend.3 = (bf16[256,256]{1,0:T(8,128)(2,1)}, bf16[256,256]{1,0:T(8,128)(2,1)}, bf16[256,256]{1,0:T(8,128)(2,1)}, bf16[256,256]{1,0:T(8,128)(2,1)}, f32[1,1024,256]{2,1,0:T(8,128)}, /*index=5*/f32[1,16,1024]{2,1,0:T(8,128)}) custom-call(s32[2,8]{1,0:T(2,128)} %len_ref.11, s32[3]{0:T(128)} %pad_add_fusion.idx, ...), custom_call_target="tpu_custom_call" | custom-call | flops 4294967296 | bytes 4194304 | tf_op jit(solution)/shard_map/attend/pallas_call | solution.py:279
  126.1 9.0 %collective-permute-done.15.refs_16_ = bf16[4,128,1024]{2,1,0:T(8,128)(2,1)} collective-permute-done((bf16[4,128,1024]{2,1,0:T(8,128)(2,1)S(1)}, bf16[4,128,1024]{2,1,0:T(8,128)(2,1)}, u32[]{:S(2)}, u32[]{:S(2)}) %collective-permute-start.15) | collective-permute-done | bytes 1048608 | tf_op jit(solution)/shard_map/ppermute | solution.py:829
  136.4 5.4 %collective-permute-done.20.refs_5_ = bf16[256,256]{1,0:T(8,128)(2,1)S(1)} collective-permute-done((bf16[256,256]{1,0:T(8,128)(2,1)}, bf16[256,256]{1,0:T(8,128)(2,1)S(1)}, u32[]{:S(2)}, u32[]{:S(2)}) %collective-permute-start.20) | collective-permute-done | bytes 131104 | tf_op jit(solution)/shard_map/ppermute | solution.py:814
  143.4 3.7 collective-permute-done.21.refs_6_
  148.7 4.5 %collective-permute-done.22.refs_7_ = bf16[256,256]{1,0:T(8,128)(2,1)S(1)} collective-permute-done((bf16[256,256]{1,0:T(8,128)(2,1)}, bf16[256,256]{1,0:T(8,128)(2,1)S(1)}, u32[]{:S(2)}, u32[]{:S(2)}) %collective-permute-start.22) | collective-permute-done | bytes 131104 | tf_op jit(solution)/shard_map/ppermute | solution.py:814
  153.8 9.5 %collective-permute-done.28.refs_18_ = bf16[4,128,1024]{2,1,0:T(8,128)(2,1)S(1)} collective-permute-done((bf16[4,128,1024]{2,1,0:T(8,128)(2,1)}, bf16[4,128,1024]{2,1,0:T(8,128)(2,1)S(1)}, u32[]{:S(2)}, u32[]{:S(2)}) %collective-permute-start.28) | collective-permute-done | bytes 1048608 | tf_op jit(solution)/shard_map/ppermute | solution.py:829
  169.4 43.3 %middle.1 = (bf16[2,256,1024]{2,1,0:T(8,128)(2,1)}, bf16[4,4,128,1024]{3,2,1,0:T(8,128)(2,1)}, bf16[4,4,128,1024]{3,2,1,0:T(8,128)(2,1)}, bf16[512,4096]{1,0:T(8...) custom-call(s32[2,8]{1,0:T(2,128)} %len_ref.11, ...), custom_call_target="tpu_custom_call" | custom-call | flops 19327352832 | bytes 41943040 | tf_op jit(solution)/shard_map/middle/pallas_call | solution.py:610
  216.4 14.0 %up_grad.1 = (bf16[4,4,32,5248]{3,2,1,0:T(8,128)(2,1)}, bf16[4,4,32,5248]{3,2,1,0:T(8,128)(2,1)}) custom-call(s32[3]{0:T(128)} %pad_add_fusion.idx, bf16[512,1024]{1,0:T(8,128)(2,1)} %get-tuple-element.271.cx_ref, bf16[512,1024]{1,0:T(8,128)(2,1)} %get-tuple-element.272.ag_ref, bf16[512,1024]{1,0:T(8,128)(2,1)} %get-tuple-element.279.fl_ref, ...), custom_call_target="tpu_custom_call" | custom-call | flops 5502926848 | bytes 10485760 | tf_op jit(solution)/shard_map/up_grad/pallas_call | solution.py:719
  232.5 4.7 %fusion.17 = (bf16[4,2,32,5248]{3,2,1,0:T(8,128)(2,1)}, bf16[4,2,32,5248]{3,2,1,0:T(8,128)(2,1)S(1)}) fusion(bf16[4,4,32,5248]{3,2,1,0:T(8,128)(2,1)} %get-tuple-element.286), kind=kLoop, calls=%fused_computation.72 | loop fusion | bytes 10747904 | tf_op jit(solution)/shard_map/slice | solution.py:909
  245.9 19.6 %attend_back.2 = (bf16[1024,768]{1,0:T(8,128)(2,1)}, bf16[2,256,1024]{2,1,0:T(8,128)(2,1)}, bf16[2,256,1024]{2,1,0:T(8,128)(2,1)}, f32[8,1024]{1,0:T(8,128)}, f32[8,768]{1,0:T(8,128)}) custom-call(s32[2,8]{1,0:T(2,128)} %len_ref.11, s32[2,8]{1,0:T(2,128)} %tim_ref.7, s32[3]{0:T(128)} %pad_add_fusion.idx, bf16[2,1024,256]{2,1,0:T(8,128)(2,1)} %get-tuple-element.290.q_ref, ...), custom_call_target="tpu_custom_call" | custom-call | flops 10737418240 | bytes 10485760 | tf_op jit(solution)/shard_map/attend_back/pallas_call | solution.py:377
  267.8 3.5 fusion
  271.3 21.5 %attend_back.3 = (bf16[1024,768]{1,0:T(8,128)(2,1)}, bf16[2,256,1024]{2,1,0:T(8,128)(2,1)}, bf16[2,256,1024]{2,1,0:T(8,128)(2,1)}, f32[8,1024]{1,0:T(8,128)}, f32[8,768]{1,0:T(8,128)}) custom-call(s32[2,8]{1,0:T(2,128)} %len_ref.11, s32[2,8]{1,0:T(2,128)} %tim_ref.7, s32[3]{0:T(128)} %pad_add_fusion.idx, bf16[2,1024,256]{2,1,0:T(8,128)(2,1)} %get-tuple-element.290.q_ref, ...), custom_call_target="tpu_custom_call" | custom-call | flops 10737418240 | bytes 10485760 | tf_op jit(solution)/shard_map/attend_back/pallas_call | solution.py:377
  292.8 5.4 %collective-permute-done.37 = bf16[4,128,1024]{2,1,0:T(8,128)(2,1)} collective-permute-done((bf16[4,128,1024]{2,1,0:T(8,128)(2,1)}, bf16[4,128,1024]{2,1,0:T(8,128)(2,1)}, u32[]{:S(2)}, u32[]{:S(2)}) %collective-permute-start.37) | collective-permute-done | bytes 1048608 | tf_op jit(solution)/shard_map/ppermute | solution.py:829
  298.2 3.5 fusion.1
  301.6 8.6 %qkv_grad.1 = (bf16[4,4,32,896]{3,2,1,0:T(8,128)(2,1)}, bf16[4,4,32,896]{3,2,1,0:T(8,128)(2,1)}) custom-call(s32[3]{0:T(128)} %pad_add_fusion.idx, bf16[2,1024,1024]{2,1,0:T(8,128)(2,1)} %get-tuple-element.319.low_ref, bf16[1024,768]{1,0:T(8,128)(2,1)} %get-tuple-element.320.g0_ref, bf16[1024,768]{1,0:T(8,128)(2,1)} %get-tuple-element.321.g1_ref, ...), custom_call_target="tpu_custom_call" | custom-call | flops 3758096384 | bytes 12582912 | tf_op jit(solution)/shard_map/qkv_grad/pallas_call | solution.py:768
  315.8 14.9 %collective-permute-done.39 = bf16[4,1,32,5248]{3,2,1,0:T(8,128)(2,1)S(1)} collective-permute-done((bf16[4,1,32,5248]{3,2,1,0:T(8,128)(2,1)S(1)}, bf16[4,1,32,5248]{3,2,1,0:T(8,128)(2,1)S(1)}, u32[]{:S(2)}, u32[]{:S(2)}) %collective-permute-start.39) | collective-permute-done | bytes 1343520 | tf_op jit(solution)/shard_map/ppermute | solution.py:839
  334.9 6.4 %collective-permute-done.41 = bf16[4,128,1024]{2,1,0:T(8,128)(2,1)S(1)} collective-permute-done((bf16[4,128,1024]{2,1,0:T(8,128)(2,1)S(1)}, bf16[4,128,1024]{2,1,0:T(8,128)(2,1)S(1)}, u32[]{:S(2)}, u32[]{:S(2)}) %collective-permute-start.41) | collective-permute-done | bytes 1048608 | tf_op jit(solution)/shard_map/ppermute | solution.py:829
  341.3 7.2 %collective-permute-done.46 = bf16[32,5248]{1,0:T(8,128)(2,1)S(1)} collective-permute-done((bf16[32,5248]{1,0:T(8,128)(2,1)S(1)}, bf16[32,5248]{1,0:T(8,128)(2,1)S(1)}, u32[]{:S(2)}, u32[]{:S(2)}) %collective-permute-start.46) | collective-permute-done | bytes 335904 | tf_op jit(solution)/shard_map/ppermute | solution.py:824
  348.5 21.0 %collective-permute-done.45 = bf16[32,5248]{1,0:T(8,128)(2,1)S(1)} collective-permute-done((bf16[32,5248]{1,0:T(8,128)(2,1)S(1)}, bf16[32,5248]{1,0:T(8,128)(2,1)S(1)}, u32[]{:S(2)}, u32[]{:S(2)}) %collective-permute-start.45) | collective-permute-done | bytes 335904 | tf_op jit(solution)/shard_map/ppermute | solution.py:824
  378.0 4.4 %collective-permute-start.47 = (bf16[4,32,896]{2,1,0:T(8,128)(2,1)S(1)}, bf16[4,32,896]{2,1,0:T(8,128)(2,1)S(1)}, u32[]{:S(2)}, u32[]{:S(2)}) collective-permute-start(bf16[4,32,896]{2,1,0:T(8,128)(2,1)S(1)} %get-tuple-element.384), channel_id=1, source_target_pairs={{0,8},{4,12},{8,0},{12,4},{16,24},{20,28},{24,16},{28,20},{1,9},{5... | collective-permute-start | bytes 688136 | tf_op jit(solution)/shard_map/ppermute | solution.py:824
  384.0 6.5 %collective-permute-done.51 = bf16[2,1,256,1024]{3,2,1,0:T(8,128)(2,1)S(1)} collective-permute-done((bf16[2,1,256,1024]{3,2,1,0:T(8,128)(2,1)S(1)}, bf16[2,1,256,1024]{3,2,1,0:T(8,128)(2,1)S(1)}, u32[]{:S(2)}, u32[]{:S(2)}) %collective-permute-start.51) | collective-permute-done | bytes 1048608 | tf_op jit(solution)/shard_map/ppermute | solution.py:839
  390.6 7.0 %collective-permute-done.48 = bf16[4,32,896]{2,1,0:T(8,128)(2,1)S(1)} collective-permute-done((bf16[4,32,896]{2,1,0:T(8,128)(2,1)S(1)}, bf16[4,32,896]{2,1,0:T(8,128)(2,1)S(1)}, u32[]{:S(2)}, u32[]{:S(2)}) %collective-permute-start.48) | collective-permute-done | bytes 229408 | tf_op jit(solution)/shard_map/ppermute | solution.py:824
  (201 shorter events, 89.2 us)
Async XLA Ops:
  0.7 20.0 %collective-permute-start = (bf16[1,2,256,1024]{3,2,1,0:T(8,128)(2,1)}, bf16[1,2,256,1024]{3,2,1,0:T(8,128)(2,1)S(1)}, u32[]{:S(2)}, u32[]{:S(2)}) collective-permute-start(bf16[1,2,256,1024]{3,2,1,0:T(8,128)(2,1)} %bitcast.111), channel_id=1, source_target_pairs={{0,1},{1,0},{2,3},{3,2},{4,6},{5,7},{6,4},{7,5},{8,9},{9,8},{10,11... | collective-permute-start | bytes 3145736 | tf_op jit(solution)/shard_map/ppermute | solution.py:839
  22.1 33.2 %collective-permute-start.4 = (bf16[2,2,256,1024]{3,2,1,0:T(8,128)(2,1)S(1)}, bf16[2,2,256,1024]{3,2,1,0:T(8,128)(2,1)S(1)}, u32[]{:S(2)}, u32[]{:S(2)}) collective-permute-start(bf16[2,2,256,1024]{3,2,1,0:T(8,128)(2,1)S(1)} %constant_dynamic-update-slice_fusion.refs_0_), channel_id=1, source_target_pairs={{0,2},{1,3},{2,0},{3,1},{4,5},{5,4},{6,7},{7,6},{8,10},{9,11},{10,... | collective-permute-start | bytes 6291464 | tf_op jit(solution)/shard_map/ppermute | solution.py:839
  24.2 25.2 %collective-permute-start.7 = (bf16[32,5248]{1,0:T(8,128)(2,1)S(1)}, bf16[32,5248]{1,0:T(8,128)(2,1)S(1)}, u32[]{:S(2)}, u32[]{:S(2)}) collective-permute-start(bf16[32,5248]{1,0:T(8,128)(2,1)S(1)} %copy-done.10), channel_id=1, source_target_pairs={{0,24},{4,28},{8,16},{12,20},{16,8},{20,12},{24,0},{28,4},{1,25},{... | collective-permute-start | bytes 1007624 | tf_op jit(solution)/shard_map/ppermute | solution.py:824
  27.8 27.5 %collective-permute-start.6 = (bf16[32,5248]{1,0:T(8,128)(2,1)S(1)}, bf16[32,5248]{1,0:T(8,128)(2,1)S(1)}, u32[]{:S(2)}, u32[]{:S(2)}) collective-permute-start(bf16[32,5248]{1,0:T(8,128)(2,1)S(1)} %copy-done.10), channel_id=1, source_target_pairs={{0,16},{4,20},{8,24},{12,28},{16,0},{20,4},{24,8},{28,12},{1,17},{... | collective-permute-start | bytes 1007624 | tf_op jit(solution)/shard_map/ppermute | solution.py:824
  27.8 21.6 %collective-permute-start.5 = (bf16[2,32,896]{2,1,0:T(8,128)(2,1)S(1)}, bf16[2,32,896]{2,1,0:T(8,128)(2,1)S(1)}, u32[]{:S(2)}, u32[]{:S(2)}) collective-permute-start(bf16[2,32,896]{2,1,0:T(8,128)(2,1)S(1)} %pad_maximum_fusion.6), channel_id=1, source_target_pairs={{0,2},{1,3},{2,0},{3,1},{4,5},{5,4},{6,7},{7,6},{8,10},{9,11},{10,... | collective-permute-start | bytes 344072 | tf_op jit(solution)/shard_map/ppermute | solution.py:839
  56.8 23.0 %collective-permute-start.12 = (bf16[1,4,32,5248]{3,2,1,0:T(8,128)(2,1)S(1)}, bf16[1,4,32,5248]{3,2,1,0:T(8,128)(2,1)S(1)}, u32[]{:S(2)}, u32[]{:S(2)}) collective-permute-start(bf16[1,4,32,5248]{3,2,1,0:T(8,128)(2,1)S(1)} %maximum_bitcast_fusion), channel_id=1, source_target_pairs={{0,1},{1,0},{2,3},{3,2},{4,6},{5,7},{6,4},{7,5},{8,9},{9,8},{10,11... | collective-permute-start | bytes 4030472 | tf_op jit(solution)/shard_map/ppermute | solution.py:839
  57.4 21.5 %collective-permute-start.11 = (bf16[2,128,1024]{2,1,0:T(8,128)(2,1)S(1)}, bf16[2,128,1024]{2,1,0:T(8,128)(2,1)S(1)}, u32[]{:S(2)}, u32[]{:S(2)}) collective-permute-start(bf16[2,128,1024]{2,1,0:T(8,128)(2,1)S(1)} %pad_maximum_fusion.3), channel_id=1, source_target_pairs={{0,2},{1,3},{2,0},{3,1},{4,5},{5,4},{6,7},{7,6},{8,10},{9,11},{10,... | collective-permute-start | bytes 1572872 | tf_op jit(solution)/shard_map/ppermute | solution.py:839
  80.1 55.0 %collective-permute-start.19 = (bf16[2,4,32,5248]{3,2,1,0:T(8,128)(2,1)S(1)}, bf16[2,4,32,5248]{3,2,1,0:T(8,128)(2,1)}, u32[]{:S(2)}, u32[]{:S(2)}) collective-permute-start(bf16[2,4,32,5248]{3,2,1,0:T(8,128)(2,1)S(1)} %constant_dynamic-update-slice_fusion.4.refs_8_), channel_id=1, source_target_pairs={{0,2},{1,3},{2,0},{3,1},{4,5},{5,4},{6,7},{7,6},{8,10},{9,11},{10,... | collective-permute-start | bytes 8060936 | tf_op jit(solution)/shard_map/ppermute | solution.py:839
  81.0 27.4 %collective-permute-start.14 = (bf16[4,128,1024]{2,1,0:T(8,128)(2,1)S(1)}, bf16[4,128,1024]{2,1,0:T(8,128)(2,1)S(1)}, u32[]{:S(2)}, u32[]{:S(2)}) collective-permute-start(bf16[4,128,1024]{2,1,0:T(8,128)(2,1)S(1)} %constant_dynamic-update-slice_fusion.2.refs_12_), channel_id=1, source_target_pairs={{0,8},{4,12},{8,16},{12,20},{16,24},{20,28},{24,0},{28,4},{1,9},{5... | collective-permute-start | bytes 3145736 | tf_op jit(solution)/shard_map/ppermute | solution.py:829
  108.4 26.7 %collective-permute-start.15 = (bf16[4,128,1024]{2,1,0:T(8,128)(2,1)S(1)}, bf16[4,128,1024]{2,1,0:T(8,128)(2,1)}, u32[]{:S(2)}, u32[]{:S(2)}) collective-permute-start(bf16[4,128,1024]{2,1,0:T(8,128)(2,1)S(1)} %collective-permute-done.14.refs_14_), channel_id=1, source_target_pairs={{0,8},{4,12},{8,16},{12,20},{16,24},{20,28},{24,0},{28,4},{1,9},{5... | collective-permute-start | bytes 3145736 | tf_op jit(solution)/shard_map/ppermute | solution.py:829
  108.4 26.7 %collective-permute-start.16 = (bf16[256,256]{1,0:T(8,128)(2,1)}, bf16[256,256]{1,0:T(8,128)(2,1)S(1)}, u32[]{:S(2)}, u32[]{:S(2)}) collective-permute-start(bf16[256,256]{1,0:T(8,128)(2,1)} %get-tuple-element.239), channel_id=1, source_target_pairs={{0,1},{1,0},{2,3},{3,2},{4,5},{5,4},{6,7},{7,6},{8,9},{9,8},{10,11... | collective-permute-start | bytes 393224 | tf_op jit(solution)/shard_map/ppermute | solution.py:814
  109.0 26.1 %collective-permute-start.17 = (bf16[256,256]{1,0:T(8,128)(2,1)}, bf16[256,256]{1,0:T(8,128)(2,1)S(1)}, u32[]{:S(2)}, u32[]{:S(2)}) collective-permute-start(bf16[256,256]{1,0:T(8,128)(2,1)} %get-tuple-element.240), channel_id=1, source_target_pairs={{0,2},{1,3},{2,0},{3,1},{4,6},{5,7},{6,4},{7,5},{8,10},{9,11},{10,... | collective-permute-start | bytes 393224 | tf_op jit(solution)/shard_map/ppermute | solution.py:814
  110.5 24.6 %collective-permute-start.18 = (bf16[256,256]{1,0:T(8,128)(2,1)}, bf16[256,256]{1,0:T(8,128)(2,1)S(1)}, u32[]{:S(2)}, u32[]{:S(2)}) collective-permute-start(bf16[256,256]{1,0:T(8,128)(2,1)} %get-tuple-element.241), channel_id=1, source_target_pairs={{0,3},{1,2},{2,1},{3,0},{4,7},{5,6},{6,5},{7,4},{8,11},{9,10},{10,... | collective-permute-start | bytes 393224 | tf_op jit(solution)/shard_map/ppermute | solution.py:814
  135.2 30.8 %collective-permute-start.23 = (bf16[2,4,32,5248]{3,2,1,0:T(8,128)(2,1)S(1)}, bf16[2,4,32,5248]{3,2,1,0:T(8,128)(2,1)S(1)}, u32[]{:S(2)}, u32[]{:S(2)}) collective-permute-start(bf16[2,4,32,5248]{3,2,1,0:T(8,128)(2,1)S(1)} %constant_dynamic-update-slice_fusion.4.refs_8_), channel_id=1, source_target_pairs={{0,4},{4,0},{8,12},{12,8},{16,20},{20,16},{24,28},{28,24},{1,5},{5... | collective-permute-start | bytes 8060936 | tf_op jit(solution)/shard_map/ppermute | solution.py:819
  135.2 32.4 %collective-permute-start.24 = (bf16[2,4,32,5248]{3,2,1,0:T(8,128)(2,1)}, bf16[2,4,32,5248]{3,2,1,0:T(8,128)(2,1)S(1)}, u32[]{:S(2)}, u32[]{:S(2)}) collective-permute-start(bf16[2,4,32,5248]{3,2,1,0:T(8,128)(2,1)} %collective-permute-done.19.refs_9_), channel_id=1, source_target_pairs={{0,4},{4,0},{8,12},{12,8},{16,20},{20,16},{24,28},{28,24},{1,5},{5... | collective-permute-start | bytes 8060936 | tf_op jit(solution)/shard_map/ppermute | solution.py:819
  135.7 17.5 %collective-permute-start.25 = (bf16[4,128,1024]{2,1,0:T(8,128)(2,1)S(1)}, bf16[4,128,1024]{2,1,0:T(8,128)(2,1)S(1)}, u32[]{:S(2)}, u32[]{:S(2)}) collective-permute-start(bf16[4,128,1024]{2,1,0:T(8,128)(2,1)S(1)} %constant_dynamic-update-slice_fusion.2.refs_12_), channel_id=1, source_target_pairs={{0,4},{4,0},{8,12},{12,8},{16,20},{20,16},{24,28},{28,24},{1,5},{5... | collective-permute-start | bytes 3145736 | tf_op jit(solution)/shard_map/ppermute | solution.py:819
  135.8 27.5 %collective-permute-start.28 = (bf16[4,128,1024]{2,1,0:T(8,128)(2,1)}, bf16[4,128,1024]{2,1,0:T(8,128)(2,1)S(1)}, u32[]{:S(2)}, u32[]{:S(2)}) collective-permute-start(bf16[4,128,1024]{2,1,0:T(8,128)(2,1)} %collective-permute-done.15.refs_16_), channel_id=1, source_target_pairs={{0,8},{4,12},{8,16},{12,20},{16,24},{20,28},{24,0},{28,4},{1,9},{5... | collective-permute-start | bytes 3145736 | tf_op jit(solution)/shard_map/ppermute | solution.py:829
  212.7 17.7 %collective-permute-start.33 = (bf16[4,4,128,1024]{3,2,1,0:T(8,128)(2,1)}, bf16[4,4,128,1024]{3,2,1,0:T(8,128)(2,1)S(1)}, u32[]{:S(2)}, u32[]{:S(2)}) collective-permute-start(bf16[4,4,128,1024]{3,2,1,0:T(8,128)(2,1)} %get-tuple-element.284), channel_id=1, source_target_pairs={{0,4},{4,0},{8,12},{12,8},{16,20},{20,16},{24,28},{28,24},{1,5},{5... | collective-permute-start | bytes 12582920 | tf_op jit(solution)/shard_map/ppermute | solution.py:819
  212.9 17.5 %collective-permute-start.30 = (bf16[2,256,256]{2,1,0:T(8,128)(2,1)}, bf16[2,256,256]{2,1,0:T(8,128)(2,1)S(1)}, u32[]{:S(2)}, u32[]{:S(2)}) collective-permute-start(bf16[2,256,256]{2,1,0:T(8,128)(2,1)} %get-tuple-element.276), channel_id=1, source_target_pairs={{0,1},{1,0},{2,3},{3,2},{4,5},{5,4},{6,7},{7,6},{8,9},{9,8},{10,11... | collective-permute-start | bytes 786440 | tf_op jit(solution)/shard_map/ppermute | solution.py:814
  240.1 27.7 %collective-permute-start.36 = (bf16[4,128,1024]{2,1,0:T(8,128)(2,1)}, bf16[4,128,1024]{2,1,0:T(8,128)(2,1)}, u32[]{:S(2)}, u32[]{:S(2)}) collective-permute-start(bf16[4,128,1024]{2,1,0:T(8,128)(2,1)} %fusion.2), channel_id=1, source_target_pairs={{0,8},{4,12},{8,16},{12,20},{16,24},{20,28},{24,0},{28,4},{1,9},{5... | collective-permute-start | bytes 3145736 | tf_op jit(solution)/shard_map/ppermute | solution.py:829
  240.1 70.2 %collective-permute-start.38 = (bf16[4,2,32,5248]{3,2,1,0:T(8,128)(2,1)}, bf16[4,2,32,5248]{3,2,1,0:T(8,128)(2,1)}, u32[]{:S(2)}, u32[]{:S(2)}) collective-permute-start(bf16[4,2,32,5248]{3,2,1,0:T(8,128)(2,1)} %get-tuple-element.378), channel_id=1, source_target_pairs={{0,4},{4,0},{8,12},{12,8},{16,20},{20,16},{24,28},{28,24},{1,5},{5... | collective-permute-start | bytes 8060936 | tf_op jit(solution)/shard_map/ppermute | solution.py:819
  244.3 65.9 %collective-permute-start.35 = (bf16[4,2,32,5248]{3,2,1,0:T(8,128)(2,1)}, bf16[4,2,32,5248]{3,2,1,0:T(8,128)(2,1)}, u32[]{:S(2)}, u32[]{:S(2)}) collective-permute-start(bf16[4,2,32,5248]{3,2,1,0:T(8,128)(2,1)} %add_convert_fusion), channel_id=1, source_target_pairs={{0,2},{1,3},{2,0},{3,1},{4,5},{5,4},{6,7},{7,6},{8,10},{9,11},{10,... | collective-permute-start | bytes 8060936 | tf_op jit(solution)/shard_map/ppermute | solution.py:839
  271.3 26.9 %collective-permute-start.37 = (bf16[4,128,1024]{2,1,0:T(8,128)(2,1)}, bf16[4,128,1024]{2,1,0:T(8,128)(2,1)}, u32[]{:S(2)}, u32[]{:S(2)}) collective-permute-start(bf16[4,128,1024]{2,1,0:T(8,128)(2,1)} %fusion), channel_id=1, source_target_pairs={{0,8},{4,12},{8,16},{12,20},{16,24},{20,28},{24,0},{28,4},{1,9},{5... | collective-permute-start | bytes 3145736 | tf_op jit(solution)/shard_map/ppermute | solution.py:829
  312.6 18.0 %collective-permute-start.39 = (bf16[4,1,32,5248]{3,2,1,0:T(8,128)(2,1)S(1)}, bf16[4,1,32,5248]{3,2,1,0:T(8,128)(2,1)S(1)}, u32[]{:S(2)}, u32[]{:S(2)}) collective-permute-start(bf16[4,1,32,5248]{3,2,1,0:T(8,128)(2,1)S(1)} %add_convert_fusion.1), channel_id=1, source_target_pairs={{0,1},{1,0},{2,3},{3,2},{4,6},{5,7},{6,4},{7,5},{8,9},{9,8},{10,11... | collective-permute-start | bytes 4030472 | tf_op jit(solution)/shard_map/ppermute | solution.py:839
  313.4 27.9 %collective-permute-start.41 = (bf16[4,128,1024]{2,1,0:T(8,128)(2,1)S(1)}, bf16[4,128,1024]{2,1,0:T(8,128)(2,1)S(1)}, u32[]{:S(2)}, u32[]{:S(2)}) collective-permute-start(bf16[4,128,1024]{2,1,0:T(8,128)(2,1)S(1)} %copy-done.5), channel_id=1, source_target_pairs={{0,8},{4,12},{8,16},{12,20},{16,24},{20,28},{24,0},{28,4},{1,9},{5... | collective-permute-start | bytes 3145736 | tf_op jit(solution)/shard_map/ppermute | solution.py:829
  330.7 38.8 %collective-permute-start.42 = (bf16[2,256,1024]{2,1,0:T(8,128)(2,1)S(1)}, bf16[2,256,1024]{2,1,0:T(8,128)(2,1)S(1)}, u32[]{:S(2)}, u32[]{:S(2)}) collective-permute-start(bf16[2,256,1024]{2,1,0:T(8,128)(2,1)S(1)} %copy-done.17), channel_id=1, source_target_pairs={{0,2},{1,3},{2,0},{3,1},{4,5},{5,4},{6,7},{7,6},{8,10},{9,11},{10,... | collective-permute-start | bytes 3145736 | tf_op jit(solution)/shard_map/ppermute | solution.py:839
  332.2 37.3 %collective-permute-start.43 = (bf16[2,256,1024]{2,1,0:T(8,128)(2,1)S(1)}, bf16[2,256,1024]{2,1,0:T(8,128)(2,1)S(1)}, u32[]{:S(2)}, u32[]{:S(2)}) collective-permute-start(bf16[2,256,1024]{2,1,0:T(8,128)(2,1)S(1)} %copy-done.18), channel_id=1, source_target_pairs={{0,2},{1,3},{2,0},{3,1},{4,5},{5,4},{6,7},{7,6},{8,10},{9,11},{10,... | collective-permute-start | bytes 3145736 | tf_op jit(solution)/shard_map/ppermute | solution.py:839
  334.8 34.7 %collective-permute-start.45 = (bf16[32,5248]{1,0:T(8,128)(2,1)S(1)}, bf16[32,5248]{1,0:T(8,128)(2,1)S(1)}, u32[]{:S(2)}, u32[]{:S(2)}) collective-permute-start(bf16[32,5248]{1,0:T(8,128)(2,1)S(1)} %get-tuple-element.376), channel_id=1, source_target_pairs={{0,16},{4,20},{8,24},{12,28},{16,0},{20,4},{24,8},{28,12},{1,17},{... | collective-permute-start | bytes 1007624 | tf_op jit(solution)/shard_map/ppermute | solution.py:824
  341.3 28.2 %collective-permute-start.44 = (bf16[32,5248]{1,0:T(8,128)(2,1)S(1)}, bf16[32,5248]{1,0:T(8,128)(2,1)S(1)}, u32[]{:S(2)}, u32[]{:S(2)}) collective-permute-start(bf16[32,5248]{1,0:T(8,128)(2,1)S(1)} %get-tuple-element.377), channel_id=1, source_target_pairs={{0,8},{4,12},{8,0},{12,4},{16,24},{20,28},{24,16},{28,20},{1,9},{5... | collective-permute-start | bytes 1007624 | tf_op jit(solution)/shard_map/ppermute | solution.py:824
  371.0 26.6 %collective-permute-start.50 = (bf16[1,2,128,1024]{3,2,1,0:T(8,128)(2,1)S(1)}, bf16[1,2,128,1024]{3,2,1,0:T(8,128)(2,1)S(1)}, u32[]{:S(2)}, u32[]{:S(2)}) collective-permute-start(bf16[1,2,128,1024]{3,2,1,0:T(8,128)(2,1)S(1)} %add_convert_fusion.5), channel_id=1, source_target_pairs={{0,2},{1,3},{2,0},{3,1},{4,5},{5,4},{6,7},{7,6},{8,10},{9,11},{10,... | collective-permute-start | bytes 1572872 | tf_op jit(solution)/shard_map/ppermute | solution.py:839
  378.0 19.5 %collective-permute-start.48 = (bf16[4,32,896]{2,1,0:T(8,128)(2,1)S(1)}, bf16[4,32,896]{2,1,0:T(8,128)(2,1)S(1)}, u32[]{:S(2)}, u32[]{:S(2)}) collective-permute-start(bf16[4,32,896]{2,1,0:T(8,128)(2,1)S(1)} %get-tuple-element.383), channel_id=1, source_target_pairs={{0,16},{4,20},{8,24},{12,28},{16,0},{20,4},{24,8},{28,12},{1,17},{... | collective-permute-start | bytes 688136 | tf_op jit(solution)/shard_map/ppermute | solution.py:824
  378.0 19.5 %collective-permute-start.47 = (bf16[4,32,896]{2,1,0:T(8,128)(2,1)S(1)}, bf16[4,32,896]{2,1,0:T(8,128)(2,1)S(1)}, u32[]{:S(2)}, u32[]{:S(2)}) collective-permute-start(bf16[4,32,896]{2,1,0:T(8,128)(2,1)S(1)} %get-tuple-element.384), channel_id=1, source_target_pairs={{0,8},{4,12},{8,0},{12,4},{16,24},{20,28},{24,16},{28,20},{1,9},{5... | collective-permute-start | bytes 688136 | tf_op jit(solution)/shard_map/ppermute | solution.py:824
  (60 other events, 925.8 us)

commit v3 on v2

--- a/solution.py
+++ b/solution.py
@@ -102,9 +102,11 @@
 def pack_kernel(ns, count, idx, *refs):
     srcs, (out_ref, outer_ref), dsts, sem = refs[:count], refs[count : count + 2], refs[count + 2 : -1], refs[-1]
     r, model = srcs[0].shape
-    ff = srcs[-1].shape[1]
+    ff = srcs[-2].shape[1]
     hg = model // ns
     targets = list(dsts) + [outer_ref.at[:, 0:model], outer_ref.at[:, model : model + ff]]
+    targets.append(outer_ref.at[:, model + ff + PAD :])
+    srcs = list(srcs[:-1]) + [srcs[-1].at[0:r]]
     copies = [pltpu.make_async_copy(a, b, sem.at[n]) for n, (a, b) in enumerate(zip(srcs, targets))]
     for copy in copies:
         copy.start()
@@ -122,22 +124,22 @@
     row = dsts[-1][...].astype(F32).reshape(1, 4 * r)
     if PAD > 4 * r:
         row = jnp.concatenate([row, jnp.zeros((1, PAD - 4 * r), F32)], axis=1)
-    outer_ref[:, model + ff :] = jnp.broadcast_to(row, (r, PAD)).astype(BF16)
-
-
-def pack(ns, idx, w_query, w_key, w_value, vectors, b_up, w_out, w_up):
+    outer_ref[:, model + ff : model + ff + PAD] = jnp.broadcast_to(row, (r, PAD)).astype(BF16)
+
+
+def pack(ns, idx, w_query, w_key, w_value, vectors, b_up, w_out, w_up, w_down):
     r, model = w_query.shape
-    args = (w_query, w_key, w_value, *vectors, b_up, w_out, w_up)
+    args = (w_query, w_key, w_value, *vectors, b_up, w_out, w_up, w_down)
     return pl.pallas_call(
         functools.partial(pack_kernel, ns, len(args)),
         name="pack",
         out_shape=[
             jax.ShapeDtypeStruct((ns, r, 3 * (model // ns) + PAD), BF16),
-            jax.ShapeDtypeStruct((r, model + w_up.shape[1] + PAD), BF16),
+            jax.ShapeDtypeStruct((r, model + w_up.shape[1] + PAD + model), BF16),
         ],
         in_specs=[sspec()] + [aspec()] * len(args),
         out_specs=[vspec()] * 2,
-        scratch_shapes=[VMEM(a.shape, a.dtype) for a in args[:-2]]
+        scratch_shapes=[VMEM(a.shape, a.dtype) for a in args[:-3]]
         + [pltpu.SemaphoreType.DMA((len(args),))],
         compiler_params=params(60),
     )(idx, *args)
@@ -216,6 +218,7 @@
 
 
 def attend_kernel(ns, s, len_ref, idx, q_ref, k_ref, v_ref, *refs):
+    refs = refs[ns:] if s else refs
     ctx_refs = refs[:ns]
     ctxf_ref, lse_ref, bias, probs, scale = refs[ns:]
     j = idx[2]
@@ -238,7 +241,7 @@
     pl.when(jnp.logical_not(alone))(lambda: heads(lambda st, at: st + bias[:, at]))
     for k in range(ns):
         here = pl.ds(pl.multiple_of((j ^ k) * rows, rows), rows)
-        ctx_refs[k][...] = ctxf_ref[0, here, :].astype(BF16)
+        ctx_refs[k][0] = ctxf_ref[0, here, :].astype(BF16)
 
 
 def whole_sequence(len_ref, seq, full):
@@ -267,11 +270,11 @@
         ctxf_ref[0, :, cols] = tn(probs[h % probs.shape[0]], vh) * by_row[:, h : h + 1]
 
 
-def attend(ns, seq, lengths, idx, q, k, v):
+def attend(ns, seq, lengths, idx, q, k, v, before):
     seqs, full, hg = q.shape
     rows = full // ns
     groups = hg // PAIR
-    outs = [jax.ShapeDtypeStruct((rows, hg), BF16)] * ns + [
+    outs = [jax.ShapeDtypeStruct((seqs, rows, hg), BF16)] * ns + [
         jax.ShapeDtypeStruct((1, full, hg), F32),
         jax.ShapeDtypeStruct((1, 8 * groups, full), F32),
     ]
@@ -281,8 +284,8 @@
         name="attend",
         out_shape=outs,
         grid=(groups,),
-        in_specs=[sspec(), sspec(), wide, wide, wide],
-        out_specs=[pl.BlockSpec((rows, PAIR), lambda i: (0, i))] * ns
+        in_specs=[sspec(), sspec(), wide, wide, wide] + [aspec()] * len(before),
+        out_specs=[pl.BlockSpec((1, rows, PAIR), lambda i: (seq, 0, i))] * ns
         + [
             pl.BlockSpec((1, full, PAIR), lambda i: (0, 0, i)),
             pl.BlockSpec((1, 8, full), lambda i: (0, i, 0)),
@@ -294,7 +297,8 @@
         ],
         compiler_params=params(58, 1),
         cost_estimate=cost(4 * 4 * full * full * hg, 4 << 20),
-    )(lengths, idx, q, k, v)
+        input_output_aliases={5 + n: n for n in range(len(before))},
+    )(lengths, idx, q, k, v, *before)
     return res[:ns], res[ns], res[ns + 1]
 
 
@@ -404,20 +408,21 @@
 
 
 def middle_kernel(ns, nz, r, len_ref, tim_ref, idx, tok_ref, cot_ref, small_ref, *refs):
-    ctxs = refs[: 2 * ns]
-    refs = refs[2 * ns :]
+    ctxs = refs[:ns]
+    refs = refs[ns:]
     outer, dn, rest = refs[:4], refs[4 : 4 + 2 * nz], refs[4 + 2 * nz :]
-    out_ref, keep_o, send_o, ug_o, fl_o, cx_o, ag_o, r1_o = rest[:8]
+    out_ref, keep_o, send_o, ahead_o, ug_o, fl_o, cx_o, ag_o, r1_o = rest[:9]
+    rest = rest[1:]
     dctx = rest[8 : 8 + ns]
     sum_ref, gbup_ref = rest[8 + ns : 10 + ns]
     wu, wd, act, slope, ug, fl, cx, dg, first, norm, inv, stage, bup_ref, slots, wsem, osem, gsem = rest[10 + ns :]
     z, c, j = idx[0], idx[1], idx[2]
     seqs, rows, model = tok_ref.shape
     ff = wd.shape[0]
-    hg = ctxs[0].shape[1]
+    hg = ctxs[0].shape[2]
     tokens = seqs * rows
-    ends = (0, model, wu.shape[1])
-    for part in range(2):
+    ends = (0, model, wu.shape[1], wu.shape[1] + model)
+    for part in range(3):
         at = slice(ends[part], ends[part + 1])
         for n, src in enumerate(outer):
             core = c ^ (n // 2)
@@ -425,24 +430,24 @@
                 shift = shift_of(ns, core, m + (n % 2) * (ns // 2))
                 for a in range(nz):
                     d = ((z ^ a) * 2 + core) * ns + (j ^ shift)
-                    pltpu.make_async_copy(
-                        src.at[m, a, :, at],
-                        wu.at[pl.ds(pl.multiple_of(d * r, r), r), at],
-                        wsem.at[part],
-                    ).start()
+                    if part < 2:
+                        dst = wu.at[pl.ds(pl.multiple_of(d * r, r), r), at]
+                    else:
+                        dst = wd.at[pl.ds(pl.multiple_of(d * 4 * r, 4 * r), r), :]
+                    pltpu.make_async_copy(src.at[m, a, :, at], dst, wsem.at[part]).start()
     for n, src in enumerate(dn):
         core = c ^ (n % 2)
         for m in range(ns):
             d = (lax.rem(z + nz - n // 2, nz) * 2 + core) * ns + (j ^ shift_of(ns, core, m))
             pltpu.make_async_copy(
                 src.at[m],
-                wd.at[pl.ds(pl.multiple_of(d * 4 * r, 4 * r), 4 * r), :],
+                wd.at[pl.ds(pl.multiple_of(d * 4 * r + r, r), 3 * r), :],
                 wsem.at[2],
             ).start()
     for k in range(ns):
         at = pl.ds(pl.multiple_of((j ^ k) * hg, 128), hg)
         for s in range(seqs):
-            cx[s * rows : (s + 1) * rows, at] = ctxs[s * ns + k][...]
+            cx[s * rows : (s + 1) * rows, at] = ctxs[k][s]
     sum_ref[...] = jnp.zeros_like(sum_ref)
     pltpu.make_async_copy(cx, cx_o, osem.at[0]).start()
     u1_all = wu.at[:, 0 : ends[1]]
@@ -524,19 +529,20 @@
 
     wide = ns * 4 * r
 
-    def grad_copy(n, dst):
-        return pltpu.make_async_copy(slots.at[n % 2], dst.at[n % nz], gsem.at[n % 2])
+    def grad_copy(n):
+        a = n % nz
+        dst = keep_o.at[a] if n >= nz else ahead_o.at[0] if a == nz - 1 else send_o.at[a]
+        return pltpu.make_async_copy(slots.at[n % 2], dst, gsem.at[n % 2])
 
     for n in range(2 * nz):
         core = c ^ 1 if n < nz else c
-        dst = send_o if n < nz else keep_o
         own = pl.multiple_of((lax.rem(z + n % nz, nz) * 2 + core) * wide, wide)
         total = tn(act[:, pl.ds(own, wide)], dg[...])
         if n >= 2:
-            grad_copy(n - 2, send_o if n - 2 < nz else keep_o).wait()
+            grad_copy(n - 2).wait()
         for b in range(ns):
             slots[n % 2, place_of(ns, core, j ^ b)] = total[b * 4 * r : (b + 1) * 4 * r].astype(BF16)
-        grad_copy(n, dst).start()
+        grad_copy(n).start()
 
     def one_up_grad(n, _):
         at = pl.ds(pl.multiple_of(n * WIDE, WIDE), WIDE)
@@ -584,7 +590,7 @@
     r1_copy.start()
     pltpu.make_async_copy(cx, cx_o, osem.at[0]).wait()
     for n in (2 * nz - 2, 2 * nz - 1):
-        grad_copy(n, keep_o).wait()
+        grad_copy(n).wait()
     pltpu.make_async_copy(ug, ug_o, osem.at[4]).wait()
     ag_copy.wait()
     r1_copy.wait()
@@ -593,13 +599,14 @@
 def middle(ns, nz, r, lengths, timesteps, idx, tokens, cotangent, small, ctxs, outer, dn):
     seqs, rows, model = tokens.shape
     total = seqs * rows
-    ff = dn[0].shape[1] * ns * nz * 2
-    hg = ctxs[0].shape[1]
+    ff = 4 * r * ns * nz * 2
+    hg = ctxs[0].shape[2]
     sh = lambda *a: jax.ShapeDtypeStruct(a[:-1], a[-1])
     outs = [
         sh(seqs, rows, model, BF16),
         sh(nz, ns, 4 * r, model, BF16),
-        sh(nz, ns, 4 * r, model, BF16),
+        sh(nz - 1, ns, 4 * r, model, BF16),
+        sh(1, ns, 4 * r, model, BF16),
         sh(total, ff, BF16),
         sh(total, model, BF16),
         sh(total, model, BF16),
@@ -612,9 +619,9 @@
         name="middle",
         out_shape=outs,
         in_specs=[sspec()] * 3
-        + [vspec()] * (3 + 2 * ns)
+        + [vspec()] * (3 + ns)
         + [aspec()] * (len(outer) + len(dn)),
-        out_specs=[vspec()] + [aspec()] * 7 + [vspec()] * (ns + 2),
+        out_specs=[vspec()] + [aspec()] * 8 + [vspec()] * (ns + 2),
         scratch_shapes=[
             VMEM((model, model + ff + PAD), BF16),
             VMEM((ff, model), BF16),
@@ -639,7 +646,7 @@
             2 * total * (2 * model * model + 4 * model * ff), 40 << 20, 3 * total * ff
         ),
     )(lengths, timesteps, idx, tokens, cotangent, small, *ctxs, *outer, *dn)
-    return res[:8], res[8 : 8 + ns], res[8 + ns], res[9 + ns]
+    return res[:9], res[9 : 9 + ns], res[9 + ns], res[10 + ns]
 
 
 def place_of(ns, core, offset):
@@ -658,6 +665,19 @@
         dst[:, first + a * wide : first + (a + 1) * wide] = got
 
 
+def store_halves(ns, nz, r, core, idx, total, low, high):
+    for b in range(ns):
+        slot = place_of(ns, core, idx[2] ^ b)
+
+        def put(dst, slot):
+            for a in range(nz):
+                n = (a * ns + b) * r
+                dst[a, slot] = total[n : n + r].astype(BF16)
+
+        pl.when(slot < ns // 2)(lambda: put(low, slot))
+        pl.when(slot >= ns // 2)(lambda: put(high, slot - ns // 2))
+
+
 def store_slots(ns, nz, r, core, walk, idx, total, dst, at=slice(None)):
     for a in range(nz):
         for b in range(ns):
@@ -666,7 +686,7 @@
             dst[a, slot, :, at] = total[n : n + r].astype(BF16)
 
 
-def up_grad_kernel(ns, nz, r, idx, cx_ref, ag_ref, fl_ref, ug_ref, gbup_ref, keep_ref, send_ref, left):
+def up_grad_kernel(ns, nz, r, idx, cx_ref, ag_ref, fl_ref, ug_ref, gbup_ref, keep_ref, send_ref, ahead_ref, left):
     i = pl.program_id(0)
     split = ag_ref.shape[1] // WIDE
     last = pl.num_programs(0) - 1
@@ -676,7 +696,7 @@
     def both(right):
         total = tn(left[...], right)
         store_slots(ns, nz, r, c, True, idx, total[:half], keep_ref)
-        store_slots(ns, nz, r, c ^ 1, True, idx, total[half:], send_ref)
+        store_halves(ns, nz, r, c ^ 1, idx, total[half:], send_ref, ahead_ref)
 
     @pl.when(i == 0)
     def _():
@@ -698,15 +718,16 @@
 
     @pl.when(i == last)
     def _():
-        keep_ref[...] = jnp.zeros_like(keep_ref)
-        send_ref[...] = jnp.zeros_like(send_ref)
-        for cc, dst in enumerate((keep_ref, send_ref)):
+        for dst in (keep_ref, send_ref, ahead_ref):
+            dst[...] = jnp.zeros_like(dst)
+        for cc in range(2):
             core = c ^ cc
             for a in range(nz):
                 for b in range(ns):
                     d = ((idx[0] ^ a) * 2 + core) * ns + (idx[2] ^ shift_of(ns, core, b))
                     row = gbup_ref[pl.ds(d, 1), :]
-                    dst[a, b, :, 0 : 4 * r] = jnp.broadcast_to(row, (r, 4 * r)).astype(BF16)
+                    dst = keep_ref if cc == 0 else send_ref if b < ns // 2 else ahead_ref
+                    dst[a, b if cc == 0 else b % (ns // 2), :, 0 : 4 * r] = jnp.broadcast_to(row, (r, 4 * r)).astype(BF16)
 
 
 def up_grad(ns, nz, r, idx, cx, ag, fl, ug, gbup):
@@ -715,11 +736,12 @@
     width = model + ff + PAD
     split, top = model // WIDE, ff // WIDE - 1
     one = lambda shape: pl.BlockSpec(shape, lambda i: (0,) * len(shape))
-    block = pl.BlockSpec((nz, ns, r, WIDE), lambda i: (0, 0, 0, i))
+    block = lambda n: pl.BlockSpec((nz, n, r, WIDE), lambda i: (0, 0, 0, i))
     return pl.pallas_call(
         functools.partial(up_grad_kernel, ns, nz, r),
         name="up_grad",
-        out_shape=[jax.ShapeDtypeStruct((nz, ns, r, width), BF16)] * 2,
+        out_shape=[jax.ShapeDtypeStruct((nz, ns, r, width), BF16)]
+        + [jax.ShapeDtypeStruct((nz, ns // 2, r, width), BF16)] * 2,
         grid=(pl.cdiv(width, WIDE),),
         in_specs=[
             sspec(),
@@ -729,7 +751,7 @@
             pl.BlockSpec((total, WIDE), lambda i: (0, jnp.minimum(jnp.maximum(i - split, 0), top))),
             one(gbup.shape),
         ],
-        out_specs=[block, block],
+        out_specs=[block(ns), block(ns // 2), block(ns // 2)],
         scratch_shapes=[VMEM((total, model), BF16)],
         compiler_params=params(58, 1),
         cost_estimate=cost(2 * total * model * width, 10 << 20),
@@ -877,73 +899,55 @@
 
 
 class Scatter:
-    def __init__(self, keep, send, ns, nz):
+    def __init__(self, keep, send, ahead, ns, nz):
         self.ns, self.nz = ns, nz
-        self.terms = [keep] + self.exchange(send)
+        self.ahead = to_mate(ahead)
+        self.terms = [keep]
+        self.send = send
         self.last = None
 
-    def exchange(self, send):
-        return [to_mate(send)]
-
-    def high(self, half):
-        return [t[: self.nz, half : self.ns] for t in self.terms]
+    def fetch(self):
+        self.terms = self.terms + [to_mate(self.send)]
 
     def bit(self):
         half = self.ns // 2
-        self.last = added(self.high(half)).astype(BF16)
-        self.terms = self.terms + [to_bit(self.last, self.ns.bit_length() - 2)]
+        parts = [t[: self.nz, half : self.ns] for t in self.terms[: 2 if self.ahead is None else 1]]
+        parts += [t[: self.nz, half : self.ns] for t in self.terms[2:]]
+        if isinstance(self, ScatterDirect) and self.ahead is not None:
+            parts, self.ahead = parts + [self.ahead], None
+        self.last = added(parts).astype(BF16)
+        self.got = to_bit(self.last, self.ns.bit_length() - 2)
         self.ns = half
 
-    def finish(self, at=slice(None), row=slice(None)):
-        while self.step():
-            pass
+    def take(self):
+        self.terms = self.terms + [self.got]
+
+    def total(self, at=slice(None), row=slice(None)):
         return added([t[0, 0, row, at] for t in self.terms])
 
 
 class ScatterDirect(Scatter):
-    ahead = None
-
-    def exchange(self, send):
-        half = self.ns // 2
-        self.ahead = to_mate(send[:, half:])
-        return [to_mate(send[:, :half])]
-
-    def high(self, half):
-        if self.ahead is None:
-            return super().high(half)
-        parts = [t[: self.nz, half : self.ns] for t in self.terms[:1]] + [self.ahead]
-        self.ahead = None
-        return parts
-
-    def step(self):
-        if self.ns > 1:
-            self.bit()
-        elif self.nz > 1:
-            self.last = [added([t[a, 0] for t in self.terms]).astype(BF16) for a in range(1, self.nz)]
-            self.terms = self.terms + [to_z(v, a + 1)[None, None] for a, v in enumerate(self.last)]
-            self.nz = 1
+    def all_z(self):
+        self.last = [added([t[a, 0] for t in self.terms]).astype(BF16) for a in range(1, self.nz)]
+        self.got = [to_z(v, a + 1)[None, None] for a, v in enumerate(self.last)]
+        self.nz = 1
+
+    def take_z(self):
+        self.terms = self.terms + list(self.got)
+
+
+class ScatterRing(Scatter):
+    def ring(self):
+        self.nz -= 1
+        if self.ahead is not None:
+            parts, self.ahead = [self.terms[0][self.nz], self.ahead[0]], None
         else:
-            return False
-        return True
-
-
-class ScatterRing(Scatter):
-    moving = None
-
-    def fix(self):
-        self.terms = self.terms + [self.moving[None]]
-
-    def step(self):
-        if self.nz > 1:
-            self.nz -= 1
-            parts = [t[self.nz] for t in self.terms] + ([] if self.moving is None else [self.moving])
-            self.last = added(parts).astype(BF16)
-            self.moving = to_ring(self.last)
-        elif self.ns > 1:
-            self.bit()
-        else:
-            return False
-        return True
+            parts = [t[self.nz] for t in self.terms] + [self.got]
+        self.last = added(parts).astype(BF16)
+        self.got = to_ring(self.last)
+
+    def take_ring(self):
+        self.terms = self.terms + [self.got[None]]
 
 
 def body(
@@ -980,8 +984,8 @@
 
     high = ns.bit_length() - 1
     vectors = [b_query, b_value, b_out, gain_one, shift_one, b_down, gain_two, shift_two, w_time, b_time]
-    mine, outer = pack(ns, idx, w_query, w_key, w_value, vectors, b_up, w_out, w_up)
-    tok, down = tokens[None], w_down[None]
+    mine, outer = pack(ns, idx, w_query, w_key, w_value, vectors, b_up, w_out, w_up, w_down)
+    tok, down = tokens[None], w_down[r:][None]
     kept = [mine[m] for m in range(ns)]
     outer_z, near_z = [], []
     waiting = list(range(1, nz))
@@ -989,7 +993,7 @@
         got = [to_bit(tok, place), to_bit(down, place) if place < high - 1 else None]
         away = [m for m in range(ns) if m & (1 << place)]
         pieces = to_bit(jnp.stack([kept[m] for m in away]), place)
-        now = waiting[:1] if place < high - 1 else waiting
+        now = waiting[:2] if place < high - 1 else waiting
         waiting = waiting[len(now) :]
         outer_z = outer_z + [to_z(outer, a) for a in now]
         tok, down, outer, kept, got, pieces, outer_z = hold(tok, down, outer, kept, got, pieces, outer_z)
@@ -1017,71 +1021,106 @@
 
     projected = project(ns, nz, lengths, timesteps, idx, toks, qa, qb)
     q, k, v, low, w_qkv, small = projected
-    fronts, ctxs = [], []
+    mates, _ = after([cur, down], qb)
+    fronts, mates, before = [], [to_mate(m) for m in mates], []
     for s in range(seqs):
-        front = attend(ns, s, lengths, idx, q, k, v)
-        front, downs = hold(front, downs)
+        front = attend(ns, s, lengths, idx, q, k, v, before)
+        front, downs, mates = hold(front, downs, mates)
         downs.append(to_ring(downs[-1]))
-        if s == seqs - 1:
-            front, ctxs, cur_next = hold(front, ctxs, cur_next)
+        if s == 0:
+            mates = list(mates) + [to_mate(downs[1])]
+        else:
+            front, cur_next = hold(front, cur_next)
         fronts.append(front)
-        ctxs = ctxs + [front[0][0]] + [to_seq(front[0][n], n) for n in range(1, ns)]
+        before = front[0]
         q, _ = after(q, front[0])
-    near_half, _ = after(cur, fronts[-1][0])
-    outer = [cur, cur_next, to_mate(near_half), to_mate(cur_next)]
+    ctxs = [before[0]] + [to_seq(before[n], n) for n in range(1, ns)]
     while len(downs) < nz:
         downs.append(to_ring(downs[-1]))
-    downs = [x for d in downs for x in (d, to_mate(d))]
+    ctxs, downs = hold(ctxs, downs)
+    outer = [cur, cur_next, mates[0], to_mate(cur_next)]
+    mates = list(mates[1:]) + [to_mate(d) for d in downs[2:]]
+    downs = [x for pair in zip(downs, mates) for x in pair]
     kept, dctx_out, sums, gbup = middle(
         ns, nz, r, lengths, timesteps, idx, tokens, cotangent, small, ctxs, outer, downs
     )
-    output, keep, send, ug, fl, cx, ag, r1 = kept
-
-    two = ScatterRing(keep, send, ns, nz)
+    output, keep, send, ahead, ug, fl, cx, ag, r1 = kept
+
+    two = ScatterRing(keep, send, ahead, ns, nz)
     dctx = [to_seq(dctx_out[n], n) for n in range(1, ns)]
-    (fl, ug), _ = after((fl, ug), dctx_out)
+    two.send, two.ahead = hold(two.send, two.ahead)
+    two.fetch()
+    two.ring()
+    (fl, ug), _ = after((fl, ug), (dctx_out, two.last))
     got = up_grad(ns, nz, r, idx, cx, ag, fl, ug, gbup)
-    got, (dctx, two.terms[-1]) = after(got, (dctx, two.terms[-1]))
+    got, dctx, two.got, two.terms = hold(got, dctx, two.got, two.terms)
     dctx = [dctx_out[0]] + list(dctx)
     one = ScatterDirect(*got, ns, nz)
-    two.step()
-    one.step()
+    two.ring()
+    one.bit()
+    one.send, _ = after(one.send, one.last)
+    one.fetch()
     dctx, _ = after(dctx, (one.last, two.last))
     r1 = r1.reshape(seqs, rows, model)
-    backs = []
+    backs, planes = [], []
     for s in range(seqs):
         back = attend_back(ns, s, lengths, timesteps, idx, q, k, v, fronts[s][1], fronts[s][2], w_qkv, dctx)
-        back, two.moving = hold(back, two.moving)
+        back, two.got, one.got, planes = hold(back, two.got, one.got, planes)
         backs.append(back)
-        two.step()
-        dctx, _ = after(dctx, two.last)
-    low, _ = after(low, two.last)
+        planes = list(planes)
+        one.take()
+        sent = []
+        if two.nz > 1:
+            two.ring()
+            sent.append(two.last)
+        if one.ns > 1:
+            one.bit()
+            sent.append(one.last)
+        elif one.nz > 1:
+            one.all_z()
+            sent.append(one.last)
+        away = after(back[2], sent)[0] if s else back[2]
+        planes.append([back[1], to_bit(away, high - 1)])
+        dctx, _ = after(dctx, (sent, back[2]))
+    two.got, _ = after(two.got, one.last)
+    while two.nz > 1:
+        two.ring()
+    two.take_ring()
+    while one.ns > 1:
+        one.take()
+        one.bit()
+    if one.nz > 1:
+        one.take()
+        one.all_z()
+    low, _ = after(low, (one.last, backs[-1][2]))
     keep, send = qkv_grad(
         ns, nz, r, idx, low, backs[0][0], backs[1][0], sums, backs[0][3], backs[1][3], backs[0][4], backs[1][4]
     )
+    keep, send, one.got, planes = hold(keep, send, one.got, planes)
     near = [keep, to_mate(send)]
-
-    one.terms[-1], near[0] = hold(one.terms[-1], near[0])
-    one.step()
-    one.terms[-1], near[1] = hold(one.terms[-1], near[1])
-    planes = [[b[1], b[2]] for b in backs]
-    planes, _ = after(planes, one.terms[-1])
-    planes = [[p[0], to_bit(p[1], high - 1)] for p in planes]
-    one.step()
-    near, two.moving, planes, one.terms = hold(near, two.moving, planes, one.terms)
-    two.fix()
-    near_z = [to_z(added([t[a] for t in near]).astype(BF16), a) for a in range(1, nz)]
-    two.step()
+    one.take_z()
+    two.bit()
     n = ns // 2
+    away = []
     while n > 1:
         away = added_rows([[t[n // 2 : n] for t in p] for p in planes])
         n //= 2
         got = to_bit(away, n.bit_length() - 1)
-        planes = [p + [got[i]] for i, p in enumerate(planes)]
-    near_z, two.terms, planes = hold(near_z, two.terms, planes)
+        planes = [list(p) + [got[i]] for i, p in enumerate(planes)]
+    near[0], _ = after(near[0], (two.last, away))
+    away = [added([t[a] for t in near]).astype(BF16) for a in range(1, nz)]
+    near_z = [to_z(v, a + 1) for a, v in enumerate(away)]
+    one.terms, _ = after(one.terms, near_z[-1])
+    ends = (slice(0, model), slice(model, 5 * model))
+    outs = [one.total(at) for at in ends] + [one.total(slice(5 * model, 5 * model + 4 * r), 0)]
+    near_z, two.got, planes, outs = hold(near_z, two.got, planes, outs)
+    two.take()
+    while two.ns > 1:
+        two.bit()
+        two.take()
     own = added([t[0] for t in near] + near_z)
     others = [to_seq(own[n].astype(BF16), n) for n in range(1, ns)]
-    grad_down = two.finish()
+    grad_down = two.total()
     grad_tokens = jnp.stack([added([t[0] for t in p] + [r1[s]]).astype(BF16) for s, p in enumerate(planes)])
     g_query, g_key, g_value, vectors = finish(ns, r, model, idx, own[0], others)
     return (
@@ -1092,12 +1131,12 @@
         g_key,
         g_value,
         vectors[1],
-        one.finish(slice(0, model)),
+        outs[0],
         vectors[2],
         vectors[3],
         vectors[4],
-        one.finish(slice(model, 5 * model)),
-        one.finish(slice(5 * model, 5 * model + 4 * r), 0),
+        outs[1],
+        outs[2],
         grad_down,
         vectors[5],
         vectors[6],

time: 417 us -> 393 us (0.942)
  waiting for transfers between devices: 169 us -> 140 us
  starting transfers between devices: 49 us -> 53.6 us
  other arithmetic: 29.7 us -> 33.9 us
    ppermute x12, waiting for transfers between devices: 56.6 us -> 41.6 us  [to_z(): return lax.ppermute(value, 'dp', [(i, i ^ 2 * a) for i in range(nd)])]
    ppermute x15, waiting for transfers between devices: 54.2 us -> 42.1 us  [to_bit(): return lax.ppermute(value, ('dp', 'seq'), pairs)]
    ppermute x12, starting transfers between devices: 14.7 us -> 20.8 us  [to_z(): return lax.ppermute(value, 'dp', [(i, i ^ 2 * a) for i in range(nd)])]
    slice x1 -> x0, local copies, waits for them, and re-layouts: 4.69 us -> none  [exchange(): return [to_mate(send[:, :half])]]
    ppermute x6, waiting for transfers between devices: 35.5 us -> 31.2 us  [to_ring(): return lax.ppermute(value, 'dp', [(i, (i + 2) % nd) for i in range(nd)])]
    ppermute x11 -> x12, waiting for transfers between devices: 9.02 us -> 12.6 us  [to_mate(): return lax.ppermute(value, 'dp', [(i, i ^ 1) for i in range(nd)])]
    ppermute x12 -> x9, starting transfers between devices: 14.2 us -> 10.7 us  [to_seq(): return lax.ppermute(value, 'seq', [(i, i ^ k) for i in range(ns)])]
    ppermute x12 -> x9, waiting for transfers between devices: 13.7 us -> 12.4 us  [to_seq(): return lax.ppermute(value, 'seq', [(i, i ^ k) for i in range(ns)])]
  transfers between devices with their start and end apart: 56 -> 54, of which waited for: 25 -> 21; matrix products, arithmetic and copies ran while one was open for 6% -> 6% of each run, Pallas kernels for 25% -> 27%
where the time goes in v3:
time: 393 us; the launch traced here: 388 us
  Pallas kernels  148 us (38%)
  waiting for transfers between devices  140 us (36%)
  starting transfers between devices  53.6 us (14%)
  other arithmetic  33.9 us (9%)
  local copies, waits for them, and re-layouts  10.7 us (3%)
    pallas_call x1, Pallas kernels, middle(): pl.pallas_call(functools.partial(middle_kernel, ns, nz, r), name='middle'...  43.2 us
    ppermute x15, waiting for transfers between devices, to_bit(): return lax.ppermute(value, ('dp', 'seq'), pairs)  42.1 us
    ppermute x12, waiting for transfers between devices, to_z(): return lax.ppermute(value, 'dp', [(i, i ^ 2 * a) for i in range(nd)])  41.6 us
    pallas_call x2, Pallas kernels, attend_back(): pl.pallas_call(functools.partial(attend_back_kernel, ns, seq), name='atte...  41.2 us
    ppermute x6, waiting for transfers between devices, to_ring(): return lax.ppermute(value, 'dp', [(i, (i + 2) % nd) for i in range(nd)])  31.2 us
    pallas_call x2, Pallas kernels, attend(): pl.pallas_call(functools.partial(attend_kernel, ns, seq), name='attend',...  26.7 us
    ppermute x12, starting transfers between devices, to_z(): return lax.ppermute(value, 'dp', [(i, i ^ 2 * a) for i in range(nd)])  20.8 us
    ppermute x15, starting transfers between devices, to_bit(): return lax.ppermute(value, ('dp', 'seq'), pairs)  17 us
  transfers between devices with their start and end apart: 54, of which 21 were waited for; matrix products, arithmetic and copies ran while one was open for 6% of the time, Pallas kernels for 27%

profile of v3, /device:TPU:0, one launch (start us, length us, event | category | flops | bytes accessed | tf_op | source)
XLA Modules:
  0.0 387.6 jit_solution(16197026987710570107)
XLA Ops:
  0.7 3.0 collective-permute-start
  4.2 2.9 pack.1
  15.4 4.6 %collective-permute-done.2 = bf16[2,32,896]{2,1,0:T(8,128)(2,1)S(1)} collective-permute-done((bf16[2,32,896]{2,1,0:T(8,128)(2,1)S(1)}, bf16[2,32,896]{2,1,0:T(8,128)(2,1)S(1)}, u32[]{:S(2)}, u32[]{:S(2)}) %collective-permute-start.2) | collective-permute-done | bytes 114720 | tf_op jit(solution)/shard_map/ppermute | solution.py:861
  20.0 7.8 %collective-permute-done.4 = bf16[32,6272]{1,0:T(8,128)(2,1)S(1)} collective-permute-done((bf16[32,6272]{1,0:T(8,128)(2,1)}, bf16[32,6272]{1,0:T(8,128)(2,1)S(1)}, u32[]{:S(2)}, u32[]{:S(2)}) %collective-permute-start.4) | collective-permute-done | bytes 401440 | tf_op jit(solution)/shard_map/ppermute | solution.py:846
  29.9 3.2 collective-permute-start.7
  34.8 21.9 %collective-permute-done.6 = bf16[2,32,896]{2,1,0:T(8,128)(2,1)S(1)} collective-permute-done((bf16[2,32,896]{2,1,0:T(8,128)(2,1)S(1)}, bf16[2,32,896]{2,1,0:T(8,128)(2,1)S(1)}, u32[]{:S(2)}, u32[]{:S(2)}) %collective-permute-start.6) | collective-permute-done | bytes 114720 | tf_op jit(solution)/shard_map/ppermute | solution.py:861
  59.1 3.3 collective-permute-start.10
  63.5 6.0 %collective-permute-done.10 = bf16[4,32,896]{2,1,0:T(8,128)(2,1)S(1)} collective-permute-done((bf16[4,32,896]{2,1,0:T(8,128)(2,1)S(1)}, bf16[4,32,896]{2,1,0:T(8,128)(2,1)S(1)}, u32[]{:S(2)}, u32[]{:S(2)}) %collective-permute-start.10) | collective-permute-done | bytes 229408 | tf_op jit(solution)/shard_map/ppermute | solution.py:846
  69.5 11.0 %collective-permute-done.9 = bf16[4,32,896]{2,1,0:T(8,128)(2,1)S(1)} collective-permute-done((bf16[4,32,896]{2,1,0:T(8,128)(2,1)S(1)}, bf16[4,32,896]{2,1,0:T(8,128)(2,1)S(1)}, u32[]{:S(2)}, u32[]{:S(2)}) %collective-permute-start.9) | collective-permute-done | bytes 229408 | tf_op jit(solution)/shard_map/ppermute | solution.py:846
  85.8 9.5 %project.1 = (bf16[2,1024,256]{2,1,0:T(8,128)(2,1)}, bf16[2,1024,256]{2,1,0:T(8,128)(2,1)}, bf16[2,1024,256]{2,1,0:T(8,128)(2,1)}, bf16[2,1024,1024]{2,1,0:T(8,1...) custom-call(s32[2,8]{1,0:T(2,128)} %len_ref.11, s32[2,8]{1,0:T(2,128)} %tim_ref.7, s32[3]{0:T(128)} %pad_add_fusion.idx, ...), custom_call_target="tpu_custom_call" | custom-call | flops 3221225472 | bytes 14680064 | tf_op jit(solution)/shard_map/project/pallas_call | solution.py:194
  95.3 12.5 %attend.2 = (bf16[2,256,256]{2,1,0:T(8,128)(2,1)}, bf16[2,256,256]{2,1,0:T(8,128)(2,1)}, bf16[2,256,256]{2,1,0:T(8,128)(2,1)}, bf16[2,256,256]{2,1,0:T(8,128)(2,...) custom-call(s32[2,8]{1,0:T(2,128)} %len_ref.11, s32[3]{0:T(128)} %pad_add_fusion.idx, ...), custom_call_target="tpu_custom_call" | custom-call | flops 4294967296 | bytes 4194304 | tf_op jit(solution)/shard_map/attend/pallas_call | solution.py:282
  110.5 14.2 %attend.3 = (bf16[2,256,256]{2,1,0:T(8,128)(2,1)}, bf16[2,256,256]{2,1,0:T(8,128)(2,1)}, bf16[2,256,256]{2,1,0:T(8,128)(2,1)}, bf16[2,256,256]{2,1,0:T(8,128)(2,...) custom-call(s32[2,8]{1,0:T(2,128)} %len_ref.11, ...), custom_call_target="tpu_custom_call", output_to_operand_aliasing={{0}: (5, {}), {1}: (6, {}), {2}: (7, {}), {3}: (8, {})} | custom-call | flops 4294967296 | bytes 4194304 | tf_op jit(solution)/shard_map/attend/pallas_call | solution.py:282
  124.7 7.2 %collective-permute-done.17.refs_12_ = bf16[4,96,1024]{2,1,0:T(8,128)(2,1)} collective-permute-done((bf16[4,96,1024]{2,1,0:T(8,128)(2,1)S(1)}, bf16[4,96,1024]{2,1,0:T(8,128)(2,1)}, u32[]{:S(2)}, u32[]{:S(2)}) %collective-permute-start.17) | collective-permute-done | bytes 786464 | tf_op jit(solution)/shard_map/ppermute | solution.py:851
  135.5 5.8 %collective-permute-done.20.refs_1_ = bf16[2,256,256]{2,1,0:T(8,128)(2,1)S(1)} collective-permute-done((bf16[2,256,256]{2,1,0:T(8,128)(2,1)}, bf16[2,256,256]{2,1,0:T(8,128)(2,1)S(1)}, u32[]{:S(2)}, u32[]{:S(2)}) %collective-permute-start.20) | collective-permute-done | bytes 262176 | tf_op jit(solution)/shard_map/ppermute | solution.py:836
  141.4 6.5 %collective-permute-done.21.refs_2_ = bf16[2,256,256]{2,1,0:T(8,128)(2,1)S(1)} collective-permute-done((bf16[2,256,256]{2,1,0:T(8,128)(2,1)}, bf16[2,256,256]{2,1,0:T(8,128)(2,1)S(1)}, u32[]{:S(2)}, u32[]{:S(2)}) %collective-permute-start.21) | collective-permute-done | bytes 262176 | tf_op jit(solution)/shard_map/ppermute | solution.py:836
  149.3 4.5 %collective-permute-done.23.refs_14_ = bf16[4,96,1024]{2,1,0:T(8,128)(2,1)S(1)} collective-permute-done((bf16[4,96,1024]{2,1,0:T(8,128)(2,1)}, bf16[4,96,1024]{2,1,0:T(8,128)(2,1)S(1)}, u32[]{:S(2)}, u32[]{:S(2)}) %collective-permute-start.23) | collective-permute-done | bytes 786464 | tf_op jit(solution)/shard_map/ppermute | solution.py:851
  154.4 3.1 collective-permute-done.25.refs_13_
  160.2 43.2 %middle.1 = (bf16[2,256,1024]{2,1,0:T(8,128)(2,1)}, bf16[4,4,128,1024]{3,2,1,0:T(8,128)(2,1)}, bf16[3,4,128,1024]{3,2,1,0:T(8,128)(2,1)}, bf16[1,4,128,1024]{3,2...) custom-call(s32[2,8]{1,0:T(2,128)} %len_ref.11, ...), custom_call_target="tpu_custom_call" | custom-call | flops 19327352832 | bytes 41943040 | tf_op jit(solution)/shard_map/middle/pallas_call | solution.py:617
  211.8 14.6 %up_grad.1 = (bf16[4,4,32,5248]{3,2,1,0:T(8,128)(2,1)}, bf16[4,2,32,5248]{3,2,1,0:T(8,128)(2,1)}, bf16[4,2,32,5248]{3,2,1,0:T(8,128)(2,1)}) custom-call(s32[3]{0:T(128)} %pad_add_fusion.idx, bf16[512,1024]{1,0:T(8,128)(2,1)} %get-tuple-element.303.cx_ref, bf16[512,1024]{1,0:T(8,128)(2,1)} %get-tuple-element.304.ag_ref, ...), custom_call_target="tpu_custom_call" | custom-call | flops 5502926848 | bytes 10485760 | tf_op jit(solution)/shard_map/up_grad/pallas_call | solution.py:740
  226.5 9.0 %collective-permute-done.31 = bf16[4,128,1024]{2,1,0:T(8,128)(2,1)S(1)} collective-permute-done((bf16[4,128,1024]{2,1,0:T(8,128)(2,1)S(1)}, bf16[4,128,1024]{2,1,0:T(8,128)(2,1)S(1)}, u32[]{:S(2)}, u32[]{:S(2)}) %collective-permute-start.31) | collective-permute-done | bytes 1048608 | tf_op jit(solution)/shard_map/ppermute | solution.py:851
  237.1 5.2 %collective-permute-done.33 = bf16[4,2,32,5248]{3,2,1,0:T(8,128)(2,1)S(1)} collective-permute-done((bf16[4,2,32,5248]{3,2,1,0:T(8,128)(2,1)}, bf16[4,2,32,5248]{3,2,1,0:T(8,128)(2,1)S(1)}, u32[]{:S(2)}, u32[]{:S(2)}) %collective-permute-start.33) | collective-permute-done | bytes 2687008 | tf_op jit(solution)/shard_map/ppermute | solution.py:841
  242.3 4.0 %add_convert_fusion = bf16[4,2,32,5248]{3,2,1,0:T(8,128)(2,1)} fusion(bf16[4,2,32,5248]{3,2,1,0:T(8,128)(2,1)S(1)} %collective-permute-done.33, bf16[4,4,32,5248]{3,2,1,0:T(8,128)(2,1)} %get-tuple-element.388), kind=kLoop, calls=%fused_computation | loop fusion | flops 5373952 | bytes 8060928 | tf_op jit(solution)/shard_map/convert_element_type | solution.py:918
  250.8 19.7 %attend_back.2 = (bf16[1024,768]{1,0:T(8,128)(2,1)}, bf16[2,256,1024]{2,1,0:T(8,128)(2,1)}, bf16[2,256,1024]{2,1,0:T(8,128)(2,1)}, f32[8,1024]{1,0:T(8,128)}, f32[8,768]{1,0:T(8,128)}) custom-call(s32[2,8]{1,0:T(2,128)} %len_ref.11, s32[2,8]{1,0:T(2,128)} %tim_ref.7, s32[3]{0:T(128)} %pad_add_fusion.idx, bf16[2,1024,256]{2,1,0:T(8,128)(2,1)} %get-tuple-element.326.q_ref, ...), custom_call_target="tpu_custom_call" | custom-call | flops 10737418240 | bytes 10485760 | tf_op jit(solution)/shard_map/attend_back/pallas_call | solution.py:381
  270.4 7.4 %collective-permute-done.35 = bf16[4,128,1024]{2,1,0:T(8,128)(2,1)S(1)} collective-permute-done((bf16[4,128,1024]{2,1,0:T(8,128)(2,1)}, bf16[4,128,1024]{2,1,0:T(8,128)(2,1)S(1)}, u32[]{:S(2)}, u32[]{:S(2)}) %collective-permute-start.35) | collective-permute-done | bytes 1048608 | tf_op jit(solution)/shard_map/ppermute | solution.py:851
  287.2 21.5 %attend_back.3 = (bf16[1024,768]{1,0:T(8,128)(2,1)}, bf16[2,256,1024]{2,1,0:T(8,128)(2,1)}, bf16[2,256,1024]{2,1,0:T(8,128)(2,1)}, f32[8,1024]{1,0:T(8,128)}, f32[8,768]{1,0:T(8,128)}) custom-call(s32[2,8]{1,0:T(2,128)} %len_ref.11, s32[2,8]{1,0:T(2,128)} %tim_ref.7, s32[3]{0:T(128)} %pad_add_fusion.idx, bf16[2,1024,256]{2,1,0:T(8,128)(2,1)} %get-tuple-element.326.q_ref, ...), custom_call_target="tpu_custom_call" | custom-call | flops 10737418240 | bytes 10485760 | tf_op jit(solution)/shard_map/attend_back/pallas_call | solution.py:381
  308.7 3.1 collective-permute-done.37
  311.8 3.3 fusion.11
  316.1 4.4 %collective-permute-start.40 = (bf16[32,5248]{1,0:T(8,128)(2,1)S(1)}, bf16[32,5248]{1,0:T(8,128)(2,1)}, u32[]{:S(2)}, u32[]{:S(2)}) collective-permute-start(bf16[32,5248]{1,0:T(8,128)(2,1)S(1)} %get-tuple-element.417), channel_id=1, source_target_pairs={{0,8},{4,12},{8,0},{12,4},{16,24},{20,28},{24,16},{28,20},{1,9},{5... | collective-permute-start | bytes 1007624 | tf_op jit(solution)/shard_map/ppermute | solution.py:846
  320.5 8.7 %qkv_grad.1 = (bf16[4,4,32,896]{3,2,1,0:T(8,128)(2,1)}, bf16[4,4,32,896]{3,2,1,0:T(8,128)(2,1)}) custom-call(s32[3]{0:T(128)} %pad_add_fusion.idx, bf16[2,1024,1024]{2,1,0:T(8,128)(2,1)} %get-tuple-element.362.low_ref, bf16[1024,768]{1,0:T(8,128)(2,1)} %get-tuple-element.363.g0_ref, bf16[1024,768]{1,0:T(8,128)(2,1)} %get-tuple-element.364.g1_ref, ...), custom_call_target="tpu_custom_call" | custom-call | flops 3758096384 | bytes 12582912 | tf_op jit(solution)/shard_map/qkv_grad/pallas_call | solution.py:790
  329.3 16.6 %collective-permute-done.41 = bf16[32,5248]{1,0:T(8,128)(2,1)} collective-permute-done((bf16[32,5248]{1,0:T(8,128)(2,1)S(1)}, bf16[32,5248]{1,0:T(8,128)(2,1)}, u32[]{:S(2)}, u32[]{:S(2)}) %collective-permute-start.41) | collective-permute-done | bytes 335904 | tf_op jit(solution)/shard_map/ppermute | solution.py:846
  351.7 3.2 collective-permute-start.45
  354.9 13.4 %collective-permute-done.49 = bf16[2,1,256,1024]{3,2,1,0:T(8,128)(2,1)S(1)} collective-permute-done((bf16[2,1,256,1024]{3,2,1,0:T(8,128)(2,1)S(1)}, bf16[2,1,256,1024]{3,2,1,0:T(8,128)(2,1)S(1)}, u32[]{:S(2)}, u32[]{:S(2)}) %collective-permute-start.49) | collective-permute-done | bytes 1048608 | tf_op jit(solution)/shard_map/ppermute | solution.py:861
  (182 shorter events, 82.0 us)
Async XLA Ops:
  0.7 27.3 %collective-permute-start = (bf16[1,2,256,1024]{3,2,1,0:T(8,128)(2,1)}, bf16[1,2,256,1024]{3,2,1,0:T(8,128)(2,1)S(1)}, u32[]{:S(2)}, u32[]{:S(2)}) collective-permute-start(bf16[1,2,256,1024]{3,2,1,0:T(8,128)(2,1)} %bitcast.110), channel_id=1, source_target_pairs={{0,1},{1,0},{2,3},{3,2},{4,6},{5,7},{6,4},{7,5},{8,9},{9,8},{10,11... | collective-permute-start | bytes 3145736 | tf_op jit(solution)/shard_map/ppermute | solution.py:861
  7.1 20.7 %collective-permute-start.4 = (bf16[32,6272]{1,0:T(8,128)(2,1)}, bf16[32,6272]{1,0:T(8,128)(2,1)S(1)}, u32[]{:S(2)}, u32[]{:S(2)}) collective-permute-start(bf16[32,6272]{1,0:T(8,128)(2,1)} %get-tuple-element.234), channel_id=1, source_target_pairs={{0,16},{4,20},{8,24},{12,28},{16,0},{20,4},{24,8},{28,12},{1,17},{... | collective-permute-start | bytes 1204232 | tf_op jit(solution)/shard_map/ppermute | solution.py:846
  9.8 18.2 %collective-permute-start.3 = (bf16[32,6272]{1,0:T(8,128)(2,1)}, bf16[32,6272]{1,0:T(8,128)(2,1)S(1)}, u32[]{:S(2)}, u32[]{:S(2)}) collective-permute-start(bf16[32,6272]{1,0:T(8,128)(2,1)} %get-tuple-element.234), channel_id=1, source_target_pairs={{0,8},{4,12},{8,0},{12,4},{16,24},{20,28},{24,16},{28,20},{1,9},{5... | collective-permute-start | bytes 1204232 | tf_op jit(solution)/shard_map/ppermute | solution.py:846
  29.4 27.3 %collective-permute-start.5 = (bf16[2,2,256,1024]{3,2,1,0:T(8,128)(2,1)S(1)}, bf16[2,2,256,1024]{3,2,1,0:T(8,128)(2,1)S(1)}, u32[]{:S(2)}, u32[]{:S(2)}) collective-permute-start(bf16[2,2,256,1024]{3,2,1,0:T(8,128)(2,1)S(1)} %constant_dynamic-update-slice_fusion.refs_0_), channel_id=1, source_target_pairs={{0,2},{1,3},{2,0},{3,1},{4,5},{5,4},{6,7},{7,6},{8,10},{9,11},{10,... | collective-permute-start | bytes 6291464 | tf_op jit(solution)/shard_map/ppermute | solution.py:861
  29.9 26.8 %collective-permute-start.7 = (bf16[32,6272]{1,0:T(8,128)(2,1)S(1)}, bf16[32,6272]{1,0:T(8,128)(2,1)S(1)}, u32[]{:S(2)}, u32[]{:S(2)}) collective-permute-start(bf16[32,6272]{1,0:T(8,128)(2,1)S(1)} %copy-done.12), channel_id=1, source_target_pairs={{0,24},{4,28},{8,16},{12,20},{16,8},{20,12},{24,0},{28,4},{1,25},{... | collective-permute-start | bytes 1204232 | tf_op jit(solution)/shard_map/ppermute | solution.py:846
  33.2 23.5 %collective-permute-start.6 = (bf16[2,32,896]{2,1,0:T(8,128)(2,1)S(1)}, bf16[2,32,896]{2,1,0:T(8,128)(2,1)S(1)}, u32[]{:S(2)}, u32[]{:S(2)}) collective-permute-start(bf16[2,32,896]{2,1,0:T(8,128)(2,1)S(1)} %pad_maximum_fusion.6), channel_id=1, source_target_pairs={{0,2},{1,3},{2,0},{3,1},{4,5},{5,4},{6,7},{7,6},{8,10},{9,11},{10,... | collective-permute-start | bytes 344072 | tf_op jit(solution)/shard_map/ppermute | solution.py:861
  57.0 23.5 %collective-permute-start.12 = (bf16[1,4,32,6272]{3,2,1,0:T(8,128)(2,1)S(1)}, bf16[1,4,32,6272]{3,2,1,0:T(8,128)(2,1)S(1)}, u32[]{:S(2)}, u32[]{:S(2)}) collective-permute-start(bf16[1,4,32,6272]{3,2,1,0:T(8,128)(2,1)S(1)} %maximum_bitcast_fusion), channel_id=1, source_target_pairs={{0,1},{1,0},{2,3},{3,2},{4,6},{5,7},{6,4},{7,5},{8,9},{9,8},{10,11... | collective-permute-start | bytes 4816904 | tf_op jit(solution)/shard_map/ppermute | solution.py:861
  58.5 21.9 %collective-permute-start.11 = (bf16[2,96,1024]{2,1,0:T(8,128)(2,1)S(1)}, bf16[2,96,1024]{2,1,0:T(8,128)(2,1)S(1)}, u32[]{:S(2)}, u32[]{:S(2)}) collective-permute-start(bf16[2,96,1024]{2,1,0:T(8,128)(2,1)S(1)} %pad_maximum_fusion.3), channel_id=1, source_target_pairs={{0,2},{1,3},{2,0},{3,1},{4,5},{5,4},{6,7},{7,6},{8,10},{9,11},{10,... | collective-permute-start | bytes 1179656 | tf_op jit(solution)/shard_map/ppermute | solution.py:861
  62.3 18.1 %collective-permute-start.9 = (bf16[4,32,896]{2,1,0:T(8,128)(2,1)S(1)}, bf16[4,32,896]{2,1,0:T(8,128)(2,1)S(1)}, u32[]{:S(2)}, u32[]{:S(2)}) collective-permute-start(bf16[4,32,896]{2,1,0:T(8,128)(2,1)S(1)} %pad_maximum_fusion.4), channel_id=1, source_target_pairs={{0,16},{4,20},{8,24},{12,28},{16,0},{20,4},{24,8},{28,12},{1,17},{... | collective-permute-start | bytes 688136 | tf_op jit(solution)/shard_map/ppermute | solution.py:846
  83.2 24.6 %collective-permute-start.15 = (bf16[2,4,32,6272]{3,2,1,0:T(8,128)(2,1)S(1)}, bf16[2,4,32,6272]{3,2,1,0:T(8,128)(2,1)}, u32[]{:S(2)}, u32[]{:S(2)}) collective-permute-start(bf16[2,4,32,6272]{3,2,1,0:T(8,128)(2,1)S(1)} %constant_dynamic-update-slice_fusion.4.refs_4_), channel_id=1, source_target_pairs={{0,4},{4,0},{8,12},{12,8},{16,20},{20,16},{24,28},{28,24},{1,5},{5... | collective-permute-start | bytes 9633800 | tf_op jit(solution)/shard_map/ppermute | solution.py:841
  83.4 48.5 %collective-permute-start.19 = (bf16[2,4,32,6272]{3,2,1,0:T(8,128)(2,1)S(1)}, bf16[2,4,32,6272]{3,2,1,0:T(8,128)(2,1)}, u32[]{:S(2)}, u32[]{:S(2)}) collective-permute-start(bf16[2,4,32,6272]{3,2,1,0:T(8,128)(2,1)S(1)} %constant_dynamic-update-slice_fusion.4.refs_4_), channel_id=1, source_target_pairs={{0,2},{1,3},{2,0},{3,1},{4,5},{5,4},{6,7},{7,6},{8,10},{9,11},{10,... | collective-permute-start | bytes 9633800 | tf_op jit(solution)/shard_map/ppermute | solution.py:861
  85.0 22.8 %collective-permute-start.14 = (bf16[4,96,1024]{2,1,0:T(8,128)(2,1)S(1)}, bf16[4,96,1024]{2,1,0:T(8,128)(2,1)S(1)}, u32[]{:S(2)}, u32[]{:S(2)}) collective-permute-start(bf16[4,96,1024]{2,1,0:T(8,128)(2,1)S(1)} %constant_dynamic-update-slice_fusion.2.refs_8_), channel_id=1, source_target_pairs={{0,8},{4,12},{8,16},{12,20},{16,24},{20,28},{24,0},{28,4},{1,9},{5... | collective-permute-start | bytes 2359304 | tf_op jit(solution)/shard_map/ppermute | solution.py:851
  85.8 22.1 %collective-permute-start.16 = (bf16[4,96,1024]{2,1,0:T(8,128)(2,1)S(1)}, bf16[4,96,1024]{2,1,0:T(8,128)(2,1)S(1)}, u32[]{:S(2)}, u32[]{:S(2)}) collective-permute-start(bf16[4,96,1024]{2,1,0:T(8,128)(2,1)S(1)} %constant_dynamic-update-slice_fusion.2.refs_8_), channel_id=1, source_target_pairs={{0,4},{4,0},{8,12},{12,8},{16,20},{20,16},{24,28},{28,24},{1,5},{5... | collective-permute-start | bytes 2359304 | tf_op jit(solution)/shard_map/ppermute | solution.py:841
  110.5 21.4 %collective-permute-start.17 = (bf16[4,96,1024]{2,1,0:T(8,128)(2,1)S(1)}, bf16[4,96,1024]{2,1,0:T(8,128)(2,1)}, u32[]{:S(2)}, u32[]{:S(2)}) collective-permute-start(bf16[4,96,1024]{2,1,0:T(8,128)(2,1)S(1)} %collective-permute-done.14.refs_10_), channel_id=1, source_target_pairs={{0,8},{4,12},{8,16},{12,20},{16,24},{20,28},{24,0},{28,4},{1,9},{5... | collective-permute-start | bytes 2359304 | tf_op jit(solution)/shard_map/ppermute | solution.py:851
  131.9 25.6 %collective-permute-start.24 = (bf16[2,4,32,6272]{3,2,1,0:T(8,128)(2,1)}, bf16[2,4,32,6272]{3,2,1,0:T(8,128)(2,1)S(1)}, u32[]{:S(2)}, u32[]{:S(2)}) collective-permute-start(bf16[2,4,32,6272]{3,2,1,0:T(8,128)(2,1)} %collective-permute-done.19.refs_5_), channel_id=1, source_target_pairs={{0,4},{4,0},{8,12},{12,8},{16,20},{20,16},{24,28},{28,24},{1,5},{5... | collective-permute-start | bytes 9633800 | tf_op jit(solution)/shard_map/ppermute | solution.py:841
  131.9 22.0 %collective-permute-start.23 = (bf16[4,96,1024]{2,1,0:T(8,128)(2,1)}, bf16[4,96,1024]{2,1,0:T(8,128)(2,1)S(1)}, u32[]{:S(2)}, u32[]{:S(2)}) collective-permute-start(bf16[4,96,1024]{2,1,0:T(8,128)(2,1)} %collective-permute-done.17.refs_12_), channel_id=1, source_target_pairs={{0,8},{4,12},{8,16},{12,20},{16,24},{20,28},{24,0},{28,4},{1,9},{5... | collective-permute-start | bytes 2359304 | tf_op jit(solution)/shard_map/ppermute | solution.py:851
  206.4 29.1 %collective-permute-start.32 = (bf16[3,4,128,1024]{3,2,1,0:T(8,128)(2,1)}, bf16[3,4,128,1024]{3,2,1,0:T(8,128)(2,1)S(1)}, u32[]{:S(2)}, u32[]{:S(2)}) collective-permute-start(bf16[3,4,128,1024]{3,2,1,0:T(8,128)(2,1)} %get-tuple-element.321), channel_id=1, source_target_pairs={{0,4},{4,0},{8,12},{12,8},{16,20},{20,16},{24,28},{28,24},{1,5},{5... | collective-permute-start | bytes 9437192 | tf_op jit(solution)/shard_map/ppermute | solution.py:841
  208.1 27.3 %collective-permute-start.31 = (bf16[4,128,1024]{2,1,0:T(8,128)(2,1)S(1)}, bf16[4,128,1024]{2,1,0:T(8,128)(2,1)S(1)}, u32[]{:S(2)}, u32[]{:S(2)}) collective-permute-start(bf16[4,128,1024]{2,1,0:T(8,128)(2,1)S(1)} %fusion.2), channel_id=1, source_target_pairs={{0,8},{4,12},{8,16},{12,20},{16,24},{20,28},{24,0},{28,4},{1,9},{5... | collective-permute-start | bytes 3145736 | tf_op jit(solution)/shard_map/ppermute | solution.py:851
  208.2 18.2 %collective-permute-start.28 = (bf16[2,256,256]{2,1,0:T(8,128)(2,1)}, bf16[2,256,256]{2,1,0:T(8,128)(2,1)S(1)}, u32[]{:S(2)}, u32[]{:S(2)}) collective-permute-start(bf16[2,256,256]{2,1,0:T(8,128)(2,1)} %get-tuple-element.308), channel_id=1, source_target_pairs={{0,1},{1,0},{2,3},{3,2},{4,5},{5,4},{6,7},{7,6},{8,9},{9,8},{10,11... | collective-permute-start | bytes 786440 | tf_op jit(solution)/shard_map/ppermute | solution.py:836
  246.3 32.7 %collective-permute-start.36 = (bf16[4,2,32,5248]{3,2,1,0:T(8,128)(2,1)}, bf16[4,2,32,5248]{3,2,1,0:T(8,128)(2,1)}, u32[]{:S(2)}, u32[]{:S(2)}) collective-permute-start(bf16[4,2,32,5248]{3,2,1,0:T(8,128)(2,1)} %add_convert_fusion), channel_id=1, source_target_pairs={{0,2},{1,3},{2,0},{3,1},{4,5},{5,4},{6,7},{7,6},{8,10},{9,11},{10,... | collective-permute-start | bytes 8060936 | tf_op jit(solution)/shard_map/ppermute | solution.py:861
  247.4 31.6 %collective-permute-start.34 = (bf16[4,2,32,5248]{3,2,1,0:T(8,128)(2,1)}, bf16[4,2,32,5248]{3,2,1,0:T(8,128)(2,1)}, u32[]{:S(2)}, u32[]{:S(2)}) collective-permute-start(bf16[4,2,32,5248]{3,2,1,0:T(8,128)(2,1)} %get-tuple-element.325), channel_id=1, source_target_pairs={{0,4},{4,0},{8,12},{12,8},{16,20},{20,16},{24,28},{28,24},{1,5},{5... | collective-permute-start | bytes 8060936 | tf_op jit(solution)/shard_map/ppermute | solution.py:841
  250.8 27.1 %collective-permute-start.35 = (bf16[4,128,1024]{2,1,0:T(8,128)(2,1)}, bf16[4,128,1024]{2,1,0:T(8,128)(2,1)S(1)}, u32[]{:S(2)}, u32[]{:S(2)}) collective-permute-start(bf16[4,128,1024]{2,1,0:T(8,128)(2,1)} %fusion.1), channel_id=1, source_target_pairs={{0,8},{4,12},{8,16},{12,20},{16,24},{20,28},{24,0},{28,4},{1,9},{5... | collective-permute-start | bytes 3145736 | tf_op jit(solution)/shard_map/ppermute | solution.py:851
  281.7 30.1 %collective-permute-start.38 = (bf16[4,1,32,5248]{3,2,1,0:T(8,128)(2,1)S(1)}, bf16[4,1,32,5248]{3,2,1,0:T(8,128)(2,1)}, u32[]{:S(2)}, u32[]{:S(2)}) collective-permute-start(bf16[4,1,32,5248]{3,2,1,0:T(8,128)(2,1)S(1)} %add_convert_fusion.1), channel_id=1, source_target_pairs={{0,1},{1,0},{2,3},{3,2},{4,6},{5,7},{6,4},{7,5},{8,9},{9,8},{10,11... | collective-permute-start | bytes 4030472 | tf_op jit(solution)/shard_map/ppermute | solution.py:861
  286.4 25.5 %collective-permute-start.37 = (bf16[4,128,1024]{2,1,0:T(8,128)(2,1)}, bf16[4,128,1024]{2,1,0:T(8,128)(2,1)}, u32[]{:S(2)}, u32[]{:S(2)}) collective-permute-start(bf16[4,128,1024]{2,1,0:T(8,128)(2,1)} %fusion), channel_id=1, source_target_pairs={{0,8},{4,12},{8,16},{12,20},{16,24},{20,28},{24,0},{28,4},{1,9},{5... | collective-permute-start | bytes 3145736 | tf_op jit(solution)/shard_map/ppermute | solution.py:851
  286.4 25.5 %collective-permute-start.39 = (bf16[2,256,1024]{2,1,0:T(8,128)(2,1)}, bf16[2,256,1024]{2,1,0:T(8,128)(2,1)}, u32[]{:S(2)}, u32[]{:S(2)}) collective-permute-start(bf16[2,256,1024]{2,1,0:T(8,128)(2,1)} %get-tuple-element.349), channel_id=1, source_target_pairs={{0,2},{1,3},{2,0},{3,1},{4,5},{5,4},{6,7},{7,6},{8,10},{9,11},{10,... | collective-permute-start | bytes 3145736 | tf_op jit(solution)/shard_map/ppermute | solution.py:861
  315.2 30.7 %collective-permute-start.43 = (bf16[2,256,1024]{2,1,0:T(8,128)(2,1)}, bf16[2,256,1024]{2,1,0:T(8,128)(2,1)}, u32[]{:S(2)}, u32[]{:S(2)}) collective-permute-start(bf16[2,256,1024]{2,1,0:T(8,128)(2,1)} %get-tuple-element.375), channel_id=1, source_target_pairs={{0,2},{1,3},{2,0},{3,1},{4,5},{5,4},{6,7},{7,6},{8,10},{9,11},{10,... | collective-permute-start | bytes 3145736 | tf_op jit(solution)/shard_map/ppermute | solution.py:861
  316.1 29.7 %collective-permute-start.41 = (bf16[32,5248]{1,0:T(8,128)(2,1)S(1)}, bf16[32,5248]{1,0:T(8,128)(2,1)}, u32[]{:S(2)}, u32[]{:S(2)}) collective-permute-start(bf16[32,5248]{1,0:T(8,128)(2,1)S(1)} %get-tuple-element.416), channel_id=1, source_target_pairs={{0,16},{4,20},{8,24},{12,28},{16,0},{20,4},{24,8},{28,12},{1,17},{... | collective-permute-start | bytes 1007624 | tf_op jit(solution)/shard_map/ppermute | solution.py:846
  316.1 29.7 %collective-permute-start.40 = (bf16[32,5248]{1,0:T(8,128)(2,1)S(1)}, bf16[32,5248]{1,0:T(8,128)(2,1)}, u32[]{:S(2)}, u32[]{:S(2)}) collective-permute-start(bf16[32,5248]{1,0:T(8,128)(2,1)S(1)} %get-tuple-element.417), channel_id=1, source_target_pairs={{0,8},{4,12},{8,0},{12,4},{16,24},{20,28},{24,16},{28,20},{1,9},{5... | collective-permute-start | bytes 1007624 | tf_op jit(solution)/shard_map/ppermute | solution.py:846
  347.8 20.5 %collective-permute-start.49 = (bf16[2,1,256,1024]{3,2,1,0:T(8,128)(2,1)S(1)}, bf16[2,1,256,1024]{3,2,1,0:T(8,128)(2,1)S(1)}, u32[]{:S(2)}, u32[]{:S(2)}) collective-permute-start(bf16[2,1,256,1024]{3,2,1,0:T(8,128)(2,1)S(1)} %pad_maximum_fusion), channel_id=1, source_target_pairs={{0,1},{1,0},{2,3},{3,2},{4,6},{5,7},{6,4},{7,5},{8,9},{9,8},{10,11... | collective-permute-start | bytes 3145736 | tf_op jit(solution)/shard_map/ppermute | solution.py:861
  349.6 24.3 %collective-permute-start.48 = (bf16[1,2,128,1024]{3,2,1,0:T(8,128)(2,1)S(1)}, bf16[1,2,128,1024]{3,2,1,0:T(8,128)(2,1)S(1)}, u32[]{:S(2)}, u32[]{:S(2)}) collective-permute-start(bf16[1,2,128,1024]{3,2,1,0:T(8,128)(2,1)S(1)} %add_convert_fusion.5), channel_id=1, source_target_pairs={{0,2},{1,3},{2,0},{3,1},{4,5},{5,4},{6,7},{7,6},{8,10},{9,11},{10,... | collective-permute-start | bytes 1572872 | tf_op jit(solution)/shard_map/ppermute | solution.py:861
  351.7 22.2 %collective-permute-start.46 = (bf16[4,32,896]{2,1,0:T(8,128)(2,1)S(1)}, bf16[4,32,896]{2,1,0:T(8,128)(2,1)S(1)}, u32[]{:S(2)}, u32[]{:S(2)}) collective-permute-start(bf16[4,32,896]{2,1,0:T(8,128)(2,1)S(1)} %get-tuple-element.421), channel_id=1, source_target_pairs={{0,16},{4,20},{8,24},{12,28},{16,0},{20,4},{24,8},{28,12},{1,17},{... | collective-permute-start | bytes 688136 | tf_op jit(solution)/shard_map/ppermute | solution.py:846
  351.7 22.2 %collective-permute-start.45 = (bf16[4,32,896]{2,1,0:T(8,128)(2,1)S(1)}, bf16[4,32,896]{2,1,0:T(8,128)(2,1)S(1)}, u32[]{:S(2)}, u32[]{:S(2)}) collective-permute-start(bf16[4,32,896]{2,1,0:T(8,128)(2,1)S(1)} %get-tuple-element.422), channel_id=1, source_target_pairs={{0,8},{4,12},{8,0},{12,4},{16,24},{20,28},{24,16},{28,20},{1,9},{5... | collective-permute-start | bytes 688136 | tf_op jit(solution)/shard_map/ppermute | solution.py:846
  (51 other events, 511.4 us)

commit v4 on v3

--- a/solution.py
+++ b/solution.py
@@ -1092,36 +1092,36 @@
     if one.nz > 1:
         one.take()
         one.all_z()
+    two.bit()
     low, _ = after(low, (one.last, backs[-1][2]))
     keep, send = qkv_grad(
         ns, nz, r, idx, low, backs[0][0], backs[1][0], sums, backs[0][3], backs[1][3], backs[0][4], backs[1][4]
     )
-    keep, send, one.got, planes = hold(keep, send, one.got, planes)
+    keep, send, one.got, two.got, planes = hold(keep, send, one.got, two.got, planes)
     near = [keep, to_mate(send)]
     one.take_z()
-    two.bit()
+    two.take()
+    away = [added([t[a] for t in near]).astype(BF16) for a in range(1, nz)]
+    near_z = [to_z(v, a + 1) for a, v in enumerate(away)]
+    planes, two.terms, _ = hold(planes, two.terms, away)
+    while two.ns > 1:
+        two.bit()
+        two.take()
     n = ns // 2
-    away = []
     while n > 1:
         away = added_rows([[t[n // 2 : n] for t in p] for p in planes])
         n //= 2
         got = to_bit(away, n.bit_length() - 1)
         planes = [list(p) + [got[i]] for i, p in enumerate(planes)]
-    near[0], _ = after(near[0], (two.last, away))
-    away = [added([t[a] for t in near]).astype(BF16) for a in range(1, nz)]
-    near_z = [to_z(v, a + 1) for a, v in enumerate(away)]
     one.terms, _ = after(one.terms, near_z[-1])
     ends = (slice(0, model), slice(model, 5 * model))
     outs = [one.total(at) for at in ends] + [one.total(slice(5 * model, 5 * model + 4 * r), 0)]
-    near_z, two.got, planes, outs = hold(near_z, two.got, planes, outs)
-    two.take()
-    while two.ns > 1:
-        two.bit()
-        two.take()
+    near_z, two.terms, outs = hold(near_z, two.terms, outs)
     own = added([t[0] for t in near] + near_z)
     others = [to_seq(own[n].astype(BF16), n) for n in range(1, ns)]
     grad_down = two.total()
     grad_tokens = jnp.stack([added([t[0] for t in p] + [r1[s]]).astype(BF16) for s, p in enumerate(planes)])
+    others, grad_tokens, grad_down = hold(others, grad_tokens, grad_down)
     g_query, g_key, g_value, vectors = finish(ns, r, model, idx, own[0], others)
     return (
         output,

time: 393 us -> 390 us (level)
  waiting for transfers between devices: 140 us -> 132 us
    ppermute x15, waiting for transfers between devices: 42.1 us -> 27.6 us  [to_bit(): return lax.ppermute(value, ('dp', 'seq'), pairs)]
    ppermute x12, waiting for transfers between devices: 41.6 us -> 45.8 us  [to_z(): return lax.ppermute(value, 'dp', [(i, i ^ 2 * a) for i in range(nd)])]
  transfers between devices with their start and end apart: 54 -> 54, of which waited for: 21 -> 22; matrix products, arithmetic and copies ran while one was open for 6% -> 7% of each run, Pallas kernels for 27% -> 27%
where the time goes in v4:
time: 390 us; the launch traced here: 384 us
  Pallas kernels  148 us (38%)
  waiting for transfers between devices  132 us (34%)
  starting transfers between devices  55.9 us (14%)
  other arithmetic  36.4 us (9%)
  local copies, waits for them, and re-layouts  10.5 us (3%)
    ppermute x12, waiting for transfers between devices, to_z(): return lax.ppermute(value, 'dp', [(i, i ^ 2 * a) for i in range(nd)])  45.8 us
    pallas_call x1, Pallas kernels, middle(): pl.pallas_call(functools.partial(middle_kernel, ns, nz, r), name='middle'...  43.3 us
    pallas_call x2, Pallas kernels, attend_back(): pl.pallas_call(functools.partial(attend_back_kernel, ns, seq), name='atte...  41.3 us
    ppermute x6, waiting for transfers between devices, to_ring(): return lax.ppermute(value, 'dp', [(i, (i + 2) % nd) for i in range(nd)])  30.7 us
    ppermute x15, waiting for transfers between devices, to_bit(): return lax.ppermute(value, ('dp', 'seq'), pairs)  27.6 us
    pallas_call x2, Pallas kernels, attend(): pl.pallas_call(functools.partial(attend_kernel, ns, seq), name='attend',...  26.7 us
    ppermute x12, starting transfers between devices, to_z(): return lax.ppermute(value, 'dp', [(i, i ^ 2 * a) for i in range(nd)])  20.8 us
    ppermute x15, starting transfers between devices, to_bit(): return lax.ppermute(value, ('dp', 'seq'), pairs)  18.8 us
  transfers between devices with their start and end apart: 54, of which 22 were waited for; matrix products, arithmetic and copies ran while one was open for 7% of the time, Pallas kernels for 27%

profile of v4, /device:TPU:0, one launch (start us, length us, event | category | flops | bytes accessed | tf_op | source)
XLA Modules:
  0.0 384.1 jit_solution(13104598518989171266)
XLA Ops:
  0.7 3.0 collective-permute-start
  15.4 4.6 %collective-permute-done.2 = bf16[2,32,896]{2,1,0:T(8,128)(2,1)S(1)} collective-permute-done((bf16[2,32,896]{2,1,0:T(8,128)(2,1)S(1)}, bf16[2,32,896]{2,1,0:T(8,128)(2,1)S(1)}, u32[]{:S(2)}, u32[]{:S(2)}) %collective-permute-start.2) | collective-permute-done | bytes 114720 | tf_op jit(solution)/shard_map/ppermute | solution.py:861
  20.0 7.8 %collective-permute-done.4 = bf16[32,6272]{1,0:T(8,128)(2,1)S(1)} collective-permute-done((bf16[32,6272]{1,0:T(8,128)(2,1)}, bf16[32,6272]{1,0:T(8,128)(2,1)S(1)}, u32[]{:S(2)}, u32[]{:S(2)}) %collective-permute-start.4) | collective-permute-done | bytes 401440 | tf_op jit(solution)/shard_map/ppermute | solution.py:846
  29.9 3.2 collective-permute-start.7
  34.8 21.9 %collective-permute-done.6 = bf16[2,32,896]{2,1,0:T(8,128)(2,1)S(1)} collective-permute-done((bf16[2,32,896]{2,1,0:T(8,128)(2,1)S(1)}, bf16[2,32,896]{2,1,0:T(8,128)(2,1)S(1)}, u32[]{:S(2)}, u32[]{:S(2)}) %collective-permute-start.6) | collective-permute-done | bytes 114720 | tf_op jit(solution)/shard_map/ppermute | solution.py:861
  59.1 3.3 collective-permute-start.10
  63.5 6.0 %collective-permute-done.10 = bf16[4,32,896]{2,1,0:T(8,128)(2,1)S(1)} collective-permute-done((bf16[4,32,896]{2,1,0:T(8,128)(2,1)S(1)}, bf16[4,32,896]{2,1,0:T(8,128)(2,1)S(1)}, u32[]{:S(2)}, u32[]{:S(2)}) %collective-permute-start.10) | collective-permute-done | bytes 229408 | tf_op jit(solution)/shard_map/ppermute | solution.py:846
  69.5 11.0 %collective-permute-done.9 = bf16[4,32,896]{2,1,0:T(8,128)(2,1)S(1)} collective-permute-done((bf16[4,32,896]{2,1,0:T(8,128)(2,1)S(1)}, bf16[4,32,896]{2,1,0:T(8,128)(2,1)S(1)}, u32[]{:S(2)}, u32[]{:S(2)}) %collective-permute-start.9) | collective-permute-done | bytes 229408 | tf_op jit(solution)/shard_map/ppermute | solution.py:846
  85.8 9.4 %project.1 = (bf16[2,1024,256]{2,1,0:T(8,128)(2,1)}, bf16[2,1024,256]{2,1,0:T(8,128)(2,1)}, bf16[2,1024,256]{2,1,0:T(8,128)(2,1)}, bf16[2,1024,1024]{2,1,0:T(8,1...) custom-call(s32[2,8]{1,0:T(2,128)} %len_ref.11, s32[2,8]{1,0:T(2,128)} %tim_ref.7, s32[3]{0:T(128)} %pad_add_fusion.idx, ...), custom_call_target="tpu_custom_call" | custom-call | flops 3221225472 | bytes 14680064 | tf_op jit(solution)/shard_map/project/pallas_call | solution.py:194
  95.2 12.5 %attend.2 = (bf16[2,256,256]{2,1,0:T(8,128)(2,1)}, bf16[2,256,256]{2,1,0:T(8,128)(2,1)}, bf16[2,256,256]{2,1,0:T(8,128)(2,1)}, bf16[2,256,256]{2,1,0:T(8,128)(2,...) custom-call(s32[2,8]{1,0:T(2,128)} %len_ref.11, s32[3]{0:T(128)} %pad_add_fusion.idx, ...), custom_call_target="tpu_custom_call" | custom-call | flops 4294967296 | bytes 4194304 | tf_op jit(solution)/shard_map/attend/pallas_call | solution.py:282
  110.8 14.2 %attend.3 = (bf16[2,256,256]{2,1,0:T(8,128)(2,1)}, bf16[2,256,256]{2,1,0:T(8,128)(2,1)}, bf16[2,256,256]{2,1,0:T(8,128)(2,1)}, bf16[2,256,256]{2,1,0:T(8,128)(2,...) custom-call(s32[2,8]{1,0:T(2,128)} %len_ref.11, ...), custom_call_target="tpu_custom_call", output_to_operand_aliasing={{0}: (5, {}), {1}: (6, {}), {2}: (7, {}), {3}: (8, {})} | custom-call | flops 4294967296 | bytes 4194304 | tf_op jit(solution)/shard_map/attend/pallas_call | solution.py:282
  125.0 6.7 %collective-permute-done.17.refs_12_ = bf16[4,96,1024]{2,1,0:T(8,128)(2,1)} collective-permute-done((bf16[4,96,1024]{2,1,0:T(8,128)(2,1)S(1)}, bf16[4,96,1024]{2,1,0:T(8,128)(2,1)}, u32[]{:S(2)}, u32[]{:S(2)}) %collective-permute-start.17) | collective-permute-done | bytes 786464 | tf_op jit(solution)/shard_map/ppermute | solution.py:851
  135.4 5.8 %collective-permute-done.20.refs_1_ = bf16[2,256,256]{2,1,0:T(8,128)(2,1)S(1)} collective-permute-done((bf16[2,256,256]{2,1,0:T(8,128)(2,1)}, bf16[2,256,256]{2,1,0:T(8,128)(2,1)S(1)}, u32[]{:S(2)}, u32[]{:S(2)}) %collective-permute-start.20) | collective-permute-done | bytes 262176 | tf_op jit(solution)/shard_map/ppermute | solution.py:836
  141.3 6.5 %collective-permute-done.21.refs_2_ = bf16[2,256,256]{2,1,0:T(8,128)(2,1)S(1)} collective-permute-done((bf16[2,256,256]{2,1,0:T(8,128)(2,1)}, bf16[2,256,256]{2,1,0:T(8,128)(2,1)S(1)}, u32[]{:S(2)}, u32[]{:S(2)}) %collective-permute-start.21) | collective-permute-done | bytes 262176 | tf_op jit(solution)/shard_map/ppermute | solution.py:836
  149.2 4.5 %collective-permute-done.23.refs_14_ = bf16[4,96,1024]{2,1,0:T(8,128)(2,1)S(1)} collective-permute-done((bf16[4,96,1024]{2,1,0:T(8,128)(2,1)}, bf16[4,96,1024]{2,1,0:T(8,128)(2,1)S(1)}, u32[]{:S(2)}, u32[]{:S(2)}) %collective-permute-start.23) | collective-permute-done | bytes 786464 | tf_op jit(solution)/shard_map/ppermute | solution.py:851
  154.3 3.1 collective-permute-done.25.refs_13_
  160.1 43.3 %middle.1 = (bf16[2,256,1024]{2,1,0:T(8,128)(2,1)}, bf16[4,4,128,1024]{3,2,1,0:T(8,128)(2,1)}, bf16[3,4,128,1024]{3,2,1,0:T(8,128)(2,1)}, bf16[1,4,128,1024]{3,2...) custom-call(s32[2,8]{1,0:T(2,128)} %len_ref.11, ...), custom_call_target="tpu_custom_call" | custom-call | flops 19327352832 | bytes 41943040 | tf_op jit(solution)/shard_map/middle/pallas_call | solution.py:617
  211.7 14.6 %up_grad.1 = (bf16[4,4,32,5248]{3,2,1,0:T(8,128)(2,1)}, bf16[4,2,32,5248]{3,2,1,0:T(8,128)(2,1)}, bf16[4,2,32,5248]{3,2,1,0:T(8,128)(2,1)}) custom-call(s32[3]{0:T(128)} %pad_add_fusion.idx, bf16[512,1024]{1,0:T(8,128)(2,1)} %get-tuple-element.314.cx_ref, bf16[512,1024]{1,0:T(8,128)(2,1)} %get-tuple-element.315.ag_ref, ...), custom_call_target="tpu_custom_call" | custom-call | flops 5502926848 | bytes 10485760 | tf_op jit(solution)/shard_map/up_grad/pallas_call | solution.py:740
  226.4 9.0 %collective-permute-done.31 = bf16[4,128,1024]{2,1,0:T(8,128)(2,1)S(1)} collective-permute-done((bf16[4,128,1024]{2,1,0:T(8,128)(2,1)S(1)}, bf16[4,128,1024]{2,1,0:T(8,128)(2,1)S(1)}, u32[]{:S(2)}, u32[]{:S(2)}) %collective-permute-start.31) | collective-permute-done | bytes 1048608 | tf_op jit(solution)/shard_map/ppermute | solution.py:851
  237.0 5.2 %collective-permute-done.33 = bf16[4,2,32,5248]{3,2,1,0:T(8,128)(2,1)S(1)} collective-permute-done((bf16[4,2,32,5248]{3,2,1,0:T(8,128)(2,1)}, bf16[4,2,32,5248]{3,2,1,0:T(8,128)(2,1)S(1)}, u32[]{:S(2)}, u32[]{:S(2)}) %collective-permute-start.33) | collective-permute-done | bytes 2687008 | tf_op jit(solution)/shard_map/ppermute | solution.py:841
  242.2 3.9 %add_convert_fusion = bf16[4,2,32,5248]{3,2,1,0:T(8,128)(2,1)} fusion(bf16[4,2,32,5248]{3,2,1,0:T(8,128)(2,1)S(1)} %collective-permute-done.33, bf16[4,4,32,5248]{3,2,1,0:T(8,128)(2,1)} %get-tuple-element.403), kind=kLoop, calls=%fused_computation | loop fusion | flops 5373952 | bytes 8060928 | tf_op jit(solution)/shard_map/convert_element_type | solution.py:918
  250.6 19.7 %attend_back.2 = (bf16[1024,768]{1,0:T(8,128)(2,1)}, bf16[2,256,1024]{2,1,0:T(8,128)(2,1)}, bf16[2,256,1024]{2,1,0:T(8,128)(2,1)}, f32[8,1024]{1,0:T(8,128)}, f32[8,768]{1,0:T(8,128)}) custom-call(s32[2,8]{1,0:T(2,128)} %len_ref.11, s32[2,8]{1,0:T(2,128)} %tim_ref.7, s32[3]{0:T(128)} %pad_add_fusion.idx, bf16[2,1024,256]{2,1,0:T(8,128)(2,1)} %get-tuple-element.337.q_ref, ...), custom_call_target="tpu_custom_call" | custom-call | flops 10737418240 | bytes 10485760 | tf_op jit(solution)/shard_map/attend_back/pallas_call | solution.py:381
  270.3 7.3 %collective-permute-done.35 = bf16[4,128,1024]{2,1,0:T(8,128)(2,1)S(1)} collective-permute-done((bf16[4,128,1024]{2,1,0:T(8,128)(2,1)}, bf16[4,128,1024]{2,1,0:T(8,128)(2,1)S(1)}, u32[]{:S(2)}, u32[]{:S(2)}) %collective-permute-start.35) | collective-permute-done | bytes 1048608 | tf_op jit(solution)/shard_map/ppermute | solution.py:851
  283.3 2.9 fusion
  287.0 21.5 %attend_back.3 = (bf16[1024,768]{1,0:T(8,128)(2,1)}, bf16[2,256,1024]{2,1,0:T(8,128)(2,1)}, bf16[2,256,1024]{2,1,0:T(8,128)(2,1)}, f32[8,1024]{1,0:T(8,128)}, f32[8,768]{1,0:T(8,128)}) custom-call(s32[2,8]{1,0:T(2,128)} %len_ref.11, s32[2,8]{1,0:T(2,128)} %tim_ref.7, s32[3]{0:T(128)} %pad_add_fusion.idx, bf16[2,1024,256]{2,1,0:T(8,128)(2,1)} %get-tuple-element.337.q_ref, ...), custom_call_target="tpu_custom_call" | custom-call | flops 10737418240 | bytes 10485760 | tf_op jit(solution)/shard_map/attend_back/pallas_call | solution.py:381
  308.5 3.2 collective-permute-done.37
  311.7 3.4 fusion.13
  319.4 4.4 %collective-permute-start.40 = (bf16[32,5248]{1,0:T(8,128)(2,1)S(1)}, bf16[32,5248]{1,0:T(8,128)(2,1)}, u32[]{:S(2)}, u32[]{:S(2)}) collective-permute-start(bf16[32,5248]{1,0:T(8,128)(2,1)S(1)} %get-tuple-element.439), channel_id=1, source_target_pairs={{0,8},{4,12},{8,0},{12,4},{16,24},{20,28},{24,16},{28,20},{1,9},{5... | collective-permute-start | bytes 1007624 | tf_op jit(solution)/shard_map/ppermute | solution.py:846
  323.8 8.6 %qkv_grad.1 = (bf16[4,4,32,896]{3,2,1,0:T(8,128)(2,1)}, bf16[4,4,32,896]{3,2,1,0:T(8,128)(2,1)}) custom-call(s32[3]{0:T(128)} %pad_add_fusion.idx, bf16[2,1024,1024]{2,1,0:T(8,128)(2,1)} %get-tuple-element.373.low_ref, bf16[1024,768]{1,0:T(8,128)(2,1)} %get-tuple-element.374.g0_ref, bf16[1024,768]{1,0:T(8,128)(2,1)} %get-tuple-element.375.g1_ref, ...), custom_call_target="tpu_custom_call" | custom-call | flops 3758096384 | bytes 12582912 | tf_op jit(solution)/shard_map/qkv_grad/pallas_call | solution.py:790
  332.5 15.5 %collective-permute-done.41 = bf16[32,5248]{1,0:T(8,128)(2,1)} collective-permute-done((bf16[32,5248]{1,0:T(8,128)(2,1)}, bf16[32,5248]{1,0:T(8,128)(2,1)}, u32[]{:S(2)}, u32[]{:S(2)}) %collective-permute-start.41) | collective-permute-done | bytes 335904 | tf_op jit(solution)/shard_map/ppermute | solution.py:846
  353.3 3.2 collective-permute-start.46
  368.1 4.2 %collective-permute-done.47 = bf16[4,32,896]{2,1,0:T(8,128)(2,1)S(1)} collective-permute-done((bf16[4,32,896]{2,1,0:T(8,128)(2,1)S(1)}, bf16[4,32,896]{2,1,0:T(8,128)(2,1)S(1)}, u32[]{:S(2)}, u32[]{:S(2)}) %collective-permute-start.47) | collective-permute-done | bytes 229408 | tf_op jit(solution)/shard_map/ppermute | solution.py:846
  (179 shorter events, 89.2 us)
Async XLA Ops:
  0.7 27.3 %collective-permute-start = (bf16[1,2,256,1024]{3,2,1,0:T(8,128)(2,1)}, bf16[1,2,256,1024]{3,2,1,0:T(8,128)(2,1)S(1)}, u32[]{:S(2)}, u32[]{:S(2)}) collective-permute-start(bf16[1,2,256,1024]{3,2,1,0:T(8,128)(2,1)} %bitcast.112), channel_id=1, source_target_pairs={{0,1},{1,0},{2,3},{3,2},{4,6},{5,7},{6,4},{7,5},{8,9},{9,8},{10,11... | collective-permute-start | bytes 3145736 | tf_op jit(solution)/shard_map/ppermute | solution.py:861
  7.1 20.7 %collective-permute-start.4 = (bf16[32,6272]{1,0:T(8,128)(2,1)}, bf16[32,6272]{1,0:T(8,128)(2,1)S(1)}, u32[]{:S(2)}, u32[]{:S(2)}) collective-permute-start(bf16[32,6272]{1,0:T(8,128)(2,1)} %get-tuple-element.245), channel_id=1, source_target_pairs={{0,16},{4,20},{8,24},{12,28},{16,0},{20,4},{24,8},{28,12},{1,17},{... | collective-permute-start | bytes 1204232 | tf_op jit(solution)/shard_map/ppermute | solution.py:846
  9.8 18.2 %collective-permute-start.3 = (bf16[32,6272]{1,0:T(8,128)(2,1)}, bf16[32,6272]{1,0:T(8,128)(2,1)S(1)}, u32[]{:S(2)}, u32[]{:S(2)}) collective-permute-start(bf16[32,6272]{1,0:T(8,128)(2,1)} %get-tuple-element.245), channel_id=1, source_target_pairs={{0,8},{4,12},{8,0},{12,4},{16,24},{20,28},{24,16},{28,20},{1,9},{5... | collective-permute-start | bytes 1204232 | tf_op jit(solution)/shard_map/ppermute | solution.py:846
  29.4 27.3 %collective-permute-start.5 = (bf16[2,2,256,1024]{3,2,1,0:T(8,128)(2,1)S(1)}, bf16[2,2,256,1024]{3,2,1,0:T(8,128)(2,1)S(1)}, u32[]{:S(2)}, u32[]{:S(2)}) collective-permute-start(bf16[2,2,256,1024]{3,2,1,0:T(8,128)(2,1)S(1)} %constant_dynamic-update-slice_fusion.refs_0_), channel_id=1, source_target_pairs={{0,2},{1,3},{2,0},{3,1},{4,5},{5,4},{6,7},{7,6},{8,10},{9,11},{10,... | collective-permute-start | bytes 6291464 | tf_op jit(solution)/shard_map/ppermute | solution.py:861
  29.9 26.8 %collective-permute-start.7 = (bf16[32,6272]{1,0:T(8,128)(2,1)S(1)}, bf16[32,6272]{1,0:T(8,128)(2,1)S(1)}, u32[]{:S(2)}, u32[]{:S(2)}) collective-permute-start(bf16[32,6272]{1,0:T(8,128)(2,1)S(1)} %copy-done.11), channel_id=1, source_target_pairs={{0,24},{4,28},{8,16},{12,20},{16,8},{20,12},{24,0},{28,4},{1,25},{... | collective-permute-start | bytes 1204232 | tf_op jit(solution)/shard_map/ppermute | solution.py:846
  33.2 23.5 %collective-permute-start.6 = (bf16[2,32,896]{2,1,0:T(8,128)(2,1)S(1)}, bf16[2,32,896]{2,1,0:T(8,128)(2,1)S(1)}, u32[]{:S(2)}, u32[]{:S(2)}) collective-permute-start(bf16[2,32,896]{2,1,0:T(8,128)(2,1)S(1)} %pad_maximum_fusion.6), channel_id=1, source_target_pairs={{0,2},{1,3},{2,0},{3,1},{4,5},{5,4},{6,7},{7,6},{8,10},{9,11},{10,... | collective-permute-start | bytes 344072 | tf_op jit(solution)/shard_map/ppermute | solution.py:861
  57.0 23.5 %collective-permute-start.12 = (bf16[1,4,32,6272]{3,2,1,0:T(8,128)(2,1)S(1)}, bf16[1,4,32,6272]{3,2,1,0:T(8,128)(2,1)S(1)}, u32[]{:S(2)}, u32[]{:S(2)}) collective-permute-start(bf16[1,4,32,6272]{3,2,1,0:T(8,128)(2,1)S(1)} %maximum_bitcast_fusion), channel_id=1, source_target_pairs={{0,1},{1,0},{2,3},{3,2},{4,6},{5,7},{6,4},{7,5},{8,9},{9,8},{10,11... | collective-permute-start | bytes 4816904 | tf_op jit(solution)/shard_map/ppermute | solution.py:861
  58.5 21.9 %collective-permute-start.11 = (bf16[2,96,1024]{2,1,0:T(8,128)(2,1)S(1)}, bf16[2,96,1024]{2,1,0:T(8,128)(2,1)S(1)}, u32[]{:S(2)}, u32[]{:S(2)}) collective-permute-start(bf16[2,96,1024]{2,1,0:T(8,128)(2,1)S(1)} %pad_maximum_fusion.3), channel_id=1, source_target_pairs={{0,2},{1,3},{2,0},{3,1},{4,5},{5,4},{6,7},{7,6},{8,10},{9,11},{10,... | collective-permute-start | bytes 1179656 | tf_op jit(solution)/shard_map/ppermute | solution.py:861
  62.3 18.1 %collective-permute-start.9 = (bf16[4,32,896]{2,1,0:T(8,128)(2,1)S(1)}, bf16[4,32,896]{2,1,0:T(8,128)(2,1)S(1)}, u32[]{:S(2)}, u32[]{:S(2)}) collective-permute-start(bf16[4,32,896]{2,1,0:T(8,128)(2,1)S(1)} %pad_maximum_fusion.4), channel_id=1, source_target_pairs={{0,16},{4,20},{8,24},{12,28},{16,0},{20,4},{24,8},{28,12},{1,17},{... | collective-permute-start | bytes 688136 | tf_op jit(solution)/shard_map/ppermute | solution.py:846
  62.3 18.1 %collective-permute-start.8 = (bf16[4,32,896]{2,1,0:T(8,128)(2,1)S(1)}, bf16[4,32,896]{2,1,0:T(8,128)(2,1)S(1)}, u32[]{:S(2)}, u32[]{:S(2)}) collective-permute-start(bf16[4,32,896]{2,1,0:T(8,128)(2,1)S(1)} %pad_maximum_fusion.4), channel_id=1, source_target_pairs={{0,8},{4,12},{8,0},{12,4},{16,24},{20,28},{24,16},{28,20},{1,9},{5... | collective-permute-start | bytes 688136 | tf_op jit(solution)/shard_map/ppermute | solution.py:846
  83.2 24.5 %collective-permute-start.15 = (bf16[2,4,32,6272]{3,2,1,0:T(8,128)(2,1)S(1)}, bf16[2,4,32,6272]{3,2,1,0:T(8,128)(2,1)}, u32[]{:S(2)}, u32[]{:S(2)}) collective-permute-start(bf16[2,4,32,6272]{3,2,1,0:T(8,128)(2,1)S(1)} %constant_dynamic-update-slice_fusion.4.refs_4_), channel_id=1, source_target_pairs={{0,4},{4,0},{8,12},{12,8},{16,20},{20,16},{24,28},{28,24},{1,5},{5... | collective-permute-start | bytes 9633800 | tf_op jit(solution)/shard_map/ppermute | solution.py:841
  83.4 48.4 %collective-permute-start.19 = (bf16[2,4,32,6272]{3,2,1,0:T(8,128)(2,1)S(1)}, bf16[2,4,32,6272]{3,2,1,0:T(8,128)(2,1)}, u32[]{:S(2)}, u32[]{:S(2)}) collective-permute-start(bf16[2,4,32,6272]{3,2,1,0:T(8,128)(2,1)S(1)} %constant_dynamic-update-slice_fusion.4.refs_4_), channel_id=1, source_target_pairs={{0,2},{1,3},{2,0},{3,1},{4,5},{5,4},{6,7},{7,6},{8,10},{9,11},{10,... | collective-permute-start | bytes 9633800 | tf_op jit(solution)/shard_map/ppermute | solution.py:861
  85.0 22.7 %collective-permute-start.14 = (bf16[4,96,1024]{2,1,0:T(8,128)(2,1)S(1)}, bf16[4,96,1024]{2,1,0:T(8,128)(2,1)S(1)}, u32[]{:S(2)}, u32[]{:S(2)}) collective-permute-start(bf16[4,96,1024]{2,1,0:T(8,128)(2,1)S(1)} %constant_dynamic-update-slice_fusion.2.refs_8_), channel_id=1, source_target_pairs={{0,8},{4,12},{8,16},{12,20},{16,24},{20,28},{24,0},{28,4},{1,9},{5... | collective-permute-start | bytes 2359304 | tf_op jit(solution)/shard_map/ppermute | solution.py:851
  85.8 21.9 %collective-permute-start.16 = (bf16[4,96,1024]{2,1,0:T(8,128)(2,1)S(1)}, bf16[4,96,1024]{2,1,0:T(8,128)(2,1)S(1)}, u32[]{:S(2)}, u32[]{:S(2)}) collective-permute-start(bf16[4,96,1024]{2,1,0:T(8,128)(2,1)S(1)} %constant_dynamic-update-slice_fusion.2.refs_8_), channel_id=1, source_target_pairs={{0,4},{4,0},{8,12},{12,8},{16,20},{20,16},{24,28},{28,24},{1,5},{5... | collective-permute-start | bytes 2359304 | tf_op jit(solution)/shard_map/ppermute | solution.py:841
  110.4 21.4 %collective-permute-start.17 = (bf16[4,96,1024]{2,1,0:T(8,128)(2,1)S(1)}, bf16[4,96,1024]{2,1,0:T(8,128)(2,1)}, u32[]{:S(2)}, u32[]{:S(2)}) collective-permute-start(bf16[4,96,1024]{2,1,0:T(8,128)(2,1)S(1)} %collective-permute-done.14.refs_10_), channel_id=1, source_target_pairs={{0,8},{4,12},{8,16},{12,20},{16,24},{20,28},{24,0},{28,4},{1,9},{5... | collective-permute-start | bytes 2359304 | tf_op jit(solution)/shard_map/ppermute | solution.py:851
  131.8 25.6 %collective-permute-start.24 = (bf16[2,4,32,6272]{3,2,1,0:T(8,128)(2,1)}, bf16[2,4,32,6272]{3,2,1,0:T(8,128)(2,1)S(1)}, u32[]{:S(2)}, u32[]{:S(2)}) collective-permute-start(bf16[2,4,32,6272]{3,2,1,0:T(8,128)(2,1)} %collective-permute-done.19.refs_5_), channel_id=1, source_target_pairs={{0,4},{4,0},{8,12},{12,8},{16,20},{20,16},{24,28},{28,24},{1,5},{5... | collective-permute-start | bytes 9633800 | tf_op jit(solution)/shard_map/ppermute | solution.py:841
  131.8 22.0 %collective-permute-start.23 = (bf16[4,96,1024]{2,1,0:T(8,128)(2,1)}, bf16[4,96,1024]{2,1,0:T(8,128)(2,1)S(1)}, u32[]{:S(2)}, u32[]{:S(2)}) collective-permute-start(bf16[4,96,1024]{2,1,0:T(8,128)(2,1)} %collective-permute-done.17.refs_12_), channel_id=1, source_target_pairs={{0,8},{4,12},{8,16},{12,20},{16,24},{20,28},{24,0},{28,4},{1,9},{5... | collective-permute-start | bytes 2359304 | tf_op jit(solution)/shard_map/ppermute | solution.py:851
  206.3 29.1 %collective-permute-start.32 = (bf16[3,4,128,1024]{3,2,1,0:T(8,128)(2,1)}, bf16[3,4,128,1024]{3,2,1,0:T(8,128)(2,1)S(1)}, u32[]{:S(2)}, u32[]{:S(2)}) collective-permute-start(bf16[3,4,128,1024]{3,2,1,0:T(8,128)(2,1)} %get-tuple-element.332), channel_id=1, source_target_pairs={{0,4},{4,0},{8,12},{12,8},{16,20},{20,16},{24,28},{28,24},{1,5},{5... | collective-permute-start | bytes 9437192 | tf_op jit(solution)/shard_map/ppermute | solution.py:841
  208.1 27.3 %collective-permute-start.31 = (bf16[4,128,1024]{2,1,0:T(8,128)(2,1)S(1)}, bf16[4,128,1024]{2,1,0:T(8,128)(2,1)S(1)}, u32[]{:S(2)}, u32[]{:S(2)}) collective-permute-start(bf16[4,128,1024]{2,1,0:T(8,128)(2,1)S(1)} %fusion.2), channel_id=1, source_target_pairs={{0,8},{4,12},{8,16},{12,20},{16,24},{20,28},{24,0},{28,4},{1,9},{5... | collective-permute-start | bytes 3145736 | tf_op jit(solution)/shard_map/ppermute | solution.py:851
  208.1 18.2 %collective-permute-start.28 = (bf16[2,256,256]{2,1,0:T(8,128)(2,1)}, bf16[2,256,256]{2,1,0:T(8,128)(2,1)S(1)}, u32[]{:S(2)}, u32[]{:S(2)}) collective-permute-start(bf16[2,256,256]{2,1,0:T(8,128)(2,1)} %get-tuple-element.319), channel_id=1, source_target_pairs={{0,1},{1,0},{2,3},{3,2},{4,5},{5,4},{6,7},{7,6},{8,9},{9,8},{10,11... | collective-permute-start | bytes 786440 | tf_op jit(solution)/shard_map/ppermute | solution.py:836
  246.1 32.7 %collective-permute-start.36 = (bf16[4,2,32,5248]{3,2,1,0:T(8,128)(2,1)}, bf16[4,2,32,5248]{3,2,1,0:T(8,128)(2,1)}, u32[]{:S(2)}, u32[]{:S(2)}) collective-permute-start(bf16[4,2,32,5248]{3,2,1,0:T(8,128)(2,1)} %add_convert_fusion), channel_id=1, source_target_pairs={{0,2},{1,3},{2,0},{3,1},{4,5},{5,4},{6,7},{7,6},{8,10},{9,11},{10,... | collective-permute-start | bytes 8060936 | tf_op jit(solution)/shard_map/ppermute | solution.py:861
  247.2 31.6 %collective-permute-start.34 = (bf16[4,2,32,5248]{3,2,1,0:T(8,128)(2,1)}, bf16[4,2,32,5248]{3,2,1,0:T(8,128)(2,1)}, u32[]{:S(2)}, u32[]{:S(2)}) collective-permute-start(bf16[4,2,32,5248]{3,2,1,0:T(8,128)(2,1)} %get-tuple-element.336), channel_id=1, source_target_pairs={{0,4},{4,0},{8,12},{12,8},{16,20},{20,16},{24,28},{28,24},{1,5},{5... | collective-permute-start | bytes 8060936 | tf_op jit(solution)/shard_map/ppermute | solution.py:841
  250.6 27.1 %collective-permute-start.35 = (bf16[4,128,1024]{2,1,0:T(8,128)(2,1)}, bf16[4,128,1024]{2,1,0:T(8,128)(2,1)S(1)}, u32[]{:S(2)}, u32[]{:S(2)}) collective-permute-start(bf16[4,128,1024]{2,1,0:T(8,128)(2,1)} %fusion.1), channel_id=1, source_target_pairs={{0,8},{4,12},{8,16},{12,20},{16,24},{20,28},{24,0},{28,4},{1,9},{5... | collective-permute-start | bytes 3145736 | tf_op jit(solution)/shard_map/ppermute | solution.py:851
  281.5 30.2 %collective-permute-start.38 = (bf16[4,1,32,5248]{3,2,1,0:T(8,128)(2,1)S(1)}, bf16[4,1,32,5248]{3,2,1,0:T(8,128)(2,1)}, u32[]{:S(2)}, u32[]{:S(2)}) collective-permute-start(bf16[4,1,32,5248]{3,2,1,0:T(8,128)(2,1)S(1)} %add_convert_fusion.1), channel_id=1, source_target_pairs={{0,1},{1,0},{2,3},{3,2},{4,6},{5,7},{6,4},{7,5},{8,9},{9,8},{10,11... | collective-permute-start | bytes 4030472 | tf_op jit(solution)/shard_map/ppermute | solution.py:861
  286.2 25.5 %collective-permute-start.37 = (bf16[4,128,1024]{2,1,0:T(8,128)(2,1)}, bf16[4,128,1024]{2,1,0:T(8,128)(2,1)}, u32[]{:S(2)}, u32[]{:S(2)}) collective-permute-start(bf16[4,128,1024]{2,1,0:T(8,128)(2,1)} %fusion), channel_id=1, source_target_pairs={{0,8},{4,12},{8,16},{12,20},{16,24},{20,28},{24,0},{28,4},{1,9},{5... | collective-permute-start | bytes 3145736 | tf_op jit(solution)/shard_map/ppermute | solution.py:851
  286.2 25.5 %collective-permute-start.39 = (bf16[2,256,1024]{2,1,0:T(8,128)(2,1)}, bf16[2,256,1024]{2,1,0:T(8,128)(2,1)}, u32[]{:S(2)}, u32[]{:S(2)}) collective-permute-start(bf16[2,256,1024]{2,1,0:T(8,128)(2,1)} %get-tuple-element.360), channel_id=1, source_target_pairs={{0,2},{1,3},{2,0},{3,1},{4,5},{5,4},{6,7},{7,6},{8,10},{9,11},{10,... | collective-permute-start | bytes 3145736 | tf_op jit(solution)/shard_map/ppermute | solution.py:861
  315.1 32.9 %collective-permute-start.44 = (bf16[2,256,1024]{2,1,0:T(8,128)(2,1)}, bf16[2,256,1024]{2,1,0:T(8,128)(2,1)S(1)}, u32[]{:S(2)}, u32[]{:S(2)}) collective-permute-start(bf16[2,256,1024]{2,1,0:T(8,128)(2,1)} %get-tuple-element.388), channel_id=1, source_target_pairs={{0,2},{1,3},{2,0},{3,1},{4,5},{5,4},{6,7},{7,6},{8,10},{9,11},{10,... | collective-permute-start | bytes 3145736 | tf_op jit(solution)/shard_map/ppermute | solution.py:861
  318.4 29.6 %collective-permute-start.43 = (bf16[1,2,128,1024]{3,2,1,0:T(8,128)(2,1)}, bf16[1,2,128,1024]{3,2,1,0:T(8,128)(2,1)S(1)}, u32[]{:S(2)}, u32[]{:S(2)}) collective-permute-start(bf16[1,2,128,1024]{3,2,1,0:T(8,128)(2,1)} %add_convert_fusion.5), channel_id=1, source_target_pairs={{0,2},{1,3},{2,0},{3,1},{4,5},{5,4},{6,7},{7,6},{8,10},{9,11},{10,... | collective-permute-start | bytes 1572872 | tf_op jit(solution)/shard_map/ppermute | solution.py:861
  319.4 28.5 %collective-permute-start.41 = (bf16[32,5248]{1,0:T(8,128)(2,1)}, bf16[32,5248]{1,0:T(8,128)(2,1)}, u32[]{:S(2)}, u32[]{:S(2)}) collective-permute-start(bf16[32,5248]{1,0:T(8,128)(2,1)} %get-tuple-element.438), channel_id=1, source_target_pairs={{0,16},{4,20},{8,24},{12,28},{16,0},{20,4},{24,8},{28,12},{1,17},{... | collective-permute-start | bytes 1007624 | tf_op jit(solution)/shard_map/ppermute | solution.py:846
  319.4 28.5 %collective-permute-start.40 = (bf16[32,5248]{1,0:T(8,128)(2,1)S(1)}, bf16[32,5248]{1,0:T(8,128)(2,1)}, u32[]{:S(2)}, u32[]{:S(2)}) collective-permute-start(bf16[32,5248]{1,0:T(8,128)(2,1)S(1)} %get-tuple-element.439), channel_id=1, source_target_pairs={{0,8},{4,12},{8,0},{12,4},{16,24},{20,28},{24,16},{28,20},{1,9},{5... | collective-permute-start | bytes 1007624 | tf_op jit(solution)/shard_map/ppermute | solution.py:846
  353.3 19.0 %collective-permute-start.47 = (bf16[4,32,896]{2,1,0:T(8,128)(2,1)S(1)}, bf16[4,32,896]{2,1,0:T(8,128)(2,1)S(1)}, u32[]{:S(2)}, u32[]{:S(2)}) collective-permute-start(bf16[4,32,896]{2,1,0:T(8,128)(2,1)S(1)} %get-tuple-element.443), channel_id=1, source_target_pairs={{0,16},{4,20},{8,24},{12,28},{16,0},{20,4},{24,8},{28,12},{1,17},{... | collective-permute-start | bytes 688136 | tf_op jit(solution)/shard_map/ppermute | solution.py:846
  353.3 19.0 %collective-permute-start.46 = (bf16[4,32,896]{2,1,0:T(8,128)(2,1)S(1)}, bf16[4,32,896]{2,1,0:T(8,128)(2,1)S(1)}, u32[]{:S(2)}, u32[]{:S(2)}) collective-permute-start(bf16[4,32,896]{2,1,0:T(8,128)(2,1)S(1)} %get-tuple-element.444), channel_id=1, source_target_pairs={{0,8},{4,12},{8,0},{12,4},{16,24},{20,28},{24,16},{28,20},{1,9},{5... | collective-permute-start | bytes 688136 | tf_op jit(solution)/shard_map/ppermute | solution.py:846
  (50 other events, 531.8 us)
